TPU v7x, 32 devices: a whole 2x2x4 slice. The times are simulated.
32 devices in a mesh: dp: 8 (over z, y), blk: 4 (over x, core).
Axes of the slice: x: 2, y: 2, z: 4, core: 2. Of those that a mesh axis runs over, the one named last changes fastest.
Arguments:
- tokens: bfloat16 [8, 768, 2048], P('dp', 'blk'), may hold values from -6 to 6
- noise_table: bfloat16 [1000, 2048], replicated, may hold values from -6 to 6
- mod_weight: bfloat16 [2048, 12288], P(None, ('dp', 'blk')), may hold values from -0.125 to 0.125
- qkv_weight: bfloat16 [2048, 6144], P(('dp', 'blk')), may hold values from -0.125 to 0.125
- out_weight: bfloat16 [2048, 2048], P(('dp', 'blk')), may hold values from -0.75 to 0.75
- up_weight: bfloat16 [2048, 8192], P(('dp', 'blk')), may hold values from -0.125 to 0.125
- down_weight: bfloat16 [2048, 8192], P(('dp', 'blk')), may hold values from -0.0625 to 0.0625
- segment: int32 [8, 768], P('dp'), may hold values from 0 to 2, never falling along the last dimension, each value on 1 to 672 neighbouring positions
- key_valid: int32 [8, 768], P('dp'), may hold values 0 or 1
- noise_level: int32 [8, 3], replicated, may hold values from 0 to 999
- cotangent: bfloat16 [8, 768, 2048], P('dp', 'blk'), may hold values from -6 to 6
Outputs:
- block_out: bfloat16 [8, 768, 2048], P('dp', 'blk')
- grad_tokens: float32 [8, 768, 2048], P('dp', 'blk')
- grad_table: float32 [1000, 2048], replicated
- grad_mod_weight: float32 [2048, 12288], P(None, ('dp', 'blk'))
- grad_qkv_weight: float32 [2048, 6144], P(('dp', 'blk'))
- grad_out_weight: float32 [2048, 2048], P(('dp', 'blk'))
- grad_up_weight: float32 [2048, 8192], P(('dp', 'blk'))
- grad_down_weight: float32 [2048, 8192], P(('dp', 'blk'))
Inputs may be any that keep to these rules, and one draw needn't show every extreme that they name: In each group segment numbers never fall along the positions, every number 0 to 2 occurs, and one image of each group covers exactly 672 positions.
All inputs are finite; a program needn't handle non-finite values. No bound on the sum of `key_valid` on one device may be relied on, other than what follows from the above.
Results may differ from a plain program's by a relative error of at most 0.013.
Values may be sent and summed in bfloat16 or wider, within the bound.
A program may use at most 640 MiB of HBM per device.

v0:
```python
import math

import jax
import jax.numpy as jnp
from jax import lax
from jax.sharding import PartitionSpec as P

HEADS = 16
HEAD_DIM = 128


EPS = 1e-06
NEG = -1e30
HIGH = lax.Precision.HIGHEST


def norm_mod(value, shift, scale):
    normed = value * lax.rsqrt(jnp.mean(value * value, axis=-1, keepdims=True) + EPS)
    return normed * (1.0 + scale) + shift


def over_rows(left, right, exact=False):
    if exact:
        return lax.dot_general(left, right, (((0,), (0,)), ((), ())), precision=HIGH)
    return lax.dot_general(
        left, right, (((0,), (0,)), ((), ())), preferred_element_type=jnp.float32
    )


def times_t(left, right, exact=False):
    if exact:
        return lax.dot_general(left, right, (((1,), (1,)), ((), ())), precision=HIGH)
    return lax.dot_general(
        left, right, (((1,), (1,)), ((), ())), preferred_element_type=jnp.float32
    )


def on_device(
    tokens,
    noise_table,
    mod_weight,
    qkv_weight,
    out_weight,
    up_weight,
    down_weight,
    segment,
    key_valid,
    noise_level,
    cotangent,
):
    rows = tokens.shape[1]
    width = tokens.shape[2]
    images = noise_level.shape[1]
    heads = HEADS
    head_dim = HEAD_DIM
    factor = 1.0 / math.sqrt(head_dim)
    group_index = lax.axis_index("dp")
    cycle_index = lax.axis_index("blk")
    cycle_size = lax.axis_size("blk")
    x_in = tokens[0].astype(jnp.float32)
    seg_all = segment[0]
    valid_all = key_valid[0]
    offset = cycle_index * rows
    seg_own = lax.dynamic_slice_in_dim(seg_all, offset, rows, 0)
    q_pos = offset + jnp.arange(rows, dtype=jnp.int32)
    levels_flat = noise_level.reshape(-1)
    cond_all = jnp.take(noise_table, levels_flat, axis=0)
    mod_cols = jnp.dot(cond_all, mod_weight, preferred_element_type=jnp.float32)
    mod_all = lax.all_gather(mod_cols, ("dp", "blk"), axis=1, tiled=True)
    mod_own = lax.dynamic_slice_in_dim(mod_all, group_index * images, images, 0)
    picker = (seg_own[:, None] == jnp.arange(images, dtype=jnp.int32)[None, :]).astype(jnp.float32)
    tok_mod = jnp.dot(picker, mod_own, precision=HIGH)
    shift1, scale1, gate1, shift2, scale2, gate2 = jnp.split(tok_mod, 6, axis=1)
    first_f, first_back = jax.vjp(norm_mod, x_in, shift1, scale1)
    first = first_f.astype(jnp.bfloat16)
    attn_w, outp_w = (
        lax.all_gather(qkv_weight, ("dp", "blk"), axis=0, tiled=True),
        lax.all_gather(out_weight, ("dp", "blk"), axis=0, tiled=True),
    )
    qkv = jnp.dot(first, attn_w, preferred_element_type=jnp.float32).astype(jnp.bfloat16)
    queries, key_rows, val_rows = jnp.split(qkv, 3, axis=1)
    q_heads = queries.reshape(rows, heads, head_dim)

    def allowed_mask(start, count):
        k_seg = lax.dynamic_slice_in_dim(seg_all, start, count, 0)
        k_valid = lax.dynamic_slice_in_dim(valid_all, start, count, 0)
        k_pos = start + jnp.arange(count, dtype=jnp.int32)
        return (seg_own[:, None] == k_seg[None, :]) & (
            (k_valid[None, :] == 1) | (q_pos[:, None] == k_pos[None, :])
        )

    top = jnp.full((heads, rows), NEG, jnp.float32)
    key_piece = lax.all_gather(key_rows, "blk", axis=0, tiled=True)
    val_piece = lax.all_gather(val_rows, "blk", axis=0, tiled=True)
    count = key_piece.shape[0]
    scores = (
        jnp.einsum(
            "qhd,khd->hqk",
            q_heads,
            key_piece.reshape(count, heads, head_dim),
            preferred_element_type=jnp.float32,
        )
        * factor
    )
    allowed = allowed_mask(jnp.int32(0), count)[None]
    masked = jnp.where(allowed, scores, NEG)
    new_top = jnp.maximum(top, jnp.max(masked, axis=-1))
    expo = jnp.where(allowed, jnp.exp(masked - new_top[..., None]), 0.0)
    total = jnp.sum(expo, axis=-1)
    accum = jnp.einsum(
        "hqk,khd->hqd",
        expo.astype(jnp.bfloat16),
        val_piece.reshape(count, heads, head_dim),
        preferred_element_type=jnp.float32,
    )
    top, total, accum = (new_top, total, accum)
    mixed_f = (accum / total[..., None]).transpose(1, 0, 2).reshape(rows, width)
    log_total = top + jnp.log(total)
    mixed = mixed_f.astype(jnp.bfloat16)
    attn = jnp.dot(mixed, outp_w, preferred_element_type=jnp.float32)
    x_mid = x_in + gate1 * attn
    second_f, second_back = jax.vjp(norm_mod, x_mid, shift2, scale2)
    second = second_f.astype(jnp.bfloat16)
    up_w, down_w = (
        lax.all_gather(up_weight, ("dp", "blk"), axis=0, tiled=True),
        lax.all_gather(down_weight, ("dp", "blk"), axis=0, tiled=True),
    )
    hidden_pre = jnp.dot(second, up_w, preferred_element_type=jnp.float32)
    hidden_f, gelu_back = jax.vjp(jax.nn.gelu, hidden_pre)
    hidden = hidden_f.astype(jnp.bfloat16)
    branch = times_t(hidden, down_w)
    block_out = (x_mid + gate2 * branch).astype(jnp.bfloat16)
    grad_in = cotangent[0].astype(jnp.float32)
    d_branch = (gate2 * grad_in).astype(jnp.bfloat16)
    d_gate2 = grad_in * branch
    fresh = lax.optimization_barrier((qkv_weight, out_weight, up_weight, down_weight, d_branch))
    attn_w, outp_w = (
        lax.all_gather(fresh[0], ("dp", "blk"), axis=0, tiled=True),
        lax.all_gather(fresh[1], ("dp", "blk"), axis=0, tiled=True),
    )
    up_w, down_w = (
        lax.all_gather(fresh[2], ("dp", "blk"), axis=0, tiled=True),
        lax.all_gather(fresh[3], ("dp", "blk"), axis=0, tiled=True),
    )
    d_hidden = jnp.dot(d_branch, down_w, preferred_element_type=jnp.float32)
    d_pre = gelu_back(d_hidden)[0].astype(jnp.bfloat16)
    d_second = times_t(d_pre, up_w)
    d_mid_norm, d_shift2, d_scale2 = second_back(d_second)
    d_mid = grad_in + d_mid_norm
    d_attn = (gate1 * d_mid).astype(jnp.bfloat16)
    d_gate1 = d_mid * attn
    d_mixed = times_t(d_attn, outp_w).astype(jnp.bfloat16)
    keys_all, vals_all = (
        lax.all_gather(key_rows, "blk", axis=0, tiled=True),
        lax.all_gather(val_rows, "blk", axis=0, tiled=True),
    )
    d_heads = d_mixed.reshape(rows, heads, head_dim)
    delta = jnp.sum(d_heads.astype(jnp.float32) * mixed_f.reshape(rows, heads, head_dim), axis=-1).T

    def back_piece(dq_total, index):
        start = index * rows
        key_piece = lax.dynamic_slice_in_dim(keys_all, start, rows, 0).reshape(
            rows, heads, head_dim
        )
        val_piece = lax.dynamic_slice_in_dim(vals_all, start, rows, 0).reshape(
            rows, heads, head_dim
        )
        scores = (
            jnp.einsum("qhd,khd->hqk", q_heads, key_piece, preferred_element_type=jnp.float32)
            * factor
        )
        allowed = allowed_mask(start, rows)[None]
        prob = jnp.where(allowed, jnp.exp(scores - log_total[..., None]), 0.0)
        d_prob = jnp.einsum("qhd,khd->hqk", d_heads, val_piece, preferred_element_type=jnp.float32)
        d_scores = (prob * (d_prob - delta[..., None])).astype(jnp.bfloat16)
        dq_total = dq_total + jnp.einsum(
            "hqk,khd->qhd", d_scores, key_piece, preferred_element_type=jnp.float32
        )
        dk_piece = (
            jnp.einsum("hqk,qhd->khd", d_scores, q_heads, preferred_element_type=jnp.float32)
            * factor
        )
        dv_piece = jnp.einsum(
            "hqk,qhd->khd", prob.astype(jnp.bfloat16), d_heads, preferred_element_type=jnp.float32
        )
        return (dq_total, (dk_piece, dv_piece))

    dq_heads, (dk_parts, dv_parts) = lax.scan(
        back_piece,
        jnp.zeros((rows, heads, head_dim), jnp.float32),
        jnp.arange(cycle_size, dtype=jnp.int32),
    )
    dk_group = dk_parts.reshape(cycle_size * rows, width)
    dv_group = dv_parts.reshape(cycle_size * rows, width)
    dk_own, dv_own = (
        lax.psum_scatter(dk_group, "blk", scatter_dimension=0, tiled=True),
        lax.psum_scatter(dv_group, "blk", scatter_dimension=0, tiled=True),
    )
    d_qkv = jnp.concatenate(
        [dq_heads.reshape(rows, width) * factor, dk_own, dv_own], axis=1
    ).astype(jnp.bfloat16)
    d_first = times_t(d_qkv, attn_w)
    d_in_norm, d_shift1, d_scale1 = first_back(d_first)
    grad_tokens = (d_mid + d_in_norm)[None]
    attn_grads = lax.psum_scatter(
        jnp.concatenate([over_rows(first, d_qkv), over_rows(mixed, d_attn)], axis=1),
        ("dp", "blk"),
        scatter_dimension=0,
        tiled=True,
    )
    mlp_grads = lax.psum_scatter(
        jnp.concatenate([over_rows(second, d_pre), over_rows(d_branch, hidden)], axis=1),
        ("dp", "blk"),
        scatter_dimension=0,
        tiled=True,
    )
    tok_grads = jnp.concatenate([d_shift1, d_scale1, d_gate1, d_shift2, d_scale2, d_gate2], axis=1)
    image_grads = over_rows(picker, tok_grads, True)
    placed = lax.dynamic_update_slice_in_dim(
        jnp.zeros((levels_flat.shape[0], 6 * width), jnp.float32),
        image_grads,
        group_index * images,
        0,
    )
    mod_grad_cols = lax.psum_scatter(placed, ("dp", "blk"), scatter_dimension=1, tiled=True)
    grad_mod_weight = over_rows(cond_all.astype(jnp.float32), mod_grad_cols, True)
    cond_grads = lax.psum(
        times_t(mod_grad_cols, mod_weight.astype(jnp.float32), True), ("dp", "blk")
    )
    grad_table = jax.ops.segment_sum(cond_grads, levels_flat, num_segments=noise_table.shape[0])
    grad_qkv_weight = attn_grads[:, : 3 * width]
    grad_out_weight = attn_grads[:, 3 * width :]
    ff_width = up_weight.shape[1]
    grad_up_weight = mlp_grads[:, :ff_width]
    grad_down_weight = mlp_grads[:, ff_width:]
    return (
        block_out[None],
        grad_tokens,
        grad_table,
        grad_mod_weight,
        grad_qkv_weight,
        grad_out_weight,
        grad_up_weight,
        grad_down_weight,
    )


def solution(mesh):
    placed = (
        P("dp", "blk", None),
        P(),
        P(None, ("dp", "blk")),
        P(("dp", "blk"), None),
        P(("dp", "blk"), None),
        P(("dp", "blk"), None),
        P(("dp", "blk"), None),
        P("dp", None),
        P("dp", None),
        P(),
        P("dp", "blk", None),
    )
    return jax.shard_map(
        on_device,
        mesh=mesh,
        in_specs=placed,
        out_specs=(
            P("dp", "blk", None),
            P("dp", "blk", None),
            P(),
            P(None, ("dp", "blk")),
            P(("dp", "blk"), None),
            P(("dp", "blk"), None),
            P(("dp", "blk"), None),
            P(("dp", "blk"), None),
        ),
        check_vma=False,
    )
```

profile of v0, /device:TPU:0, one launch (start us, length us, event | category | flops | bytes accessed | tf_op | source)
XLA Modules:
  0.0 4466.8 jit_solution(4362384468961417561)
XLA Ops:
  14.5 53.6 %all-gather.12.cloned.1.call-done = f32[24,12288]{1,0:T(8,128)} async-done(((f32[24,384]{1,0:T(8,128)}), f32[24,12288]{1,0:T(8,128)}) %all-gather.12.cloned.1.call-update) | async-done | bytes 1179664 | tf_op jit(solution)/shard_map/all_gather | solution.py:69
  77.2 148.0 %all-gather.14.cloned.1.call-done = bf16[2048,6144]{1,0:T(8,128)(2,1)} async-done(((bf16[64,6144]{1,0:T(8,128)(2,1)}), bf16[2048,6144]{1,0:T(8,128)(2,1)}) %all-gather.14.cloned.1.call-update) | async-done | bytes 25165840 | tf_op jit(solution)/shard_map/all_gather | solution.py:77
  225.2 11.1 convolution_convert_fusion
  239.5 25.1 all-gather.16.cloned.1.call-done
  275.4 19.7 all-gather.18.cloned.1.call-done
  301.8 73.6 %all-gather.20.cloned.1.call-done = bf16[2048,2048]{1,0:T(8,128)(2,1)} async-done(((bf16[64,2048]{1,0:T(8,128)(2,1)}), bf16[2048,2048]{1,0:T(8,128)(2,1)}) %all-gather.20.cloned.1.call-update) | async-done | bytes 8388624 | tf_op jit(solution)/shard_map/all_gather | solution.py:78
  391.0 190.0 %all-gather.26.cloned.1.call-done = bf16[2048,8192]{1,0:T(8,128)(2,1)} async-done(((bf16[64,8192]{1,0:T(8,128)(2,1)}), bf16[2048,8192]{1,0:T(8,128)(2,1)}) %all-gather.26.cloned.1.call-update) | async-done | bytes 33554448 | tf_op jit(solution)/shard_map/all_gather | solution.py:143
  580.9 17.8 fusion.94
  598.7 178.1 %all-gather.22.cloned.1.call-done = bf16[2048,8192]{1,0:T(8,128)(2,1)} async-done(((bf16[64,8192]{1,0:T(8,128)(2,1)}), bf16[2048,8192]{1,0:T(8,128)(2,1)}) %all-gather.22.cloned.1.call-update) | async-done | bytes 33554448 | tf_op jit(solution)/shard_map/all_gather | solution.py:125
  776.8 21.9 fusion.31
  798.6 174.0 %all-gather.28.cloned.1.call-done = bf16[2048,8192]{1,0:T(8,128)(2,1)} async-done(((bf16[64,8192]{1,0:T(8,128)(2,1)}), bf16[2048,8192]{1,0:T(8,128)(2,1)}) %all-gather.28.cloned.1.call-update) | async-done | bytes 33554448 | tf_op jit(solution)/shard_map/all_gather | solution.py:142
  972.6 19.5 multiply_reduce_fusion.1
  992.1 176.3 %all-gather.24.cloned.1.call-done = bf16[2048,8192]{1,0:T(8,128)(2,1)} async-done(((bf16[64,8192]{1,0:T(8,128)(2,1)}), bf16[2048,8192]{1,0:T(8,128)(2,1)}) %all-gather.24.cloned.1.call-update) | async-done | bytes 33554448 | tf_op jit(solution)/shard_map/all_gather | solution.py:126
  1168.5 18.8 fusion.92
  1193.6 53.3 %all-gather.30.cloned.1.call-done = bf16[2048,2048]{1,0:T(8,128)(2,1)} async-done(((bf16[64,2048]{1,0:T(8,128)(2,1)}), bf16[2048,2048]{1,0:T(8,128)(2,1)}) %all-gather.30.cloned.1.call-update) | async-done | bytes 8388624 | tf_op jit(solution)/shard_map/all_gather | solution.py:139
  1255.3 66.7 %while.15 = (s32[]{:T(128)}, f32[192,16,128]{2,0,1:T(8,128)}, f32[4,192,16,128]{3,2,1,0:T(8,128)}, f32[4,192,16,128]{3,2,1,0:T(8,128)}, s32[4]{0:T(128)S(1)}, /*...) while((s32[]{:T(128)}, f32[192,16,128]{2,0,1:T(8,128)}, ...), condition=%wide.region_7.8_spmd.clone, body=%wide.region_6.7_spmd.clone.sunk | while | flops 762200640 | bytes 60317248 | solution.py:188
  1322.0 8.5 copy.129
  1330.5 9.5 copy.130
  1342.6 27.6 fusion.91
  1370.2 17.4 reduce-scatter.7.cloned.1.call-done
  1390.0 58.6 %reduce-scatter.5.cloned.1.call-done = f32[192,2048]{1,0:T(8,128)} async-done(((f32[768,2048]{1,0:T(8,128)}), f32[192,2048]{1,0:T(8,128)}) %reduce-scatter.5.cloned.1.call-update) | async-done | bytes 1572880 | tf_op jit(solution)/shard_map/reduce_scatter | solution.py:196
  1451.0 155.1 %all-gather.32.cloned.1.call-done = bf16[2048,6144]{1,0:T(8,128)(2,1)} async-done(((bf16[64,6144]{1,0:T(8,128)(2,1)}), bf16[2048,6144]{1,0:T(8,128)(2,1)}) %all-gather.32.cloned.1.call-update) | async-done | bytes 25165840 | tf_op jit(solution)/shard_map/all_gather | solution.py:138
  1606.1 15.4 constant_dynamic-update-slice_fusion.1
  1632.3 7.6 fusion.75
  1644.0 25.7 fusion.96
  1669.8 68.6 %reduce-scatter.9.cloned.1.call-done = f32[24,384]{1,0:T(8,128)} async-done(((f32[24,12288]{1,0:T(8,128)}), f32[24,384]{1,0:T(8,128)}) %reduce-scatter.9.cloned.1.call-update) | async-done | bytes 36880 | tf_op jit(solution)/shard_map/reduce_scatter | solution.py:225
  1741.2 87.5 %pad_maximum_fusion = f32[2048,16384]{1,0:T(8,128)} fusion(f32[2048,8192]{1,0:T(8,128)} %fusion.91, f32[2048,8192]{1,0:T(8,128)} %fusion.96), kind=kLoop, calls=%fused_computation.32 | loop fusion | flops 33554432 | bytes 268435456 | tf_op jit(solution)/shard_map/concatenate | solution.py:212
  1830.3 8.1 fusion.65
  1838.4 21.1 fusion.61
  1859.5 44.5 pad_maximum_fusion.1
  1913.1 1838.2 %all-reduce.6.cloned.1.call-done = f32[2048,16384]{1,0:T(8,128)} async-done(((f32[2048,16384]{1,0:T(8,128)}), f32[2048,16384]{1,0:T(8,128)}) %all-reduce.6.cloned.1.call-update) | async-done | bytes 134217744
  3756.4 699.1 %reduce-scatter.11.cloned.1.call-done = f32[64,8192]{1,0:T(8,128)} async-done(((f32[2048,8192]{1,0:T(8,128)}), f32[64,8192]{1,0:T(8,128)}) %reduce-scatter.11.cloned.1.call-update) | async-done | bytes 2097168 | tf_op jit(solution)/shard_map/reduce_scatter | solution.py:205
  (263 shorter events, 175.9 us)
Async XLA Ops:
  7.2 60.8 %all-gather.12.cloned.1.call-start = ((), (), s32[]{:S(2)}) async-start(), calls=%async_computation.4 | async-start | bytes 1216512 | tf_op jit(solution)/shard_map/all_gather | solution.py:69
  8.8 59.2 %copy-start.42 = (pred[24]{0:T(512)(128)(4,1)}, pred[24]{0:T(512)(128)(4,1)S(1)}, u32[]{:S(2)}) copy-start(pred[24]{0:T(512)(128)(4,1)S(1)} %compare_and_fusion) | copy-start | bytes 76
  12.3 55.8 %copy-start.31 = (bf16[24,2048]{1,0:T(8,128)(2,1)}, bf16[24,2048]{1,0:T(8,128)(2,1)S(1)}, u32[]{:S(2)}) copy-start(bf16[24,2048]{1,0:T(8,128)(2,1)S(1)} %gather_fusion) | copy-start | bytes 294916
  13.3 211.9 %all-gather.14.cloned.1.call-start = ((), (), s32[]{:S(2)}) async-start(), calls=%async_computation.5 | async-start | bytes 25952256 | tf_op jit(solution)/shard_map/all_gather | solution.py:77
  14.0 250.5 %all-gather.16.cloned.1.call-start = ((), (), s32[]{:S(2)}) async-start(), calls=%async_computation.6 | async-start | bytes 3932160 | tf_op jit(solution)/shard_map/all_gather | solution.py:93
  14.4 58.6 %copy-start.39 = (f32[192]{0:T(256)}, f32[192]{0:T(256)S(1)}, u32[]{:S(2)}) copy-start(f32[192]{0:T(256)S(1)} %fusion.51) | copy-start | bytes 2308
  14.4 58.6 %copy-start.37 = (f32[192]{0:T(256)}, f32[192]{0:T(256)S(1)}, u32[]{:S(2)}) copy-start(f32[192]{0:T(256)S(1)} %fusion.80) | copy-start | bytes 2308
  77.2 159.2 %copy-start.28 = (bf16[192,2048]{1,0:T(8,128)(2,1)}, bf16[192,2048]{1,0:T(8,128)(2,1)S(1)}, u32[]{:S(2)}) copy-start(bf16[192,2048]{1,0:T(8,128)(2,1)S(1)} %fusion.45) | copy-start | bytes 2359300
  237.7 31.0 copy-start.18
  237.7 57.4 %all-gather.18.cloned.1.call-start = ((), (), s32[]{:S(2)}) async-start(), calls=%async_computation.7 | async-start | bytes 3932160 | tf_op jit(solution)/shard_map/all_gather | solution.py:94
  238.3 137.0 %all-gather.20.cloned.1.call-start = ((), (), s32[]{:S(2)}) async-start(), calls=%async_computation.8 | async-start | bytes 8650752 | tf_op jit(solution)/shard_map/all_gather | solution.py:78
  238.9 342.0 %all-gather.26.cloned.1.call-start = ((), (), s32[]{:S(2)}) async-start(), calls=%async_computation.11 | async-start | bytes 34603008 | tf_op jit(solution)/shard_map/all_gather | solution.py:143
  301.7 80.8 %copy-start.11 = (f32[192,16,128]{2,0,1:T(8,128)}, f32[192,16,128]{2,0,1:T(8,128)S(1)}, u32[]{:S(2)}) copy-start(f32[192,16,128]{2,0,1:T(8,128)S(1)} %bitcast_divide_fusion) | copy-start | bytes 4718596
  387.4 389.4 %all-gather.22.cloned.1.call-start = ((), (), s32[]{:S(2)}) async-start(), calls=%async_computation.9 | async-start | bytes 34603008 | tf_op jit(solution)/shard_map/all_gather | solution.py:125
  388.1 584.5 %all-gather.28.cloned.1.call-start = ((), (), s32[]{:S(2)}) async-start(), calls=%async_computation.12 | async-start | bytes 34603008 | tf_op jit(solution)/shard_map/all_gather | solution.py:142
  388.9 779.6 %all-gather.24.cloned.1.call-start = ((), (), s32[]{:S(2)}) async-start(), calls=%async_computation.10 | async-start | bytes 34603008 | tf_op jit(solution)/shard_map/all_gather | solution.py:126
  389.6 857.2 %all-gather.30.cloned.1.call-start = ((), (), s32[]{:S(2)}) async-start(), calls=%async_computation.13 | async-start | bytes 8650752 | tf_op jit(solution)/shard_map/all_gather | solution.py:139
  390.2 997.4 %reduce-scatter.7.cloned.1.call-start = ((), (), s32[]{:S(2)}) async-start(), calls=%async_computation.15 | async-start | bytes 7864320 | tf_op jit(solution)/shard_map/reduce_scatter | solution.py:197
  390.9 385.8 %copy-start.26 = (bf16[192,2048]{1,0:T(8,128)(2,1)S(1)}, bf16[192,2048]{1,0:T(8,128)(2,1)}, u32[]{:S(2)}) copy-start(bf16[192,2048]{1,0:T(8,128)(2,1)} %get-tuple-element.234) | copy-start | bytes 2359300
  1168.5 18.8 copy-start.21
  1330.5 118.0 %reduce-scatter.5.cloned.1.call-start = ((), (), s32[]{:S(2)}) async-start(), calls=%async_computation.14 | async-start | bytes 7864320 | tf_op jit(solution)/shard_map/reduce_scatter | solution.py:196
  1340.1 266.0 %all-gather.32.cloned.1.call-start = ((), (), s32[]{:S(2)}) async-start(), calls=%async_computation.16 | async-start | bytes 25952256 | tf_op jit(solution)/shard_map/all_gather | solution.py:138
  1340.8 397.5 %reduce-scatter.9.cloned.1.call-start = ((), (), s32[]{:S(2)}) async-start(), calls=%async_computation.17 | async-start | bytes 1216512 | tf_op jit(solution)/shard_map/reduce_scatter | solution.py:225
  1451.0 170.5 %copy-start.40 = (f32[192]{0:T(256)S(1)}, f32[192]{0:T(256)}, u32[]{:S(2)}) copy-start(f32[192]{0:T(256)} %copy-done.39) | copy-start | bytes 2308
  1451.0 170.5 %copy-start.15 = (f32[192,2048]{1,0:T(8,128)S(1)}, f32[192,2048]{1,0:T(8,128)}, u32[]{:S(2)}) copy-start(f32[192,2048]{1,0:T(8,128)} %get-tuple-element.225) | copy-start | bytes 4718596
  1451.0 170.5 %copy-start.38 = (f32[192]{0:T(256)S(1)}, f32[192]{0:T(256)}, u32[]{:S(2)}) copy-start(f32[192]{0:T(256)} %copy-done.37) | copy-start | bytes 2308
  1606.1 15.4 copy-start.17
  1644.0 264.1 %all-reduce.4.cloned.1.call-start = ((), (), s32[]{:S(2)}) async-start(), calls=%async_computation.18 | async-start | bytes 393216 | tf_op jit(solution)/shard_map/psum | solution.py:227
  1741.1 2010.2 %all-reduce.6.cloned.1.call-start = ((), (), s32[]{:S(2)}) async-start(), calls=%async_computation.20 | async-start | bytes 268435456
  1828.7 9.7 copy-start.29
  1828.8 2626.8 %reduce-scatter.11.cloned.1.call-start = ((), (), s32[]{:S(2)}) async-start(), calls=%async_computation.19 | async-start | bytes 69206016 | tf_op jit(solution)/shard_map/reduce_scatter | solution.py:205
  3751.4 708.7 %copy-start.1 = (bf16[2048,384]{1,0:T(8,128)(2,1)S(1)}, bf16[2048,384]{1,0:T(8,128)(2,1)}, u32[]{:S(2)}) copy-start(bf16[2048,384]{1,0:T(8,128)(2,1)} %param.15) | copy-start | bytes 4718596
  (48 other events, 155.8 us)
Sparse Core Ops, SparseCore 0:
  13.4 54.5 all-gather.11
  70.9 154.3 all-gather.13
  237.8 26.6 all-gather.15
  266.6 28.5 all-gather.17
  297.9 77.4 all-gather.19
  387.5 193.3 all-gather.25
  583.8 192.9 all-gather.21
  779.6 192.9 all-gather.27
  975.5 192.9 all-gather.23
  1171.2 75.6 all-gather.29
  1330.6 56.9 reduce-scatter.6
  1390.1 58.3 reduce-scatter.4
  1451.4 154.6 all-gather.31
  1644.1 94.1 reduce-scatter.8
  1744.3 122.1 all-reduce.3
  1872.7 1878.5 all-reduce.5
  3753.6 701.8 reduce-scatter.10
where the time goes:
time: 4480 us; the launch traced here: 4470 us
  waiting for transfers between devices  3930 us (88%)
  matrix products  271 us (6%)
  other arithmetic  168 us (4%)
  local copies, waits for them, and re-layouts  75.2 us (2%)
    unnamed x18, waiting for transfers between devices  1840 us
    reduce_scatter x1, waiting for transfers between devices, on_device(): lax.psum_scatter(jnp.concatenate([over_rows(first, d_qkv), over_rows(mixe...  699 us
    all_gather x1, waiting for transfers between devices, on_device(): lax.all_gather(fresh[3], ('dp', 'blk'), axis=0, tiled=True)  190 us
    all_gather x1, waiting for transfers between devices, on_device(): lax.all_gather(up_weight, ('dp', 'blk'), axis=0, tiled=True)  178 us
    all_gather x1, waiting for transfers between devices, on_device(): lax.all_gather(down_weight, ('dp', 'blk'), axis=0, tiled=True)  176 us
    all_gather x1, waiting for transfers between devices, on_device(): lax.all_gather(fresh[2], ('dp', 'blk'), axis=0, tiled=True)  174 us
    all_gather x1, waiting for transfers between devices, on_device(): lax.all_gather(fresh[0], ('dp', 'blk'), axis=0, tiled=True)  155 us
    all_gather x1, waiting for transfers between devices, on_device(): lax.all_gather(qkv_weight, ('dp', 'blk'), axis=0, tiled=True)  148 us
  transfers between devices with their start and end apart: 17, of which 16 were waited for; matrix products, arithmetic and copies ran while one was open for 8% of the time, Pallas kernels for 0%

commit v1 on v0

v1 whole, which is shorter than its diff:
```python
import functools
import math

import jax
import jax.numpy as jnp
from jax import lax
from jax.experimental import pallas as pl
from jax.experimental.pallas import tpu as pltpu
from jax.sharding import Mesh
from jax.sharding import PartitionSpec as P

HEADS = 16
HEAD_DIM = 128
EPS = 1e-06
NEG = -1e30
HIGH = lax.Precision.HIGHEST
PLANE = 8
BF = jnp.bfloat16
F32 = jnp.float32
ALL = ("z", "y", "blk")
MIB = 1 << 20


def peer(k):
    y, b = lax.axis_index("y"), lax.axis_index("blk")
    high, low = lax.div(b, 2), lax.rem(b, 2)
    if k & 4:
        y = 1 - y
    if k & 2:
        high = 1 - high
    if k & 1:
        low = 1 - low
    return {"y": y, "blk": high * 2 + low}


def place(k):
    where = peer(k)
    return where["y"] * 4 + where["blk"]


def greet(peers):
    barrier = pltpu.get_barrier_semaphore()
    for k in peers:
        pl.semaphore_signal(
            barrier, inc=1, device_id=peer(k), device_id_type=pl.DeviceIdType.MESH
        )
    pl.semaphore_wait(barrier, len(peers))


def send(src, dst, ssem, rsem, k):
    copy = pltpu.make_async_remote_copy(
        src_ref=src,
        dst_ref=dst,
        send_sem=ssem,
        recv_sem=rsem,
        device_id=peer(k),
        device_id_type=pl.DeviceIdType.MESH,
    )
    copy.start()
    return copy


def call(kernel, ins, outs, scratch, ident, vmem=16, moved=0):
    return pl.pallas_call(
        kernel,
        out_shape=outs,
        in_specs=[pl.BlockSpec(memory_space=pl.ANY)] * len(ins),
        out_specs=jax.tree.map(lambda _: pl.BlockSpec(memory_space=pl.ANY), outs),
        scratch_shapes=scratch,
        compiler_params=pltpu.CompilerParams(
            collective_id=ident, has_side_effects=True, vmem_limit_bytes=vmem * MIB
        ),
        cost_estimate=pl.CostEstimate(flops=0, bytes_accessed=moved, transcendentals=0),
    )(*ins)


def gather_kernel(x, o, lsem, ssem, rsem):
    rows = x.shape[0]
    half = rows // 2
    top, bot = pl.ds(0, half), pl.ds(half, half)
    greet((1, 2, 4))
    own = pltpu.make_async_copy(x, o.at[0], lsem)
    own.start()
    go = lambda i, src, dst, k: send(src, dst, ssem.at[i], rsem.at[i], k)
    x_bot = go(0, x.at[bot], o.at[2, bot], 2)
    y_top = go(1, x.at[top], o.at[4, top], 4)
    x_top = go(2, x.at[top], o.at[2, top], 2)
    y_bot = go(3, x.at[bot], o.at[4, bot], 4)
    sib = go(4, x, o.at[1], 1)
    x_bot.wait_recv()
    dy = go(5, o.at[2, bot], o.at[6, bot], 4)
    c0 = go(6, o.at[2, bot], o.at[3, bot], 1)
    y_top.wait_recv()
    dx = go(7, o.at[4, top], o.at[6, top], 2)
    c1 = go(8, o.at[4, top], o.at[5, top], 1)
    x_top.wait_recv()
    c2 = go(9, o.at[2, top], o.at[3, top], 1)
    y_bot.wait_recv()
    c3 = go(10, o.at[4, bot], o.at[5, bot], 1)
    dx.wait_recv()
    c4 = go(11, o.at[6, top], o.at[7, top], 1)
    dy.wait_recv()
    c5 = go(12, o.at[6, bot], o.at[7, bot], 1)
    for copy in (sib, c0, c1, c2, c3, c4, c5):
        copy.wait_recv()
    for copy in (x_bot, y_top, x_top, y_bot, sib, dy, c0, dx, c1, c2, c3, c4, c5):
        copy.wait_send()
    own.wait()


def plane_gather(x, ident):
    out = jax.ShapeDtypeStruct((PLANE,) + x.shape, x.dtype)
    dma = pltpu.SemaphoreType.DMA
    return call(
        gather_kernel, (x,), out, [dma, dma((13,)), dma((13,))], ident, 4, 8 * x.size * 16
    )


def rows_loop(rows, body):
    step = 16

    def one(i, carry):
        body(pl.ds(pl.multiple_of(i * step, step), step))
        return carry

    lax.fori_loop(0, rows // step, one, 0)


def scatter_kernel(p, o, pv, rc, q6, q2, q4, d6, rx, ry, ov, lsem, ssem, rsem):
    rows = o.shape[0]
    half = rows // 2
    top, bot = pl.ds(0, half), pl.ds(half, half)
    greet((1, 2, 4))
    go = lambda i, src, dst, k: send(src, dst, ssem.at[i], rsem.at[i], k)
    load = [pltpu.make_async_copy(p.at[2 * i], pv.at[i], lsem.at[i]) for i in range(4)]
    c7t = go(0, p.at[7, top], rc.at[3, top], 1)
    load[3].start()
    c7b = go(1, p.at[7, bot], rc.at[3, bot], 1)
    load[1].start()
    c3 = go(2, p.at[3], rc.at[1], 1)
    load[2].start()
    c5 = go(3, p.at[5], rc.at[2], 1)
    load[0].start()
    c1 = go(4, p.at[1], rc.at[0], 1)

    def add2(dst, i, start):
        def body(r):
            s = pl.ds(pl.multiple_of(start + r.start, 16), r.size)
            dst[r, :] = (pv[i, s, :].astype(F32) + rc[i, s, :].astype(F32)).astype(BF)

        rows_loop(half, body)

    def add3(dst, i, start, more):
        def body(r):
            s = pl.ds(pl.multiple_of(start + r.start, 16), r.size)
            total = pv[i, s, :].astype(F32) + rc[i, s, :].astype(F32) + more[r, :].astype(F32)
            dst[r, :] = total.astype(BF)

        rows_loop(half, body)

    load[3].wait()
    c7t.wait_recv()
    add2(q6.at[0], 3, 0)
    s6t = go(5, q6.at[0], d6.at[0], 2)
    c7b.wait_recv()
    add2(q6.at[1], 3, half)
    s6b = go(6, q6.at[1], d6.at[1], 4)
    load[1].wait()
    c3.wait_recv()
    add2(q2.at[0], 1, 0)
    s2t = go(7, q2.at[0], rx.at[0], 2)
    load[2].wait()
    c5.wait_recv()
    add2(q4.at[1], 2, half)
    s4b = go(8, q4.at[1], ry.at[1], 4)
    s6t.wait_recv()
    add3(q4.at[0], 2, 0, d6.at[0])
    s4t = go(9, q4.at[0], ry.at[0], 4)
    s6b.wait_recv()
    add3(q2.at[1], 1, half, d6.at[1])
    s2b = go(10, q2.at[1], rx.at[1], 2)
    load[0].wait()
    c1.wait_recv()
    s2t.wait_recv()
    s4t.wait_recv()

    def finish(n, start):
        def body(r):
            s = pl.ds(pl.multiple_of(start + r.start, 16), r.size)
            total = pv[0, s, :].astype(F32) + rc[0, s, :].astype(F32)
            ov[s, :] = total + rx[n, r, :].astype(F32) + ry[n, r, :].astype(F32)

        rows_loop(half, body)

    finish(0, 0)
    out0 = pltpu.make_async_copy(ov.at[top], o.at[top], lsem.at[4])
    out0.start()
    s2b.wait_recv()
    s4b.wait_recv()
    finish(1, half)
    out1 = pltpu.make_async_copy(ov.at[bot], o.at[bot], lsem.at[5])
    out1.start()
    for copy in (c7t, c7b, c3, c5, c1, s6t, s6b, s2t, s4b, s4t, s2b):
        copy.wait_send()
    out0.wait()
    out1.wait()


def plane_scatter(p, ident):
    _, rows, width = p.shape
    half = rows // 2
    dma = pltpu.SemaphoreType.DMA
    pair = pltpu.VMEM((2, half, width), BF)
    scratch = [
        pltpu.VMEM((4, rows, width), BF),
        pltpu.VMEM((4, rows, width), BF),
        pair,
        pair,
        pair,
        pair,
        pair,
        pair,
        pltpu.VMEM((rows, width), F32),
        dma((6,)),
        dma((11,)),
        dma((11,)),
    ]
    out = jax.ShapeDtypeStruct((rows, width), F32)
    return call(scatter_kernel, (p,), out, scratch, ident, 24, 8 * p.size * 2)


def spread_kernel(plan, count, *refs):
    ins, outs = refs[:count], refs[count : 2 * count]
    lsem, ssem, rsem = refs[2 * count :]
    greet(range(1, PLANE))
    mine = place(0)
    locals_, remotes = [], []
    for n, (w, base, width, col) in enumerate(plan):
        rows = ins[w].shape[0]
        here = pl.ds(pl.multiple_of(mine * rows, 16), rows)
        for k in range(1, PLANE):
            cols = pl.ds(pl.multiple_of(base + place(k) * width, 128), width)
            remotes.append(
                send(
                    ins[w].at[:, cols],
                    outs[w].at[here, pl.ds(col, width)],
                    ssem.at[n, k],
                    rsem.at[n, k],
                    k,
                )
            )
        cols = pl.ds(pl.multiple_of(base + mine * width, 128), width)
        copy = pltpu.make_async_copy(
            ins[w].at[:, cols], outs[w].at[here, pl.ds(col, width)], lsem.at[n]
        )
        copy.start()
        locals_.append(copy)
    for copy in remotes:
        copy.wait()
    for copy in locals_:
        copy.wait()


def spread(weights, ident, blocks=1):
    plan, outs = [], []
    for i, w in enumerate(weights):
        rows, cols = w.shape
        each = cols // blocks
        for b in range(blocks):
            plan.append((i, b * each, each // PLANE, b * (each // PLANE)))
        outs.append(jax.ShapeDtypeStruct((rows * PLANE, cols // PLANE), w.dtype))
    dma = pltpu.SemaphoreType.DMA
    n = len(plan)
    return call(
        functools.partial(spread_kernel, plan, len(weights)),
        tuple(weights),
        outs,
        [dma((n,)), dma((n, PLANE)), dma((n, PLANE))],
        ident,
        4,
        sum(w.size for w in weights) * 16,
    )


def collect_kernel(plan, count, *refs):
    ins, outs = refs[:count], refs[count : 2 * count]
    lsem, ssem, rsem = refs[2 * count :]
    greet(range(1, PLANE))
    mine = place(0)
    locals_, remotes = [], []
    for n, (w, base, width, col) in enumerate(plan):
        rows = outs[w].shape[0]
        cols = pl.ds(pl.multiple_of(base + mine * width, 128), width)
        for k in range(1, PLANE):
            there = pl.ds(pl.multiple_of(place(k) * rows, 16), rows)
            remotes.append(
                send(
                    ins[w].at[there, pl.ds(col, width)],
                    outs[w].at[:, cols],
                    ssem.at[n, k],
                    rsem.at[n, k],
                    k,
                )
            )
        here = pl.ds(pl.multiple_of(mine * rows, 16), rows)
        copy = pltpu.make_async_copy(
            ins[w].at[here, pl.ds(col, width)], outs[w].at[:, cols], lsem.at[n]
        )
        copy.start()
        locals_.append(copy)
    for copy in remotes:
        copy.wait()
    for copy in locals_:
        copy.wait()


def collect(grads, ident, blocks=1):
    plan, outs = [], []
    for i, g in enumerate(grads):
        rows, cols = g.shape
        each = cols * PLANE // blocks
        for b in range(blocks):
            plan.append((i, b * each, each // PLANE, b * (each // PLANE)))
        outs.append(jax.ShapeDtypeStruct((rows // PLANE, cols * PLANE), g.dtype))
    dma = pltpu.SemaphoreType.DMA
    n = len(plan)
    return call(
        functools.partial(collect_kernel, plan, len(grads)),
        tuple(grads),
        outs,
        [dma((n,)), dma((n, PLANE)), dma((n, PLANE))],
        ident,
        4,
        sum(g.size for g in grads) * 16,
    )


def chain_gather(x, nz):
    z = lax.axis_index("z")
    right, left, rights, lefts = x, x, [], []
    for s in range(1, nz):
        right = lax.ppermute(right, "z", [(i, i + 1) for i in range(s - 1, nz - 1)])
        left = lax.ppermute(left, "z", [(i, i - 1) for i in range(1, nz - s + 1)])
        rights.append(right)
        lefts.append(left)
    out = jnp.zeros((nz,) + x.shape, x.dtype)
    out = lax.dynamic_update_index_in_dim(out, x, z, 0)
    for s in range(1, nz):
        piece = jnp.where(z >= s, rights[s - 1], lefts[nz - s - 1])
        out = lax.dynamic_update_index_in_dim(out, piece, lax.rem(z - s + nz, nz), 0)
    return out.reshape((nz * x.shape[0],) + x.shape[1:]), (rights[-1], lefts[-1])


def chain_scatter(g, nz):
    z = lax.axis_index("z")
    parts = g.reshape((nz, g.shape[0] // nz) + g.shape[1:])

    def take(t):
        t = jnp.clip(t, 0, nz - 1)
        return lax.dynamic_index_in_dim(parts, t, 0, keepdims=False).astype(F32)

    right = left = None
    for s in range(1, nz):
        to_right, to_left = take(z + nz - s), take(z - nz + s)
        if s > 1:
            to_right, to_left = to_right + right.astype(F32), to_left + left.astype(F32)
        right = lax.ppermute(to_right.astype(BF), "z", [(i, i + 1) for i in range(s)])
        left = lax.ppermute(to_left.astype(BF), "z", [(i, i - 1) for i in range(nz - s, nz)])
    return take(z) + right.astype(F32) + left.astype(F32)


def norm_mod(value, shift, scale):
    normed = value * lax.rsqrt(jnp.mean(value * value, axis=-1, keepdims=True) + EPS)
    return normed * (1.0 + scale) + shift


def dot(a, b):
    return jnp.dot(a, b, preferred_element_type=F32)


def over_rows(left, right):
    return lax.dot_general(left, right, (((0,), (0,)), ((), ())), preferred_element_type=F32)


def times_t(left, right):
    return lax.dot_general(left, right, (((1,), (1,)), ((), ())), preferred_element_type=F32)


def after(value, *others):
    return lax.optimization_barrier((value,) + others)[0]


def on_device(
    tokens,
    noise_table,
    mod_weight,
    qkv_weight,
    out_weight,
    up_weight,
    down_weight,
    segment,
    key_valid,
    noise_level,
    cotangent,
):
    rows, width = tokens.shape[1:]
    images = noise_level.shape[1]
    nz = lax.axis_size("z")
    blks = lax.axis_size("blk")
    z, y, blk = (lax.axis_index(a) for a in ALL)
    devices = nz * PLANE
    group = rows * blks
    local = HEADS // PLANE
    factor = 1.0 / math.sqrt(HEAD_DIM)

    levels = noise_level.reshape(-1)
    cond = jnp.take(noise_table, levels, axis=0)
    cols = dot(cond, mod_weight)
    planes = cols.reshape(nz, 1, 2 * images, -1)
    planes = jnp.broadcast_to(planes, (nz, PLANE) + planes.shape[2:])
    mods = lax.all_to_all(
        planes.reshape((devices,) + planes.shape[2:]), ALL, 0, 0, tiled=True
    )
    mods = mods.transpose(1, 0, 2).reshape(2, images, 6, width)
    mods = jnp.where(y == 0, mods, mods[::-1])

    both = jnp.concatenate([segment, key_valid], axis=0)
    other = lax.ppermute(both, "y", [(0, 1), (1, 0)])
    order = lambda a: jnp.stack(
        [
            lax.dynamic_index_in_dim(
                a.reshape(2, blks, rows),
                (lax.div(blk, 2) ^ (k >> 1)) * 2 + (lax.rem(blk, 2) ^ (k & 1)),
                1,
                keepdims=False,
            )
            for k in range(blks)
        ],
        axis=1,
    ).reshape(2, group)
    both, other = order(both), order(other)
    seg = jnp.stack([both[0], other[0]])
    valid = jnp.stack([both[1], other[1]])
    seg_own = seg[0, :rows]

    def pick(which):
        m = mods[:, :, which]
        s = seg[:, :, None]
        out = m[:, images - 1][:, None]
        for i in range(images - 2, -1, -1):
            out = jnp.where(s == i, m[:, i][:, None], out)
        return out

    def pick_own(which):
        m = mods[0, :, which]
        s = seg_own[:, None]
        out = m[images - 1][None]
        for i in range(images - 2, -1, -1):
            out = jnp.where(s == i, m[i][None], out)
        return out

    (qkv_part,) = spread([qkv_weight], 1, blocks=3)
    qkv_w, last = chain_gather(qkv_part, nz)
    x_all = plane_gather(after(tokens[0], qkv_part), 2).reshape(2, group, width)
    move = [(nz * k + i, i * PLANE + k) for k in range(PLANE) for i in range(nz)]
    outp = lax.ppermute(out_weight, ALL, move)
    (up_part,) = spread([after(up_weight, x_all)], 3)
    outp, up_part = lax.optimization_barrier((outp, up_part) + last)[:2]
    outp_w, _ = chain_gather(outp, nz)
    up_w, last = chain_gather(up_part, nz)
    (down_part,) = spread([after(down_weight, up_part)], 4)
    down_part = after(down_part, *last)
    down_w, _ = chain_gather(down_part, nz)
    g_all = plane_gather(after(cotangent[0], down_part), 5).reshape(2, group, width)

    x_f = x_all.astype(F32)
    first = norm_mod(x_f, pick(0), pick(1)).astype(BF).reshape(2 * group, width)
    qkv = dot(first, qkv_w).astype(BF)
    heads = qkv.reshape(2, group, 3, local, HEAD_DIM)
    q_h, k_h, v_h = heads[:, :, 0], heads[:, :, 1], heads[:, :, 2]
    eye = jnp.arange(group)[:, None] == jnp.arange(group)[None, :]
    allowed = (seg[:, :, None] == seg[:, None, :]) & ((valid[:, None, :] == 1) | eye[None])
    allowed = allowed[:, None]
    scores = jnp.einsum("gqhd,gkhd->ghqk", q_h, k_h, preferred_element_type=F32) * factor
    masked = jnp.where(allowed, scores, NEG)
    top = jnp.max(masked, axis=-1)
    expo = jnp.where(allowed, jnp.exp(masked - top[..., None]), 0.0)
    total = jnp.sum(expo, axis=-1)
    prob = expo / total[..., None]
    prob_b = prob.astype(BF)
    mixed = jnp.einsum("ghqk,gkhd->gqhd", prob_b, v_h, preferred_element_type=F32)
    mixed = mixed.astype(BF).reshape(2 * group, local * HEAD_DIM)
    part = dot(mixed, outp_w).astype(BF).reshape(PLANE, rows, width)
    attn = plane_scatter(part, 6)
    x_in = tokens[0].astype(F32)
    shift1, scale1, gate1 = pick_own(0), pick_own(1), pick_own(2)
    shift2, scale2, gate2 = pick_own(3), pick_own(4), pick_own(5)
    x_mid = x_in + gate1 * attn
    second_f, second_back = jax.vjp(norm_mod, x_mid, shift2, scale2)
    second = plane_gather(second_f.astype(BF), 7).reshape(2 * group, width)
    hidden_pre = dot(second, up_w)
    hidden_f, gelu_back = jax.vjp(jax.nn.gelu, hidden_pre)
    hidden = hidden_f.astype(BF)

    d_branch = (pick(5) * g_all.astype(F32)).astype(BF).reshape(2 * group, width)
    d_down = over_rows(d_branch, hidden).astype(BF)
    d_down = chain_scatter(d_down, nz)
    part = times_t(hidden, down_w).astype(BF).reshape(PLANE, rows, width)
    branch = plane_scatter(part, 8)
    block_out = (x_mid + gate2 * branch).astype(BF)
    grad_in = cotangent[0].astype(F32)
    d_gate2 = grad_in * branch
    d_pre = gelu_back(dot(d_branch, down_w))[0].astype(BF)
    part = times_t(d_pre, up_w).astype(BF).reshape(PLANE, rows, width)
    d_up = chain_scatter(over_rows(second, d_pre).astype(BF), nz)
    d_second = plane_scatter(part, 9)
    d_mid_norm, d_shift2, d_scale2 = second_back(d_second)
    d_mid = grad_in + d_mid_norm
    d_attn = (gate1 * d_mid).astype(BF)
    d_gate1 = d_mid * attn
    d_attn_all = plane_gather(d_attn, 10).reshape(2 * group, width)
    d_outp = chain_scatter(over_rows(mixed, d_attn_all).astype(BF), nz)
    d_mixed = times_t(d_attn_all, outp_w).astype(BF).reshape(2, group, local, HEAD_DIM)
    d_prob = jnp.einsum("gqhd,gkhd->ghqk", d_mixed, v_h, preferred_element_type=F32)
    delta = jnp.sum(prob * d_prob, axis=-1, keepdims=True)
    d_scores = (prob * (d_prob - delta)).astype(BF)
    dq = jnp.einsum("ghqk,gkhd->gqhd", d_scores, k_h, preferred_element_type=F32) * factor
    dk = jnp.einsum("ghqk,gqhd->gkhd", d_scores, q_h, preferred_element_type=F32) * factor
    dv = jnp.einsum("ghqk,gqhd->gkhd", prob_b, d_mixed, preferred_element_type=F32)
    d_qkv = jnp.stack([dq, dk, dv], axis=2).astype(BF).reshape(2 * group, -1)
    part = times_t(d_qkv, qkv_w).astype(BF).reshape(PLANE, rows, width)
    d_qkv_w = chain_scatter(over_rows(first, d_qkv).astype(BF), nz)
    d_first = plane_scatter(part, 11)
    _, first_back = jax.vjp(norm_mod, x_in, shift1, scale1)
    d_in_norm, d_shift1, d_scale1 = first_back(d_first)
    grad_tokens = d_mid + d_in_norm

    tok_grads = jnp.concatenate([d_shift1, d_scale1, d_gate1, d_shift2, d_scale2, d_gate2], axis=1)
    picker = (seg_own[:, None] == jnp.arange(images, dtype=jnp.int32)[None, :]).astype(F32)
    image_grads = lax.dot_general(picker, tok_grads, (((0,), (0,)), ((), ())), precision=HIGH)
    sent = image_grads.reshape(images, devices, -1).transpose(1, 0, 2)
    got = lax.all_to_all(sent, ALL, 0, 0, tiled=True)
    mod_grads = got.reshape(2 * nz, blks, images, -1).sum(axis=1).reshape(2 * nz * images, -1)
    grad_mod = lax.dot_general(
        cond.astype(F32), mod_grads, (((0,), (0,)), ((), ())), precision=HIGH
    )
    cond_part = lax.dot_general(
        mod_grads, mod_weight.astype(F32), (((1,), (1,)), ((), ())), precision=HIGH
    )
    count = cond_part.shape[0]
    sent = cond_part.reshape(count, devices, -1).transpose(1, 0, 2)
    mine = lax.all_to_all(sent, ALL, 0, 0, tiled=True).sum(axis=0)
    sent = jnp.broadcast_to(mine[None], (devices,) + mine.shape)
    cond_grads = lax.all_to_all(sent, ALL, 0, 0, tiled=True)
    cond_grads = cond_grads.transpose(1, 0, 2).reshape(count, width)
    grad_table = jax.ops.segment_sum(cond_grads, levels, num_segments=noise_table.shape[0])

    d_up, d_down = collect([d_up.astype(BF), d_down.astype(BF)], 12)
    (d_qkv_w,) = collect([d_qkv_w.astype(BF)], 13, blocks=3)
    d_outp = lax.ppermute(d_outp, ALL, [(b, a) for a, b in move])
    return (
        block_out[None],
        grad_tokens[None],
        grad_table,
        grad_mod,
        d_qkv_w.astype(F32),
        d_outp,
        d_up.astype(F32),
        d_down.astype(F32),
    )


def solution(mesh):
    groups, blks = mesh.shape["dp"], mesh.shape["blk"]
    planes = Mesh(mesh.devices.reshape(groups // 2, 2, blks), ALL)
    dp = ("z", "y")
    whole = ("z", "y", "blk")
    placed = (
        P(dp, "blk", None),
        P(),
        P(None, whole),
        P(whole, None),
        P(whole, None),
        P(whole, None),
        P(whole, None),
        P(dp, None),
        P(dp, None),
        P(),
        P(dp, "blk", None),
    )
    return jax.shard_map(
        on_device,
        mesh=planes,
        in_specs=placed,
        out_specs=(
            P(dp, "blk", None),
            P(dp, "blk", None),
            P(),
            P(None, whole),
            P(whole, None),
            P(whole, None),
            P(whole, None),
            P(whole, None),
        ),
        check_vma=False,
    )
```

time: 4480 us -> 1010 us (0.23)
  waiting for transfers between devices: 3930 us -> 97 us
  Pallas kernels: 0 us -> 388 us
  starting transfers between devices: 1.29 us -> 171 us
  matrix products: 271 us -> 128 us
  other arithmetic: 168 us -> 119 us
    unnamed x18 -> x0, waiting for transfers between devices: 1840 us -> none
    all_gather x11 -> x0, waiting for transfers between devices: 1250 us -> none  [the longest x1 190 us: on_device(): lax.all_gather(fresh[3], ('dp', 'blk'), axis=0, tiled=True)]
    reduce_scatter x4 -> x0, waiting for transfers between devices: 844 us -> none  [the longest x1 699 us: on_device(): lax.psum_scatter(jnp.concatenate([over_rows(first, d_qkv), over_rows(mixe...]
    pallas_call x0 -> x13, Pallas kernels: none -> 388 us  [call(): pl.pallas_call(kernel, out_shape=outs, in_specs=[pl.BlockSpec(memory_spac...]
    ppermute x0 -> x51, starting transfers between devices: none -> 151 us  [the longest x12 78 us: chain_scatter(): lax.ppermute(to_right.astype(BF), 'z', [(i, i + 1) for i in range(s)])]
    concatenate x2 -> x1, other arithmetic: 132 us -> 0.71 us  [on_device(): both = jnp.concatenate([segment, key_valid], axis=0)]
    ppermute x0 -> x51, waiting for transfers between devices: none -> 97 us  [the longest x12 51.9 us: chain_scatter(): lax.ppermute(to_right.astype(BF), 'z', [(i, i + 1) for i in range(s)])]
    convert_element_type x3 -> x25, other arithmetic: 11.6 us -> 74.6 us  [the longest x8 19.3 us: chain_scatter(): to_right.astype(BF)]
  transfers between devices with their start and end apart: 17 -> 55, of which waited for: 16 -> 10; matrix products, arithmetic and copies ran while one was open for 8% -> 32% of each run, Pallas kernels for 0% -> 35%
where the time goes in v1:
time: 1010 us; the launch traced here: 1000 us
  Pallas kernels  388 us (38%)
  starting transfers between devices  171 us (17%)
  matrix products  128 us (13%)
  other arithmetic  119 us (12%)
  waiting for transfers between devices  97 us (10%)
  local copies, waits for them, and re-layouts  93.9 us (9%)
    pallas_call x13, Pallas kernels, call(): pl.pallas_call(kernel, out_shape=outs, in_specs=[pl.BlockSpec(memory_spac...  388 us
    ppermute x12, starting transfers between devices, chain_scatter(): lax.ppermute(to_right.astype(BF), 'z', [(i, i + 1) for i in range(s)])  78 us
    ppermute x12, waiting for transfers between devices, chain_scatter(): lax.ppermute(to_right.astype(BF), 'z', [(i, i + 1) for i in range(s)])  51.9 us
    ppermute x12, waiting for transfers between devices, chain_gather(): left = lax.ppermute(left, 'z', [(i, i - 1) for i in range(1, nz - s + 1)])  42.8 us
    dot_general x5, matrix products, dot(): return jnp.dot(a, b, preferred_element_type=F32)  32.1 us
    ppermute x12, starting transfers between devices, chain_gather(): right = lax.ppermute(right, 'z', [(i, i + 1) for i in range(s - 1, nz - 1)])  31.9 us
    dot_general x4, matrix products, times_t(): lax.dot_general(left, right, (((1,), (1,)), ((), ())), preferred_element_...  29.6 us
    dot_general x4, matrix products, over_rows(): lax.dot_general(left, right, (((0,), (0,)), ((), ())), preferred_element_...  29.5 us
  transfers between devices with their start and end apart: 55, of which 10 were waited for; matrix products, arithmetic and copies ran while one was open for 32% of the time, Pallas kernels for 35%

profile of v1, /device:TPU:0, one launch (start us, length us, event | category | flops | bytes accessed | tf_op | source)
XLA Modules:
  0.0 1000.3 jit_solution(11849275406766278614)
XLA Ops:
  1.9 14.1 %shard_map.170 = bf16[512,768]{1,0:T(8,128)(2,1)} custom-call(bf16[64,6144]{1,0:T(8,128)(2,1)S(1)} %copy-done.17), custom_call_target="tpu_custom_call" | custom-call | bytes 6291456 | tf_op jit(solution)/shard_map/pallas_call | solution.py:64
  39.4 34.1 %shard_map.171 = bf16[8,192,2048]{2,1,0:T(8,128)(2,1)S(1)} custom-call(bf16[192,2048]{1,0:T(8,128)(2,1)S(1)} %bitcast.291), custom_call_target="tpu_custom_call" | custom-call | bytes 50331648 | tf_op jit(solution)/shard_map/pallas_call | solution.py:64
  83.3 16.4 %shard_map.172 = bf16[512,1024]{1,0:T(8,128)(2,1)S(1)} custom-call(bf16[64,8192]{1,0:T(8,128)(2,1)S(1)} %copy-done.15), custom_call_target="tpu_custom_call" | custom-call | bytes 8388608 | tf_op jit(solution)/shard_map/pallas_call | solution.py:64
  129.9 9.5 fusion.4
  139.5 10.3 %collective-permute-done.3 = bf16[512,768]{1,0:T(8,128)(2,1)S(1)} collective-permute-done((bf16[512,768]{1,0:T(8,128)(2,1)}, bf16[512,768]{1,0:T(8,128)(2,1)S(1)}, u32[]{:S(2)}, u32[]{:S(2)}) %collective-permute-start.3) | collective-permute-done | bytes 786464 | tf_op jit(solution)/shard_map/ppermute | solution.py:343
  153.9 16.7 %collective-permute-done.4 = bf16[512,768]{1,0:T(8,128)(2,1)S(1)} collective-permute-done((bf16[512,768]{1,0:T(8,128)(2,1)S(1)}, bf16[512,768]{1,0:T(8,128)(2,1)S(1)}, u32[]{:S(2)}, u32[]{:S(2)}) %collective-permute-start.4) | collective-permute-done | bytes 786464 | tf_op jit(solution)/shard_map/ppermute | solution.py:343
  216.5 9.2 fusion.95
  229.5 14.8 %shard_map.175 = bf16[512,1024]{1,0:T(8,128)(2,1)S(1)} custom-call(bf16[64,8192]{1,0:T(8,128)(2,1)S(1)} %copy-done.16), custom_call_target="tpu_custom_call" | custom-call | bytes 8388608 | tf_op jit(solution)/shard_map/pallas_call | solution.py:64
  251.6 8.5 collective-permute-done.10
  275.1 31.4 %shard_map.173 = f32[192,2048]{1,0:T(8,128)S(1)} custom-call(bf16[8,192,2048]{2,1,0:T(8,128)(2,1)S(1)} %bitcast.290), custom_call_target="tpu_custom_call" | custom-call | bytes 50331648 | tf_op jit(solution)/shard_map/pallas_call | solution.py:64
  310.8 30.1 %shard_map.174 = bf16[8,192,2048]{2,1,0:T(8,128)(2,1)S(1)} custom-call(bf16[192,2048]{1,0:T(8,128)(2,1)S(1)} %add_convert_fusion.1.x), custom_call_target="tpu_custom_call" | custom-call | bytes 50331648 | tf_op jit(solution)/shard_map/pallas_call | solution.py:64
  350.5 30.2 %shard_map.177 = bf16[8,192,2048]{2,1,0:T(8,128)(2,1)S(1)} custom-call(bf16[192,2048]{1,0:T(8,128)(2,1)S(1)} %bitcast.292), custom_call_target="tpu_custom_call" | custom-call | bytes 50331648 | tf_op jit(solution)/shard_map/pallas_call | solution.py:64
  384.1 8.6 fusion.96
  395.1 9.5 convolution_convert_fusion.4
  418.8 14.7 %collective-permute-done.45 = bf16[512,1024]{1,0:T(8,128)(2,1)} collective-permute-done((bf16[512,1024]{1,0:T(8,128)(2,1)}, bf16[512,1024]{1,0:T(8,128)(2,1)}, u32[]{:S(2)}, u32[]{:S(2)}) %collective-permute-start.45) | collective-permute-done | bytes 1048608 | tf_op jit(solution)/shard_map/ppermute | solution.py:367
  447.3 14.6 %collective-permute-done.46 = bf16[512,1024]{1,0:T(8,128)(2,1)S(1)} collective-permute-done((bf16[512,1024]{1,0:T(8,128)(2,1)S(1)}, bf16[512,1024]{1,0:T(8,128)(2,1)S(1)}, u32[]{:S(2)}, u32[]{:S(2)}) %collective-permute-start.46) | collective-permute-done | bytes 1048608 | tf_op jit(solution)/shard_map/ppermute | solution.py:367
  464.2 8.5 collective-permute-start.47
  478.6 11.2 %convolution_convert_fusion.3 = bf16[1536,2048]{1,0:T(8,128)(2,1)S(1)} fusion(bf16[2048,1024]{1,0:T(8,128)(2,1)S(1)} %bitcast.330, f32[1536,1024]{1,0:T(8,128)} %fusion.96), kind=kOutput, calls=%fused_computation.24 | convolution fusion | flops 6459752448 | bytes 16777216 | tf_op jit(solution)/shard_map/dot_general | solution.py:386
  489.8 13.3 %fusion.15 = bf16[1536,1024]{1,0:T(8,128)(2,1)S(1)} fusion(f32[1536,1024]{1,0:T(8,128)} %fusion.96, bf16[1536,2048]{1,0:T(8,128)(2,1)S(1)} %bitcast.327, bf16[2048,1024]{1,0:T(8,128)(2,1)} %bitcast.331), kind=kOutput, calls=%fused_computation.32 | convolution fusion | flops 6473908224 | bytes 19922944 | tf_op jit(solution)/shard_map/dot_general | solution.py:378
  503.1 8.5 convolution_convert_fusion.5
  518.9 30.9 %shard_map.178 = f32[192,2048]{1,0:T(8,128)S(1)} custom-call(bf16[8,192,2048]{2,1,0:T(8,128)(2,1)S(1)} %bitcast.299), custom_call_target="tpu_custom_call" | custom-call | bytes 50331648 | tf_op jit(solution)/shard_map/pallas_call | solution.py:64
  549.8 31.4 %shard_map.176 = f32[192,2048]{1,0:T(8,128)S(1)} custom-call(bf16[8,192,2048]{2,1,0:T(8,128)(2,1)S(1)} %bitcast.298), custom_call_target="tpu_custom_call" | custom-call | bytes 50331648 | tf_op jit(solution)/shard_map/pallas_call | solution.py:64
  584.8 30.2 %shard_map.179 = bf16[8,192,2048]{2,1,0:T(8,128)(2,1)S(1)} custom-call(bf16[192,2048]{1,0:T(8,128)(2,1)S(1)} %get-tuple-element.26.x), custom_call_target="tpu_custom_call" | custom-call | bytes 50331648 | tf_op jit(solution)/shard_map/pallas_call | solution.py:64
  639.9 10.0 multiply_convert_fusion
  670.2 8.7 convolution_convert_fusion.7
  679.0 8.4 convolution_convert_fusion
  699.0 31.4 %shard_map.180 = f32[192,2048]{1,0:T(8,128)S(1)} custom-call(bf16[8,192,2048]{2,1,0:T(8,128)(2,1)S(1)} %bitcast.297), custom_call_target="tpu_custom_call" | custom-call | bytes 50331648 | tf_op jit(solution)/shard_map/pallas_call | solution.py:64
  786.3 14.0 %collective-permute-done.40 = bf16[512,1024]{1,0:T(8,128)(2,1)} collective-permute-done((bf16[512,1024]{1,0:T(8,128)(2,1)}, bf16[512,1024]{1,0:T(8,128)(2,1)}, u32[]{:S(2)}, u32[]{:S(2)}) %collective-permute-start.40) | collective-permute-done | bytes 1048608 | tf_op jit(solution)/shard_map/ppermute | solution.py:367
  816.4 11.2 %all-to-all-start.3 = ((f32[32,1,1536]{2,1,0:T(1,128)}), f32[32,1,1536]{2,1,0:T(1,128)S(1)}, u32[]{:S(2)}, u32[]{:S(2)}) async-start(f32[32,1,1536]{2,1,0:T(1,128)} %reshape.621), calls=%async_computation.3 | async-start | bytes 393216 | tf_op jit(solution)/shard_map/all_to_all | solution.py:554
  827.6 27.8 %collective-permute-start.34 = (bf16[64,2048]{1,0:T(8,128)(2,1)S(1)}, bf16[64,2048]{1,0:T(8,128)(2,1)S(1)}, u32[]{:S(2)}, u32[]{:S(2)}) collective-permute-start(bf16[64,2048]{1,0:T(8,128)(2,1)S(1)} %get-tuple-element.49), channel_id=1, source_target_pairs={{0,8},{8,16},{16,24},{1,9},{9,17},{17,25},{2,10},{10,18},{18,26},{... | collective-permute-start | bytes 786440 | tf_op jit(solution)/shard_map/ppermute | solution.py:367
  898.2 67.1 %shard_map.181 = bf16[64,6144]{1,0:T(8,128)(2,1)S(1)} custom-call(bf16[512,768]{1,0:T(8,128)(2,1)S(1)} %fusion.49.refs_0_), custom_call_target="tpu_custom_call" | custom-call | bytes 6291456 | tf_op jit(solution)/shard_map/pallas_call | solution.py:64
  969.1 26.3 %shard_map.182 = (bf16[64,8192]{1,0:T(8,128)(2,1)S(1)}, bf16[64,8192]{1,0:T(8,128)(2,1)S(1)}) custom-call(bf16[512,1024]{1,0:T(8,128)(2,1)S(1)} %fusion.36.refs_0_, bf16[512,1024]{1,0:T(8,128)(2,1)S(1)} %fusion.30.refs_1_), custom_call_target="tpu_custom_call" | custom-call | bytes 16777216 | tf_op jit(solution)/shard_map/pallas_call | solution.py:64
  (411 shorter events, 386.1 us)
Async XLA Ops:
  16.1 111.7 %collective-permute-start.2 = (bf16[512,768]{1,0:T(8,128)(2,1)}, bf16[512,768]{1,0:T(8,128)(2,1)}, u32[]{:S(2)}, u32[]{:S(2)}) collective-permute-start(bf16[512,768]{1,0:T(8,128)(2,1)} %shard_map.170), channel_id=1, source_target_pairs={{8,0},{16,8},{24,16},{9,1},{17,9},{25,17},{10,2},{18,10},{26,18},{... | collective-permute-start | bytes 2359304 | tf_op jit(solution)/shard_map/ppermute | solution.py:343
  17.4 111.9 %collective-permute-start.1 = (bf16[512,768]{1,0:T(8,128)(2,1)}, bf16[512,768]{1,0:T(8,128)(2,1)}, u32[]{:S(2)}, u32[]{:S(2)}) collective-permute-start(bf16[512,768]{1,0:T(8,128)(2,1)} %shard_map.170), channel_id=1, source_target_pairs={{0,8},{8,16},{16,24},{1,9},{9,17},{17,25},{2,10},{10,18},{18,26},{... | collective-permute-start | bytes 2359304 | tf_op jit(solution)/shard_map/ppermute | solution.py:342
  23.5 76.3 %collective-permute-start = (s32[2,768]{1,0:T(2,128)S(1)}, s32[2,768]{1,0:T(2,128)S(1)}, u32[]{:S(2)}, u32[]{:S(2)}) collective-permute-start(s32[2,768]{1,0:T(2,128)S(1)} %pad_add_fusion.2), channel_id=1, source_target_pairs={{0,4},{4,0},{1,5},{5,1},{2,6},{6,2},{3,7},{7,3},{8,12},{12,8},{9,1... | collective-permute-start | bytes 18440 | tf_op jit(solution)/shard_map/ppermute | solution.py:428
  25.1 128.9 %collective-permute-start.7 = (bf16[64,2048]{1,0:T(8,128)(2,1)}, bf16[64,2048]{1,0:T(8,128)(2,1)}, u32[]{:S(2)}, u32[]{:S(2)}) collective-permute-start(bf16[64,2048]{1,0:T(8,128)(2,1)} %param.15), channel_id=1, source_target_pairs={{0,0},{1,8},{2,16},{3,24},{4,1},{5,9},{6,17},{7,25},{8,2},{9,10},{... | collective-permute-start | bytes 786440 | tf_op jit(solution)/shard_map/ppermute | solution.py:466
  34.5 72.0 %all-to-all-start = ((f32[32,6,384]{2,1,0:T(8,128)}), f32[32,6,384]{2,1,0:T(8,128)}, u32[]{:S(2)}, u32[]{:S(2)}) async-start(f32[32,6,384]{2,1,0:T(8,128)} %bitcast.3), calls=%async_computation | async-start | bytes 786432 | tf_op jit(solution)/shard_map/all_to_all | solution.py:421
  170.6 77.8 %collective-permute-start.9 = (bf16[64,2048]{1,0:T(8,128)(2,1)}, bf16[64,2048]{1,0:T(8,128)(2,1)}, u32[]{:S(2)}, u32[]{:S(2)}) collective-permute-start(bf16[64,2048]{1,0:T(8,128)(2,1)} %collective-permute-done.7), channel_id=1, source_target_pairs={{8,0},{16,8},{24,16},{9,1},{17,9},{25,17},{10,2},{18,10},{26,18},{... | collective-permute-start | bytes 786440 | tf_op jit(solution)/shard_map/ppermute | solution.py:343
  171.9 78.9 %collective-permute-start.8 = (bf16[64,2048]{1,0:T(8,128)(2,1)}, bf16[64,2048]{1,0:T(8,128)(2,1)}, u32[]{:S(2)}, u32[]{:S(2)}) collective-permute-start(bf16[64,2048]{1,0:T(8,128)(2,1)} %collective-permute-done.7), channel_id=1, source_target_pairs={{0,8},{8,16},{16,24},{1,9},{9,17},{17,25},{2,10},{10,18},{18,26},{... | collective-permute-start | bytes 786440 | tf_op jit(solution)/shard_map/ppermute | solution.py:342
  177.1 92.9 %collective-permute-start.15 = (bf16[512,1024]{1,0:T(8,128)(2,1)S(1)}, bf16[512,1024]{1,0:T(8,128)(2,1)}, u32[]{:S(2)}, u32[]{:S(2)}) collective-permute-start(bf16[512,1024]{1,0:T(8,128)(2,1)S(1)} %shard_map.172), channel_id=1, source_target_pairs={{8,0},{16,8},{24,16},{9,1},{17,9},{25,17},{10,2},{18,10},{26,18},{... | collective-permute-start | bytes 3145736 | tf_op jit(solution)/shard_map/ppermute | solution.py:343
  178.4 93.0 %collective-permute-start.14 = (bf16[512,1024]{1,0:T(8,128)(2,1)S(1)}, bf16[512,1024]{1,0:T(8,128)(2,1)}, u32[]{:S(2)}, u32[]{:S(2)}) collective-permute-start(bf16[512,1024]{1,0:T(8,128)(2,1)S(1)} %shard_map.172), channel_id=1, source_target_pairs={{0,8},{8,16},{16,24},{1,9},{9,17},{17,25},{2,10},{10,18},{18,26},{... | collective-permute-start | bytes 3145736 | tf_op jit(solution)/shard_map/ppermute | solution.py:342
  270.1 36.4 %collective-permute-start.16 = (bf16[512,1024]{1,0:T(8,128)(2,1)}, bf16[512,1024]{1,0:T(8,128)(2,1)S(1)}, u32[]{:S(2)}, u32[]{:S(2)}) collective-permute-start(bf16[512,1024]{1,0:T(8,128)(2,1)} %collective-permute-done.15), channel_id=1, source_target_pairs={{8,0},{16,8},{9,1},{17,9},{10,2},{18,10},{11,3},{19,11},{12,4},{20... | collective-permute-start | bytes 3145736 | tf_op jit(solution)/shard_map/ppermute | solution.py:343
  271.4 36.4 %collective-permute-start.18 = (bf16[512,1024]{1,0:T(8,128)(2,1)}, bf16[512,1024]{1,0:T(8,128)(2,1)S(1)}, u32[]{:S(2)}, u32[]{:S(2)}) collective-permute-start(bf16[512,1024]{1,0:T(8,128)(2,1)} %collective-permute-done.14), channel_id=1, source_target_pairs={{8,16},{16,24},{9,17},{17,25},{10,18},{18,26},{11,19},{19,27},{12,... | collective-permute-start | bytes 3145736 | tf_op jit(solution)/shard_map/ppermute | solution.py:342
  306.6 34.4 %collective-permute-start.17 = (bf16[512,1024]{1,0:T(8,128)(2,1)S(1)}, bf16[512,1024]{1,0:T(8,128)(2,1)S(1)}, u32[]{:S(2)}, u32[]{:S(2)}) collective-permute-start(bf16[512,1024]{1,0:T(8,128)(2,1)S(1)} %collective-permute-done.16), channel_id=1, source_target_pairs={{8,0},{9,1},{10,2},{11,3},{12,4},{13,5},{14,6},{15,7}} | collective-permute-start | bytes 3145736 | tf_op jit(solution)/shard_map/ppermute | solution.py:343
  307.9 33.1 %collective-permute-start.19 = (bf16[512,1024]{1,0:T(8,128)(2,1)S(1)}, bf16[512,1024]{1,0:T(8,128)(2,1)S(1)}, u32[]{:S(2)}, u32[]{:S(2)}) collective-permute-start(bf16[512,1024]{1,0:T(8,128)(2,1)S(1)} %collective-permute-done.18), channel_id=1, source_target_pairs={{16,24},{17,25},{18,26},{19,27},{20,28},{21,29},{22,30},{23,31}} | collective-permute-start | bytes 3145736 | tf_op jit(solution)/shard_map/ppermute | solution.py:342
  341.0 70.2 %collective-permute-start.21 = (bf16[512,1024]{1,0:T(8,128)(2,1)S(1)}, bf16[512,1024]{1,0:T(8,128)(2,1)}, u32[]{:S(2)}, u32[]{:S(2)}) collective-permute-start(bf16[512,1024]{1,0:T(8,128)(2,1)S(1)} %copy-done.14), channel_id=1, source_target_pairs={{8,0},{16,8},{24,16},{9,1},{17,9},{25,17},{10,2},{18,10},{26,18},{... | collective-permute-start | bytes 3145736 | tf_op jit(solution)/shard_map/ppermute | solution.py:343
  342.3 75.3 %collective-permute-start.20 = (bf16[512,1024]{1,0:T(8,128)(2,1)S(1)}, bf16[512,1024]{1,0:T(8,128)(2,1)}, u32[]{:S(2)}, u32[]{:S(2)}) collective-permute-start(bf16[512,1024]{1,0:T(8,128)(2,1)S(1)} %copy-done.14), channel_id=1, source_target_pairs={{0,8},{8,16},{16,24},{1,9},{9,17},{17,25},{2,10},{10,18},{18,26},{... | collective-permute-start | bytes 3145736 | tf_op jit(solution)/shard_map/ppermute | solution.py:342
  416.9 30.4 %collective-permute-start.48 = (bf16[512,1024]{1,0:T(8,128)(2,1)S(1)}, bf16[512,1024]{1,0:T(8,128)(2,1)S(1)}, u32[]{:S(2)}, u32[]{:S(2)}) collective-permute-start(bf16[512,1024]{1,0:T(8,128)(2,1)S(1)} %copy-done.43), channel_id=1, source_target_pairs={{24,16},{25,17},{26,18},{27,19},{28,20},{29,21},{30,22},{31,23}} | collective-permute-start | bytes 3145736 | tf_op jit(solution)/shard_map/ppermute | solution.py:368
  439.9 32.8 %collective-permute-start.23 = (bf16[512,1024]{1,0:T(8,128)(2,1)}, bf16[512,1024]{1,0:T(8,128)(2,1)S(1)}, u32[]{:S(2)}, u32[]{:S(2)}) collective-permute-start(bf16[512,1024]{1,0:T(8,128)(2,1)} %collective-permute-done.22), channel_id=1, source_target_pairs={{8,0},{9,1},{10,2},{11,3},{12,4},{13,5},{14,6},{15,7}} | collective-permute-start | bytes 3145736 | tf_op jit(solution)/shard_map/ppermute | solution.py:343
  464.2 404.9 %collective-permute-start.47 = (bf16[512,1024]{1,0:T(8,128)(2,1)}, bf16[512,1024]{1,0:T(8,128)(2,1)}, u32[]{:S(2)}, u32[]{:S(2)}) collective-permute-start(bf16[512,1024]{1,0:T(8,128)(2,1)} %get-tuple-element.30), channel_id=1, source_target_pairs={{0,8},{8,16},{16,24},{1,9},{9,17},{17,25},{2,10},{10,18},{18,26},{... | collective-permute-start | bytes 3145736 | tf_op jit(solution)/shard_map/ppermute | solution.py:367
  688.9 66.2 %collective-permute-start.39 = (bf16[512,1024]{1,0:T(8,128)(2,1)}, bf16[512,1024]{1,0:T(8,128)(2,1)}, u32[]{:S(2)}, u32[]{:S(2)}) collective-permute-start(bf16[512,1024]{1,0:T(8,128)(2,1)} %get-tuple-element.36), channel_id=1, source_target_pairs={{0,8},{1,9},{2,10},{3,11},{4,12},{5,13},{6,14},{7,15}} | collective-permute-start | bytes 3145736 | tf_op jit(solution)/shard_map/ppermute | solution.py:367
  694.7 87.2 %collective-permute-start.42 = (bf16[512,1024]{1,0:T(8,128)(2,1)}, bf16[512,1024]{1,0:T(8,128)(2,1)}, u32[]{:S(2)}, u32[]{:S(2)}) collective-permute-start(bf16[512,1024]{1,0:T(8,128)(2,1)} %get-tuple-element.37), channel_id=1, source_target_pairs={{24,16},{25,17},{26,18},{27,19},{28,20},{29,21},{30,22},{31,23}} | collective-permute-start | bytes 3145736 | tf_op jit(solution)/shard_map/ppermute | solution.py:368
  697.0 66.3 %collective-permute-start.32 = (bf16[64,2048]{1,0:T(8,128)(2,1)}, bf16[64,2048]{1,0:T(8,128)(2,1)}, u32[]{:S(2)}, u32[]{:S(2)}) collective-permute-start(bf16[64,2048]{1,0:T(8,128)(2,1)} %get-tuple-element.51), channel_id=1, source_target_pairs={{0,8},{1,9},{2,10},{3,11},{4,12},{5,13},{6,14},{7,15}} | collective-permute-start | bytes 786440 | tf_op jit(solution)/shard_map/ppermute | solution.py:367
  763.3 36.9 %collective-permute-start.40 = (bf16[512,1024]{1,0:T(8,128)(2,1)}, bf16[512,1024]{1,0:T(8,128)(2,1)}, u32[]{:S(2)}, u32[]{:S(2)}) collective-permute-start(bf16[512,1024]{1,0:T(8,128)(2,1)} %fusion.33), channel_id=1, source_target_pairs={{0,8},{8,16},{1,9},{9,17},{2,10},{10,18},{3,11},{11,19},{4,12},{12... | collective-permute-start | bytes 3145736 | tf_op jit(solution)/shard_map/ppermute | solution.py:367
  770.9 42.6 %all-to-all-start.2 = ((f32[32,1,1536]{2,1,0:T(1,128)}), f32[32,1,1536]{2,1,0:T(1,128)S(1)}, u32[]{:S(2)}, u32[]{:S(2)}) async-start(f32[32,1,1536]{2,1,0:T(1,128)} %reshape.619), calls=%async_computation.2 | async-start | bytes 393216 | tf_op jit(solution)/shard_map/all_to_all | solution.py:552
  773.5 36.1 %collective-permute-start.49 = (bf16[512,1024]{1,0:T(8,128)(2,1)}, bf16[512,1024]{1,0:T(8,128)(2,1)S(1)}, u32[]{:S(2)}, u32[]{:S(2)}) collective-permute-start(bf16[512,1024]{1,0:T(8,128)(2,1)} %get-tuple-element.31), channel_id=1, source_target_pairs={{16,8},{24,16},{17,9},{25,17},{18,10},{26,18},{19,11},{27,19},{20,... | collective-permute-start | bytes 3145736 | tf_op jit(solution)/shard_map/ppermute | solution.py:368
  800.3 56.2 %collective-permute-start.30 = (bf16[512,768]{1,0:T(8,128)(2,1)}, bf16[512,768]{1,0:T(8,128)(2,1)}, u32[]{:S(2)}, u32[]{:S(2)}) collective-permute-start(bf16[512,768]{1,0:T(8,128)(2,1)} %get-tuple-element.39), channel_id=1, source_target_pairs={{16,8},{24,16},{17,9},{25,17},{18,10},{26,18},{19,11},{27,19},{20,... | collective-permute-start | bytes 2359304 | tf_op jit(solution)/shard_map/ppermute | solution.py:368
  805.7 54.5 %collective-permute-start.43 = (bf16[512,1024]{1,0:T(8,128)(2,1)}, bf16[512,1024]{1,0:T(8,128)(2,1)}, u32[]{:S(2)}, u32[]{:S(2)}) collective-permute-start(bf16[512,1024]{1,0:T(8,128)(2,1)} %get-tuple-element.35), channel_id=1, source_target_pairs={{16,8},{24,16},{17,9},{25,17},{18,10},{26,18},{19,11},{27,19},{20,... | collective-permute-start | bytes 3145736 | tf_op jit(solution)/shard_map/ppermute | solution.py:368
  812.2 64.5 %collective-permute-start.50 = (bf16[512,1024]{1,0:T(8,128)(2,1)}, bf16[512,1024]{1,0:T(8,128)(2,1)}, u32[]{:S(2)}, u32[]{:S(2)}) collective-permute-start(bf16[512,1024]{1,0:T(8,128)(2,1)} %fusion.26), channel_id=1, source_target_pairs={{8,0},{16,8},{24,16},{9,1},{17,9},{25,17},{10,2},{18,10},{26,18},{... | collective-permute-start | bytes 3145736 | tf_op jit(solution)/shard_map/ppermute | solution.py:368
  816.4 68.9 %all-to-all-start.3 = ((f32[32,1,1536]{2,1,0:T(1,128)}), f32[32,1,1536]{2,1,0:T(1,128)S(1)}, u32[]{:S(2)}, u32[]{:S(2)}) async-start(f32[32,1,1536]{2,1,0:T(1,128)} %reshape.621), calls=%async_computation.3 | async-start | bytes 393216 | tf_op jit(solution)/shard_map/all_to_all | solution.py:554
  827.6 45.6 %collective-permute-start.34 = (bf16[64,2048]{1,0:T(8,128)(2,1)S(1)}, bf16[64,2048]{1,0:T(8,128)(2,1)S(1)}, u32[]{:S(2)}, u32[]{:S(2)}) collective-permute-start(bf16[64,2048]{1,0:T(8,128)(2,1)S(1)} %get-tuple-element.49), channel_id=1, source_target_pairs={{0,8},{8,16},{16,24},{1,9},{9,17},{17,25},{2,10},{10,18},{18,26},{... | collective-permute-start | bytes 786440 | tf_op jit(solution)/shard_map/ppermute | solution.py:367
  860.2 33.8 %collective-permute-start.28 = (bf16[512,768]{1,0:T(8,128)(2,1)}, bf16[512,768]{1,0:T(8,128)(2,1)}, u32[]{:S(2)}, u32[]{:S(2)}) collective-permute-start(bf16[512,768]{1,0:T(8,128)(2,1)} %get-tuple-element.38), channel_id=1, source_target_pairs={{0,8},{8,16},{16,24},{1,9},{9,17},{17,25},{2,10},{10,18},{18,26},{... | collective-permute-start | bytes 2359304 | tf_op jit(solution)/shard_map/ppermute | solution.py:367
  869.1 97.5 %collective-permute-start.41 = (bf16[512,1024]{1,0:T(8,128)(2,1)}, bf16[512,1024]{1,0:T(8,128)(2,1)}, u32[]{:S(2)}, u32[]{:S(2)}) collective-permute-start(bf16[512,1024]{1,0:T(8,128)(2,1)} %get-tuple-element.34), channel_id=1, source_target_pairs={{0,8},{8,16},{16,24},{1,9},{9,17},{17,25},{2,10},{10,18},{18,26},{... | collective-permute-start | bytes 3145736 | tf_op jit(solution)/shard_map/ppermute | solution.py:367
  874.5 92.1 %collective-permute-start.44 = (bf16[512,1024]{1,0:T(8,128)(2,1)}, bf16[512,1024]{1,0:T(8,128)(2,1)}, u32[]{:S(2)}, u32[]{:S(2)}) collective-permute-start(bf16[512,1024]{1,0:T(8,128)(2,1)} %fusion.32), channel_id=1, source_target_pairs={{8,0},{16,8},{24,16},{9,1},{17,9},{25,17},{10,2},{18,10},{26,18},{... | collective-permute-start | bytes 3145736 | tf_op jit(solution)/shard_map/ppermute | solution.py:368
  (98 other events, 1805.2 us)

commit v2 on v1

v2 whole, which is shorter than its diff:
```python
import functools
import math

import jax
import jax.numpy as jnp
from jax import lax
from jax.experimental import pallas as pl
from jax.experimental.pallas import tpu as pltpu
from jax.sharding import Mesh
from jax.sharding import PartitionSpec as P

HEADS = 16
HEAD_DIM = 128
EPS = 1e-06
NEG = -1e30
HIGH = lax.Precision.HIGHEST
PLANE = 8
BF = jnp.bfloat16
F32 = jnp.float32
ALL = ("z", "y", "blk")
MIB = 1 << 20


def peer(k):
    y, b = lax.axis_index("y"), lax.axis_index("blk")
    high, low = lax.div(b, 2), lax.rem(b, 2)
    if k & 4:
        y = 1 - y
    if k & 2:
        high = 1 - high
    if k & 1:
        low = 1 - low
    return {"y": y, "blk": high * 2 + low}


def place(k):
    where = peer(k)
    return where["y"] * 4 + where["blk"]


def greet(peers):
    barrier = pltpu.get_barrier_semaphore()
    for k in peers:
        pl.semaphore_signal(
            barrier, inc=1, device_id=peer(k), device_id_type=pl.DeviceIdType.MESH
        )
    pl.semaphore_wait(barrier, len(peers))


def send(src, dst, ssem, rsem, k):
    copy = pltpu.make_async_remote_copy(
        src_ref=src,
        dst_ref=dst,
        send_sem=ssem,
        recv_sem=rsem,
        device_id=peer(k),
        device_id_type=pl.DeviceIdType.MESH,
    )
    copy.start()
    return copy


def call(kernel, ins, outs, scratch, ident, vmem=16, micros=10):
    return pl.pallas_call(
        kernel,
        out_shape=outs,
        in_specs=[pl.BlockSpec(memory_space=pl.ANY)] * len(ins),
        out_specs=jax.tree.map(lambda _: pl.BlockSpec(memory_space=pl.ANY), outs),
        scratch_shapes=scratch,
        compiler_params=pltpu.CompilerParams(
            collective_id=ident, has_side_effects=True, vmem_limit_bytes=vmem * MIB
        ),
        cost_estimate=pl.CostEstimate(
            flops=0, bytes_accessed=int(micros * 3.6e6), transcendentals=0
        ),
    )(*ins)


def gather_kernel(x, o, xv, lsem, ssem, rsem):
    rows = x.shape[0]
    half = rows // 2
    top, bot = pl.ds(0, half), pl.ds(half, half)
    load = pltpu.make_async_copy(x, xv, lsem.at[0])
    load.start()
    greet((1, 2, 4))
    load.wait()
    go = lambda i, src, dst, k: send(src, dst, ssem.at[i], rsem.at[i], k)
    x_bot = go(0, xv.at[bot], o.at[2, bot], 2)
    y_top = go(1, xv.at[top], o.at[4, top], 4)
    x_top = go(2, xv.at[top], o.at[2, top], 2)
    y_bot = go(3, xv.at[bot], o.at[4, bot], 4)
    sib = go(4, xv, o.at[1], 1)
    own = pltpu.make_async_copy(xv, o.at[0], lsem.at[1])
    own.start()
    x_bot.wait_recv()
    dy = go(5, o.at[2, bot], o.at[6, bot], 4)
    c0 = go(6, o.at[2, bot], o.at[3, bot], 1)
    y_top.wait_recv()
    dx = go(7, o.at[4, top], o.at[6, top], 2)
    c1 = go(8, o.at[4, top], o.at[5, top], 1)
    x_top.wait_recv()
    c2 = go(9, o.at[2, top], o.at[3, top], 1)
    y_bot.wait_recv()
    c3 = go(10, o.at[4, bot], o.at[5, bot], 1)
    dx.wait_recv()
    c4 = go(11, o.at[6, top], o.at[7, top], 1)
    dy.wait_recv()
    c5 = go(12, o.at[6, bot], o.at[7, bot], 1)
    for copy in (sib, c0, c1, c2, c3, c4, c5):
        copy.wait_recv()
    for copy in (x_bot, y_top, x_top, y_bot, sib, dy, c0, dx, c1, c2, c3, c4, c5):
        copy.wait_send()
    own.wait()


def plane_gather(x, ident):
    out = jax.ShapeDtypeStruct((PLANE,) + x.shape, x.dtype)
    dma = pltpu.SemaphoreType.DMA
    scratch = [pltpu.VMEM(x.shape, x.dtype), dma((2,)), dma((13,)), dma((13,))]
    return call(gather_kernel, (x,), out, scratch, ident, 8, 30)


def rows_loop(rows, body):
    step = 16

    def one(i, carry):
        body(pl.ds(pl.multiple_of(i * step, step), step))
        return carry

    lax.fori_loop(0, rows // step, one, 0)


def scatter_kernel(p, o, pv, rc, q6, q2, q4, d6, rx, ry, ov, lsem, ssem, rsem):
    rows = o.shape[0]
    half = rows // 2
    top, bot = pl.ds(0, half), pl.ds(half, half)
    greet((1, 2, 4))
    go = lambda i, src, dst, k: send(src, dst, ssem.at[i], rsem.at[i], k)
    load = [pltpu.make_async_copy(p.at[2 * i], pv.at[i], lsem.at[i]) for i in range(4)]
    c7t = go(0, p.at[7, top], rc.at[3, top], 1)
    load[3].start()
    c7b = go(1, p.at[7, bot], rc.at[3, bot], 1)
    load[1].start()
    c3 = go(2, p.at[3], rc.at[1], 1)
    load[2].start()
    c5 = go(3, p.at[5], rc.at[2], 1)
    load[0].start()
    c1 = go(4, p.at[1], rc.at[0], 1)

    def add2(dst, i, start):
        def body(r):
            s = pl.ds(pl.multiple_of(start + r.start, 16), r.size)
            dst[r, :] = (pv[i, s, :].astype(F32) + rc[i, s, :].astype(F32)).astype(BF)

        rows_loop(half, body)

    def add3(dst, i, start, more):
        def body(r):
            s = pl.ds(pl.multiple_of(start + r.start, 16), r.size)
            total = pv[i, s, :].astype(F32) + rc[i, s, :].astype(F32) + more[r, :].astype(F32)
            dst[r, :] = total.astype(BF)

        rows_loop(half, body)

    load[3].wait()
    c7t.wait_recv()
    add2(q6.at[0], 3, 0)
    s6t = go(5, q6.at[0], d6.at[0], 2)
    c7b.wait_recv()
    add2(q6.at[1], 3, half)
    s6b = go(6, q6.at[1], d6.at[1], 4)
    load[1].wait()
    c3.wait_recv()
    add2(q2.at[0], 1, 0)
    s2t = go(7, q2.at[0], rx.at[0], 2)
    load[2].wait()
    c5.wait_recv()
    add2(q4.at[1], 2, half)
    s4b = go(8, q4.at[1], ry.at[1], 4)
    s6t.wait_recv()
    add3(q4.at[0], 2, 0, d6.at[0])
    s4t = go(9, q4.at[0], ry.at[0], 4)
    s6b.wait_recv()
    add3(q2.at[1], 1, half, d6.at[1])
    s2b = go(10, q2.at[1], rx.at[1], 2)
    load[0].wait()
    c1.wait_recv()
    s2t.wait_recv()
    s4t.wait_recv()

    def finish(n, start):
        def body(r):
            s = pl.ds(pl.multiple_of(start + r.start, 16), r.size)
            total = pv[0, s, :].astype(F32) + rc[0, s, :].astype(F32)
            ov[s, :] = total + rx[n, r, :].astype(F32) + ry[n, r, :].astype(F32)

        rows_loop(half, body)

    finish(0, 0)
    out0 = pltpu.make_async_copy(ov.at[top], o.at[top], lsem.at[4])
    out0.start()
    s2b.wait_recv()
    s4b.wait_recv()
    finish(1, half)
    out1 = pltpu.make_async_copy(ov.at[bot], o.at[bot], lsem.at[5])
    out1.start()
    for copy in (c7t, c7b, c3, c5, c1, s6t, s6b, s2t, s4b, s4t, s2b):
        copy.wait_send()
    out0.wait()
    out1.wait()


def plane_scatter(p, ident):
    _, rows, width = p.shape
    half = rows // 2
    dma = pltpu.SemaphoreType.DMA
    pair = pltpu.VMEM((2, half, width), BF)
    scratch = [
        pltpu.VMEM((4, rows, width), BF),
        pltpu.VMEM((4, rows, width), BF),
        pair,
        pair,
        pair,
        pair,
        pair,
        pair,
        pltpu.VMEM((rows, width), F32),
        dma((6,)),
        dma((11,)),
        dma((11,)),
    ]
    out = jax.ShapeDtypeStruct((rows, width), F32)
    return call(scatter_kernel, (p,), out, scratch, ident, 24, 31)


def cut(weights, blocks):
    plan = []
    for i, cols in enumerate(weights):
        each = cols // blocks
        for b in range(blocks):
            plan.append((i, b * each, each // PLANE, b * (each // PLANE)))
    return plan


def spread_kernel(plan, count, *refs):
    ins, outs, held = refs[:count], refs[count : 2 * count], refs[2 * count : 3 * count]
    lsem, ssem, rsem = refs[3 * count :]
    loads = [pltpu.make_async_copy(a, v, lsem.at[i]) for i, (a, v) in enumerate(zip(ins, held))]
    for copy in loads:
        copy.start()
    greet(range(1, PLANE))
    mine = place(0)
    remotes = []
    for w, load in enumerate(loads):
        load.wait()
        rows = ins[w].shape[0]
        here = pl.ds(pl.multiple_of(mine * rows, 16), rows)
        for n, (i, base, width, col) in enumerate(plan):
            if i != w:
                continue
            for k in (6, 7, 2, 3, 4, 5, 1):
                cols = pl.ds(pl.multiple_of(base + place(k) * width, 128), width)
                remotes.append(
                    send(
                        held[w].at[:, cols],
                        outs[w].at[here, pl.ds(col, width)],
                        ssem.at[n, k],
                        rsem.at[n, k],
                        k,
                    )
                )
            cols = pl.ds(pl.multiple_of(base + mine * width, 128), width)
            copy = pltpu.make_async_copy(
                held[w].at[:, cols], outs[w].at[here, pl.ds(col, width)], ssem.at[n, 0]
            )
            copy.start()
            remotes.append(copy)
    for copy in remotes:
        copy.wait()


def spread(weights, ident, blocks=1):
    plan = cut([w.shape[1] for w in weights], blocks)
    outs = [
        jax.ShapeDtypeStruct((w.shape[0] * PLANE, w.shape[1] // PLANE), w.dtype) for w in weights
    ]
    dma = pltpu.SemaphoreType.DMA
    n = len(plan)
    scratch = [pltpu.VMEM(w.shape, w.dtype) for w in weights]
    return call(
        functools.partial(spread_kernel, plan, len(weights)),
        tuple(weights),
        outs,
        scratch + [dma((len(weights),)), dma((n, PLANE)), dma((n, PLANE))],
        ident,
        8,
        sum(w.size for w in weights) / 3e4,
    )


def collect_kernel(plan, count, *refs):
    ins, outs, held = refs[:count], refs[count : 2 * count], refs[2 * count : 3 * count]
    lsem, ssem, rsem = refs[3 * count :]
    loads = [pltpu.make_async_copy(a, v, lsem.at[i]) for i, (a, v) in enumerate(zip(ins, held))]
    for copy in loads:
        copy.start()
    greet(range(1, PLANE))
    mine = place(0)
    remotes = []
    for w, load in enumerate(loads):
        load.wait()
        rows = outs[w].shape[0]
        for n, (i, base, width, col) in enumerate(plan):
            if i != w:
                continue
            cols = pl.ds(pl.multiple_of(base + mine * width, 128), width)
            for k in (6, 7, 2, 3, 4, 5, 1):
                there = pl.ds(pl.multiple_of(place(k) * rows, 16), rows)
                remotes.append(
                    send(
                        held[w].at[there, pl.ds(col, width)],
                        outs[w].at[:, cols],
                        ssem.at[n, k],
                        rsem.at[n, k],
                        k,
                    )
                )
            here = pl.ds(pl.multiple_of(mine * rows, 16), rows)
            copy = pltpu.make_async_copy(
                held[w].at[here, pl.ds(col, width)], outs[w].at[:, cols], ssem.at[n, 0]
            )
            copy.start()
            remotes.append(copy)
    for copy in remotes:
        copy.wait()


def collect(grads, ident, blocks=1):
    plan = cut([g.shape[1] * PLANE for g in grads], blocks)
    outs = [
        jax.ShapeDtypeStruct((g.shape[0] // PLANE, g.shape[1] * PLANE), g.dtype) for g in grads
    ]
    dma = pltpu.SemaphoreType.DMA
    n = len(plan)
    scratch = [pltpu.VMEM(g.shape, g.dtype) for g in grads]
    return call(
        functools.partial(collect_kernel, plan, len(grads)),
        tuple(grads),
        outs,
        scratch + [dma((len(grads),)), dma((n, PLANE)), dma((n, PLANE))],
        ident,
        8,
        sum(g.size for g in grads) / 3e4,
    )


def flat_place():
    return lax.axis_index("z") * PLANE + lax.axis_index("y") * 4 + lax.axis_index("blk")


def flat_id(d):
    return {"z": lax.div(d, PLANE), "y": lax.rem(lax.div(d, 4), 2), "blk": lax.rem(d, 4)}


def greet_all(count):
    barrier = pltpu.get_barrier_semaphore()
    me = flat_place()

    def one(i, carry):
        pl.semaphore_signal(
            barrier,
            inc=1,
            device_id=flat_id(lax.rem(me + i, count)),
            device_id_type=pl.DeviceIdType.MESH,
        )
        return carry

    lax.fori_loop(1, count, one, 0)
    pl.semaphore_wait(barrier, count - 1)


def to_all(count, source, target, ssem, rsem):
    me = flat_place()

    def copy(i):
        d = lax.rem(me + i, count)
        return pltpu.make_async_remote_copy(
            src_ref=source(d),
            dst_ref=target.at[me],
            send_sem=ssem.at[i],
            recv_sem=rsem.at[i],
            device_id=flat_id(d),
            device_id_type=pl.DeviceIdType.MESH,
        )

    def begin(i, carry):
        copy(i).start()
        return carry

    def finish(i, carry):
        copy(i).wait()
        return carry

    lax.fori_loop(1, count, begin, 0)
    target[me] = source(me)[...]
    lax.fori_loop(1, count, finish, 0)


def exchange_kernel(count, x, o, ssem, rsem):
    greet_all(count)
    to_all(count, lambda d: x.at[d], o, ssem, rsem)


def small_call(kernel, ins, outs, scratch, ident, micros):
    vmem = pl.BlockSpec(memory_space=pltpu.VMEM)
    return pl.pallas_call(
        kernel,
        out_shape=outs,
        in_specs=[vmem] * len(ins),
        out_specs=jax.tree.map(lambda _: vmem, outs),
        scratch_shapes=scratch,
        compiler_params=pltpu.CompilerParams(
            collective_id=ident, has_side_effects=True, vmem_limit_bytes=32 * MIB
        ),
        cost_estimate=pl.CostEstimate(
            flops=0, bytes_accessed=int(micros * 3.6e6), transcendentals=0
        ),
    )(*ins)


def exchange(x, ident):
    dma = pltpu.SemaphoreType.DMA((x.shape[0],))
    return small_call(
        functools.partial(exchange_kernel, x.shape[0]),
        (x,),
        jax.ShapeDtypeStruct(x.shape, x.dtype),
        [dma, dma],
        ident,
        8,
    )


def mods_back_kernel(count, x, w, o, t, got, part, mine, s0, r0, s1, r1, s2, r2):
    greet_all(count)
    to_all(count, lambda d: x.at[d], got, s0, r0)
    groups = o.shape[0]
    for g in range(groups):
        o[g] = got[4 * g] + got[4 * g + 1] + got[4 * g + 2] + got[4 * g + 3]
    own = o[...].reshape(groups * 8, o.shape[2])
    high = own.astype(BF)
    rest = own - high.astype(F32)
    low = rest.astype(BF)
    quarter = w.shape[0] // 4
    for q in range(4):
        piece = w[q * quarter : (q + 1) * quarter, :]
        product = times_t(high, piece) + times_t(low, piece)
        for g in range(groups):
            part[4 * g + q] = product[8 * g : 8 * g + 8]
    to_all(count, lambda d: part.at[d], mine, s1, r1)

    def add(i, total):
        return total + mine[i]

    part[flat_place()] = lax.fori_loop(0, count, add, jnp.zeros(mine.shape[1:], F32))
    to_all(count, lambda d: part.at[flat_place()], t, s2, r2)


def mods_back(x, w, ident):
    count, eight, cols = x.shape
    width = w.shape[0]
    dma = pltpu.SemaphoreType.DMA((count,))
    pieces = jax.ShapeDtypeStruct((count, eight, width // 4), F32)
    return small_call(
        functools.partial(mods_back_kernel, count),
        (x, w),
        (jax.ShapeDtypeStruct((count // 4, eight, cols), F32), pieces),
        [pltpu.VMEM(x.shape, F32), pltpu.VMEM(pieces.shape, F32), pltpu.VMEM(pieces.shape, F32)]
        + [dma] * 6,
        ident,
        20,
    )


def swap(x, k):
    devices = PLANE * lax.axis_size("z")
    return lax.ppermute(x, ALL, [(i, i ^ k) for i in range(devices)])


def quiet_gather(x):
    even = jnp.stack([x] + [swap(x, k) for k in (2, 4, 6)])
    return jnp.stack([even, swap(even, 1)], axis=1).reshape((PLANE,) + x.shape)


def quiet_scatter(p):
    pairs = p.reshape((4, 2) + p.shape[1:])
    here, there = pairs[:, 0], pairs[:, 1]
    q = (here.astype(F32) + swap(there, 1).astype(F32)).astype(BF)
    x, y, xy = swap(q[1], 2), swap(q[2], 4), swap(q[3], 6)
    return q[0].astype(F32) + x.astype(F32) + y.astype(F32) + xy.astype(F32)


def z_gather(x):
    return lax.all_gather(x, "z", axis=0, tiled=True)


def z_scatter(g):
    return lax.psum_scatter(g, "z", scatter_dimension=0, tiled=True)


def norm_mod(value, shift, scale):
    normed = value * lax.rsqrt(jnp.mean(value * value, axis=-1, keepdims=True) + EPS)
    return normed * (1.0 + scale) + shift


def dot(a, b):
    return jnp.dot(a, b, preferred_element_type=F32)


def over_rows(left, right):
    return lax.dot_general(left, right, (((0,), (0,)), ((), ())), preferred_element_type=F32)


def times_t(left, right):
    return lax.dot_general(left, right, (((1,), (1,)), ((), ())), preferred_element_type=F32)


def softmax_rows(q, k, bias, factor):
    scores = times_t(q, k) * factor + bias.astype(F32)
    expo = jnp.exp(scores - jnp.max(scores, axis=-1, keepdims=True))
    return expo / jnp.sum(expo, axis=-1, keepdims=True)


def row_blocks(count):
    step = math.gcd(count, 256)
    return [slice(i, i + step) for i in range(0, count, step)]


def attend_kernel(factor, qkv, bias, o):
    n = o.shape[1]
    for c in range(0, n, HEAD_DIM):
        k = qkv[:, n + c : n + c + HEAD_DIM]
        v = qkv[:, 2 * n + c : 2 * n + c + HEAD_DIM]
        for r in row_blocks(o.shape[0]):
            prob = softmax_rows(qkv[r, c : c + HEAD_DIM], k, bias[0, r, :], factor)
            o[r, c : c + HEAD_DIM] = dot(prob.astype(BF), v).astype(BF)


def attend_back_kernel(factor, qkv, bias, d_o, d_qkv):
    n = d_o.shape[1]
    for c in range(0, n, HEAD_DIM):
        k = qkv[:, n + c : n + c + HEAD_DIM]
        v = qkv[:, 2 * n + c : 2 * n + c + HEAD_DIM]
        dk = dv = 0.0
        for r in row_blocks(d_o.shape[0]):
            q = qkv[r, c : c + HEAD_DIM]
            out = d_o[r, c : c + HEAD_DIM]
            prob = softmax_rows(q, k, bias[0, r, :], factor)
            d_prob = times_t(out, v)
            delta = jnp.sum(prob * d_prob, axis=-1, keepdims=True)
            d_scores = (prob * (d_prob - delta)).astype(BF)
            d_qkv[r, c : c + HEAD_DIM] = (dot(d_scores, k) * factor).astype(BF)
            dk = dk + over_rows(d_scores, q)
            dv = dv + over_rows(prob.astype(BF), out)
        d_qkv[:, n + c : n + c + HEAD_DIM] = (dk * factor).astype(BF)
        d_qkv[:, 2 * n + c : 2 * n + c + HEAD_DIM] = dv.astype(BF)


def per_group(kernel, ins, bias, columns, group, flops):
    block = lambda c: pl.BlockSpec((group, c), lambda i: (i, 0))
    return pl.pallas_call(
        kernel,
        grid=(bias.shape[0],),
        out_shape=jax.ShapeDtypeStruct((bias.shape[0] * group, columns), BF),
        in_specs=[block(ins[0].shape[1]), pl.BlockSpec((1, group, group), lambda i: (i, 0, 0))]
        + [block(a.shape[1]) for a in ins[1:]],
        out_specs=block(columns),
        compiler_params=pltpu.CompilerParams(vmem_limit_bytes=48 * MIB),
        cost_estimate=pl.CostEstimate(flops=flops, bytes_accessed=0, transcendentals=0),
    )(ins[0], bias, *ins[1:])


def after(value, *others):
    return lax.optimization_barrier((value,) + others)[0]


def on_device(
    tokens,
    noise_table,
    mod_weight,
    qkv_weight,
    out_weight,
    up_weight,
    down_weight,
    segment,
    key_valid,
    noise_level,
    cotangent,
):
    rows, width = tokens.shape[1:]
    images = noise_level.shape[1]
    nz = lax.axis_size("z")
    blks = lax.axis_size("blk")
    z, y, blk = (lax.axis_index(a) for a in ALL)
    devices = nz * PLANE
    group = rows * blks
    local = HEADS // PLANE
    factor = 1.0 / math.sqrt(HEAD_DIM)

    levels = noise_level.reshape(-1)
    cond = jnp.take(noise_table, levels, axis=0)
    cols = dot(cond, mod_weight).reshape(2 * nz, 1, images, -1)
    sent = jnp.broadcast_to(cols, (2 * nz, blks) + cols.shape[2:])
    sent = jnp.pad(sent.reshape((devices,) + cols.shape[2:]), ((0, 0), (0, 8 - images), (0, 0)))

    mods = exchange(sent, 14)[:, :images]

    (qkv_part,) = spread([after(qkv_weight, mods)], 1, blocks=3)
    mods = mods.transpose(1, 0, 2).reshape(images, 6, width)
    qkv_w = z_gather(qkv_part)
    move = [(nz * k + i, i * PLANE + k) for k in range(PLANE) for i in range(nz)]
    outp = lax.ppermute(after(out_weight, qkv_part), ALL, move)

    both = jnp.concatenate([segment, key_valid], axis=0)
    other = lax.ppermute(both, "y", [(0, 1), (1, 0)])
    order = lambda a: jnp.stack(
        [
            lax.dynamic_index_in_dim(
                a.reshape(2, blks, rows),
                (lax.div(blk, 2) ^ (k >> 1)) * 2 + (lax.rem(blk, 2) ^ (k & 1)),
                1,
                keepdims=False,
            )
            for k in range(blks)
        ],
        axis=1,
    ).reshape(2, group)
    both, other = order(both), order(other)
    seg = jnp.stack([both[0], other[0]])
    valid = jnp.stack([both[1], other[1]])
    seg_own = seg[0, :rows]
    eye = jnp.arange(group)[:, None] == jnp.arange(group)[None, :]
    allowed = (seg[:, :, None] == seg[:, None, :]) & ((valid[:, None, :] == 1) | eye[None])
    bias = jnp.where(allowed, 0.0, NEG).astype(BF)

    def pick(which):
        m = mods[:, which]
        s = seg_own[:, None]
        out = m[images - 1][None]
        for i in range(images - 2, -1, -1):
            out = jnp.where(s == i, m[i][None], out)
        return out

    x_in = tokens[0].astype(F32)
    grad_in = cotangent[0].astype(F32)
    shift1, scale1, gate1, shift2, scale2, gate2 = (pick(i) for i in range(6))
    first_f, first_back = jax.vjp(norm_mod, x_in, shift1, scale1)
    d_branch_own = (gate2 * grad_in).astype(BF)
    first = plane_gather(after(first_f.astype(BF), qkv_part), 2).reshape(2 * group, width)
    up_part, down_part = spread([after(up_weight, first), down_weight], 3)
    outp_w, up_w, down_w = z_gather(outp), z_gather(up_part), z_gather(down_part)

    qkv = dot(first, qkv_w).astype(BF)
    own_cols = local * HEAD_DIM
    cost = 4 * 2 * group * group * own_cols
    mixed = per_group(
        functools.partial(attend_kernel, factor), [qkv], bias, own_cols, group, 5 * cost
    )
    part = dot(mixed, outp_w).astype(BF).reshape(PLANE, rows, width)
    attn = plane_scatter(part, 6)
    x_mid = x_in + gate1 * attn
    second_f, second_back = jax.vjp(norm_mod, x_mid, shift2, scale2)
    second = plane_gather(second_f.astype(BF), 7).reshape(2 * group, width)
    hidden_pre = dot(second, up_w)
    hidden_f, gelu_back = jax.vjp(jax.nn.gelu, hidden_pre)
    hidden = hidden_f.astype(BF)

    d_branch = plane_gather(after(d_branch_own, hidden), 5).reshape(2 * group, width)
    d_down = over_rows(d_branch, hidden).astype(BF)
    d_down, d_branch = lax.optimization_barrier((d_down, d_branch))
    d_down = z_scatter(d_down)
    d_pre = gelu_back(dot(d_branch, down_w))[0].astype(BF)
    d_up = over_rows(second, d_pre).astype(BF)
    d_up, d_pre = lax.optimization_barrier((d_up, d_pre))
    d_up = z_scatter(d_up)
    part = times_t(d_pre, up_w).astype(BF).reshape(PLANE, rows, width)
    d_second = plane_scatter(part, 9)
    d_mid_norm, d_shift2, d_scale2 = second_back(d_second)
    d_mid = grad_in + d_mid_norm
    d_attn = (gate1 * d_mid).astype(BF)
    d_gate1 = d_mid * attn
    d_attn_all = plane_gather(d_attn, 10).reshape(2 * group, width)
    d_mixed = times_t(d_attn_all, outp_w).astype(BF)
    d_qkv = per_group(
        functools.partial(attend_back_kernel, factor),
        [qkv, d_mixed],
        bias,
        3 * own_cols,
        group,
        10 * cost,
    )
    d_qkv_w = over_rows(first, d_qkv).astype(BF)
    d_qkv_w, d_qkv, d_attn_all = lax.optimization_barrier((d_qkv_w, d_qkv, d_attn_all))
    d_qkv_w = z_scatter(d_qkv_w)
    d_outp = over_rows(mixed, d_attn_all).astype(BF)
    d_outp, d_qkv = lax.optimization_barrier((d_outp, d_qkv))
    d_outp = z_scatter(d_outp)
    part = times_t(d_qkv, qkv_w).astype(BF).reshape(PLANE, rows, width)
    d_first = plane_scatter(part, 11)
    d_in_norm, d_shift1, d_scale1 = first_back(d_first)
    grad_tokens = d_mid + d_in_norm
    part = times_t(after(hidden, d_first), down_w).astype(BF).reshape(PLANE, rows, width)
    branch = plane_scatter(part, 8)
    block_out = (x_mid + gate2 * branch).astype(BF)
    d_gate2 = grad_in * branch

    tok_grads = jnp.concatenate([d_shift1, d_scale1, d_gate1, d_shift2, d_scale2, d_gate2], axis=1)
    picker = (seg_own[:, None] == jnp.arange(8, dtype=jnp.int32)[None, :]).astype(F32)
    image_grads = lax.dot_general(picker, tok_grads, (((0,), (0,)), ((), ())), precision=HIGH)
    sent = image_grads.reshape(8, devices, -1).transpose(1, 0, 2)
    mod_grads, cond_grads = mods_back(sent, mod_weight, 15)
    mod_grads = mod_grads[:, :images].reshape(2 * nz * images, -1)
    grad_mod = lax.dot_general(
        cond.astype(F32), mod_grads, (((0,), (0,)), ((), ())), precision=HIGH
    )
    cond_grads = cond_grads.reshape(2 * nz, 4, 8, width // 4)[:, :, :images]
    cond_grads = cond_grads.transpose(0, 2, 1, 3).reshape(2 * nz * images, width)
    grad_table = jax.ops.segment_sum(cond_grads, levels, num_segments=noise_table.shape[0])

    d_down = after(d_down, sent)
    d_up, d_down = collect([d_up, d_down], 12)
    (d_qkv_w,) = collect([after(d_qkv_w, d_up)], 13, blocks=3)
    d_outp = lax.ppermute(d_outp, ALL, [(b, a) for a, b in move])
    return (
        block_out[None],
        grad_tokens[None],
        grad_table,
        grad_mod,
        d_qkv_w.astype(F32),
        d_outp.astype(F32),
        d_up.astype(F32),
        d_down.astype(F32),
    )


def solution(mesh):
    groups, blks = mesh.shape["dp"], mesh.shape["blk"]
    planes = Mesh(mesh.devices.reshape(groups // 2, 2, blks), ALL)
    dp = ("z", "y")
    whole = ("z", "y", "blk")
    placed = (
        P(dp, "blk", None),
        P(),
        P(None, whole),
        P(whole, None),
        P(whole, None),
        P(whole, None),
        P(whole, None),
        P(dp, None),
        P(dp, None),
        P(),
        P(dp, "blk", None),
    )
    return jax.shard_map(
        on_device,
        mesh=planes,
        in_specs=placed,
        out_specs=(
            P(dp, "blk", None),
            P(dp, "blk", None),
            P(),
            P(None, whole),
            P(whole, None),
            P(whole, None),
            P(whole, None),
            P(whole, None),
        ),
        check_vma=False,
    )
```

time: 1010 us -> 741 us (0.73)
  starting transfers between devices: 171 us -> 4.64 us
  other arithmetic: 119 us -> 23.1 us
  local copies, waits for them, and re-layouts: 93.9 us -> 30.8 us
  Pallas kernels: 388 us -> 440 us
  matrix products: 128 us -> 105 us
  waiting for transfers between devices: 97 us -> 118 us
  between operations: 2.79 us -> 15.4 us
    ppermute x49 -> x1, starting transfers between devices: 144 us -> 0.68 us  [on_device(): outp = lax.ppermute(after(out_weight, qkv_part), ALL, move)]
    pallas_call x0 -> x4, Pallas kernels: none -> 108 us  [the longest x2 89.2 us: small_call(): pl.pallas_call(kernel, out_shape=outs, in_specs=[vmem] * len(ins), out_sp...]
    ppermute x49 -> x1, waiting for transfers between devices: 97 us -> 0.01 us  [on_device(): outp = lax.ppermute(after(out_weight, qkv_part), ALL, move)]
    reduce_scatter x0 -> x4, waiting for transfers between devices: none -> 94.9 us  [z_scatter(): return lax.psum_scatter(g, 'z', scatter_dimension=0, tiled=True)]
    convert_element_type x20 -> x3, other arithmetic: 65.9 us -> 4.15 us  [the longest x1 2.21 us: on_device(): bias = jnp.where(allowed, 0.0, NEG).astype(BF)]
    pallas_call x13 -> x12, Pallas kernels: 388 us -> 332 us  [call(): pl.pallas_call(kernel, out_shape=outs, in_specs=[pl.BlockSpec(memory_spac...]
    dot_general x7 -> x0, matrix products: 29.6 us -> none  [the longest x1 6.98 us: on_device(): jnp.einsum('gqhd,gkhd->ghqk', d_mixed, v_h, preferred_element_type=F32)]
    all_to_all x4 -> x0, starting transfers between devices: 20.3 us -> none  [the longest x1 11.2 us: on_device(): cond_grads = lax.all_to_all(sent, ALL, 0, 0, tiled=True)]
  transfers between devices with their start and end apart: 55 -> 11, of which waited for: 10 -> 4; matrix products, arithmetic and copies ran while one was open for 32% -> 11% of each run, Pallas kernels for 35% -> 46%
where the time goes in v2:
time: 741 us; the launch traced here: 736 us
  Pallas kernels  440 us (59%)
  waiting for transfers between devices  118 us (16%)
  matrix products  105 us (14%)
  local copies, waits for them, and re-layouts  30.8 us (4%)
  other arithmetic  23.1 us (3%)
  between operations  15.4 us (2%)
    pallas_call x12, Pallas kernels, call(): pl.pallas_call(kernel, out_shape=outs, in_specs=[pl.BlockSpec(memory_spac...  332 us
    reduce_scatter x4, waiting for transfers between devices, z_scatter(): return lax.psum_scatter(g, 'z', scatter_dimension=0, tiled=True)  94.9 us
    pallas_call x2, Pallas kernels, small_call(): pl.pallas_call(kernel, out_shape=outs, in_specs=[vmem] * len(ins), out_sp...  89.2 us
    dot_general x5, matrix products, dot(): return jnp.dot(a, b, preferred_element_type=F32)  39.5 us
    dot_general x4, matrix products, over_rows(): lax.dot_general(left, right, (((0,), (0,)), ((), ())), preferred_element_...  32.5 us
    dot_general x4, matrix products, times_t(): lax.dot_general(left, right, (((1,), (1,)), ((), ())), preferred_element_...  26.6 us
    unnamed x125, local copies, waits for them, and re-layouts  26.3 us
    all_gather x4, waiting for transfers between devices, z_gather(): return lax.all_gather(x, 'z', axis=0, tiled=True)  19.5 us
  transfers between devices with their start and end apart: 11, of which 4 were waited for; matrix products, arithmetic and copies ran while one was open for 11% of the time, Pallas kernels for 46%

profile of v2, /device:TPU:0, one launch (start us, length us, event | category | flops | bytes accessed | tf_op | source)
XLA Modules:
  0.0 736.2 jit_solution(8427425711079484775)
XLA Ops:
  8.5 14.4 %shard_map.171 = bf16[512,768]{1,0:T(8,128)(2,1)} custom-call(bf16[64,6144]{1,0:T(8,128)(2,1)S(1)} %copy-done.12), custom_call_target="tpu_custom_call" | custom-call | bytes 47185920 | tf_op jit(solution)/shard_map/pallas_call | solution.py:64
  24.1 3.4 gather_fusion
  28.3 34.5 %shard_map.170 = f32[32,8,384]{2,1,0:T(8,128)S(1)} custom-call(f32[32,8,384]{2,1,0:T(8,128)S(1)} %pad.4.x), custom_call_target="tpu_custom_call" | custom-call | bytes 28800000 | tf_op jit(solution)/shard_map/pallas_call | solution.py:416
  65.8 36.6 %shard_map.172 = bf16[8,192,2048]{2,1,0:T(8,128)(2,1)S(1)} custom-call(bf16[192,2048]{1,0:T(8,128)(2,1)S(1)} %get-tuple-element.32.x), custom_call_target="tpu_custom_call" | custom-call | bytes 108000000 | tf_op jit(solution)/shard_map/pallas_call | solution.py:64
  105.3 25.7 %shard_map.176 = (bf16[512,1024]{1,0:T(8,128)(2,1)}, bf16[512,1024]{1,0:T(8,128)(2,1)}) custom-call(bf16[64,8192]{1,0:T(8,128)(2,1)S(1)} %copy-done.8, bf16[64,8192]{1,0:T(8,128)(2,1)S(1)} %copy-done.9), custom_call_target="tpu_custom_call" | custom-call | bytes 125829120 | tf_op jit(solution)/shard_map/pallas_call | solution.py:64
  137.3 8.2 %convolution_convert_fusion.6.qkv = bf16[1536,768]{1,0:T(8,128)(2,1)S(1)} fusion(bf16[1536,2048]{1,0:T(8,128)(2,1)} %bitcast.90, bf16[2048,768]{1,0:T(8,128)(2,1)} %all-gather.5.cloned.1.call-done), kind=kOutput, calls=%fused_computation.21 | convolution fusion | flops 4833017856 | bytes 11796480 | tf_op jit(solution)/shard_map/dot_general | solution.py:516
  145.5 6.8 shard_map.173
  153.7 3.3 convolution_convert_fusion.1
  157.0 31.4 %shard_map.174 = f32[192,2048]{1,0:T(8,128)S(1)} custom-call(bf16[8,192,2048]{2,1,0:T(8,128)(2,1)S(1)} %bitcast.89), custom_call_target="tpu_custom_call" | custom-call | bytes 111600000 | tf_op jit(solution)/shard_map/pallas_call | solution.py:64
  191.7 30.0 %shard_map.175 = bf16[8,192,2048]{2,1,0:T(8,128)(2,1)S(1)} custom-call(bf16[192,2048]{1,0:T(8,128)(2,1)S(1)} %add_convert_fusion.1.x), custom_call_target="tpu_custom_call" | custom-call | bytes 108000000 | tf_op jit(solution)/shard_map/pallas_call | solution.py:64
  224.3 13.5 %multiply_convert_fusion = (bf16[1536,1024]{1,0:T(8,128)(2,1)S(1)}, f32[1536,1024]{1,0:T(8,128)}) fusion(bf16[1536,2048]{1,0:T(8,128)(2,1)} %bitcast.94, bf16[2048,1024]{1,0:T(8,128)(2,1)} %all-gather.9.cloned.1.call-done), kind=kOutput, calls=%fused_computation.15 | convolution fusion | flops 6456606720 | bytes 19922944 | tf_op jit(solution)/shard_map/dot_general | solution.py:516
  237.9 30.6 %shard_map.177 = bf16[8,192,2048]{2,1,0:T(8,128)(2,1)S(1)} custom-call(bf16[192,2048]{1,0:T(8,128)(2,1)S(1)} %get-tuple-element.36.x), custom_call_target="tpu_custom_call" | custom-call | bytes 108000000 | tf_op jit(solution)/shard_map/pallas_call | solution.py:64
  271.0 8.6 %convolution_convert_fusion.5 = bf16[2048,1024]{1,0:T(8,128)(2,1)} fusion(bf16[1536,2048]{1,0:T(8,128)(2,1)S(1)} %bitcast.96, bf16[1536,1024]{1,0:T(8,128)(2,1)S(1)} %get-tuple-element.43), kind=kOutput, calls=%fused_computation.20 | convolution fusion | flops 6444548096 | bytes 13631488 | tf_op jit(solution)/shard_map/dot_general | solution.py:520
  279.6 19.5 %all-gather.11.cloned.1.call-done = bf16[2048,1024]{1,0:T(8,128)(2,1)} async-done(((bf16[512,1024]{1,0:T(8,128)(2,1)}), bf16[2048,1024]{1,0:T(8,128)(2,1)}) %all-gather.11.cloned.1.call-update) | async-done | bytes 4194320 | tf_op jit(solution)/shard_map/all_gather | solution.py:503
  299.1 14.1 %fusion.6 = bf16[1536,1024]{1,0:T(8,128)(2,1)S(1)} fusion(f32[1536,1024]{1,0:T(8,128)} %get-tuple-element.99, bf16[1536,2048]{1,0:T(8,128)(2,1)} %bitcast.97, bf16[2048,1024]{1,0:T(8,128)(2,1)} %all-gather.11.cloned.1.call-done), kind=kOutput, calls=%fused_computation.14 | convolution fusion | flops 6473908224 | bytes 19922944 | tf_op jit(solution)/shard_map/dot_general | solution.py:516
  314.9 11.6 %convolution_convert_fusion.4 = bf16[2048,1024]{1,0:T(8,128)(2,1)} fusion(bf16[1536,2048]{1,0:T(8,128)(2,1)} %bitcast.95, bf16[1536,1024]{1,0:T(8,128)(2,1)S(1)} %fusion.6), kind=kOutput, calls=%fused_computation.19 | convolution fusion | flops 6444548096 | bytes 13631488 | tf_op jit(solution)/shard_map/dot_general | solution.py:520
  326.4 9.6 %convolution_convert_fusion.3 = bf16[1536,2048]{1,0:T(8,128)(2,1)S(1)} fusion(bf16[1536,1024]{1,0:T(8,128)(2,1)} %copy-done.58, bf16[2048,1024]{1,0:T(8,128)(2,1)} %all-gather.9.cloned.1.call-done), kind=kOutput, calls=%fused_computation.7 | convolution fusion | flops 6445596672 | bytes 13631488 | tf_op jit(solution)/shard_map/dot_general | solution.py:524
  336.1 31.8 %shard_map.178 = f32[192,2048]{1,0:T(8,128)S(1)} custom-call(bf16[8,192,2048]{2,1,0:T(8,128)(2,1)S(1)} %bitcast.98), custom_call_target="tpu_custom_call" | custom-call | bytes 111600000 | tf_op jit(solution)/shard_map/pallas_call | solution.py:64
  371.3 30.2 %shard_map.179 = bf16[8,192,2048]{2,1,0:T(8,128)(2,1)S(1)} custom-call(bf16[192,2048]{1,0:T(8,128)(2,1)S(1)} %get-tuple-element.54.x), custom_call_target="tpu_custom_call" | custom-call | bytes 108000000 | tf_op jit(solution)/shard_map/pallas_call | solution.py:64
  406.2 12.1 %shard_map.180 = bf16[1536,768]{1,0:T(8,128)(2,1)S(1)} custom-call(bf16[1536,768]{1,0:T(8,128)(2,1)S(1)} %copy-done.15, bf16[2,768,768]{2,1,0:T(8,128)(2,1)} %select_convert_fusion.bias, bf16[1536,256]{1,0:T(8,128)(2,1)S(1)} %convolution_convert_fusion.9.d_o), custom_call_target="tpu_custom_call" | custom-call | flops 12079595520 | tf_op jit(solution)/shard_map/pallas_call | solution.py:570
  419.8 6.5 convolution_convert_fusion.7
  426.3 5.8 convolution_convert_fusion.8
  434.2 7.9 %convolution_convert_fusion = bf16[1536,2048]{1,0:T(8,128)(2,1)S(1)} fusion(bf16[1536,768]{1,0:T(8,128)(2,1)} %copy-done.16, bf16[2048,768]{1,0:T(8,128)(2,1)} %all-gather.5.cloned.1.call-done), kind=kOutput, calls=%fused_computation.4 | convolution fusion | flops 4834983936 | bytes 11796480 | tf_op jit(solution)/shard_map/dot_general | solution.py:524
  442.1 31.4 %shard_map.181 = f32[192,2048]{1,0:T(8,128)S(1)} custom-call(bf16[8,192,2048]{2,1,0:T(8,128)(2,1)S(1)} %bitcast.99), custom_call_target="tpu_custom_call" | custom-call | bytes 111600000 | tf_op jit(solution)/shard_map/pallas_call | solution.py:64
  473.5 7.2 convolution_convert_fusion.2
  480.7 31.0 %shard_map.182 = f32[192,2048]{1,0:T(8,128)S(1)} custom-call(bf16[8,192,2048]{2,1,0:T(8,128)(2,1)S(1)} %bitcast.100), custom_call_target="tpu_custom_call" | custom-call | bytes 111600000 | tf_op jit(solution)/shard_map/pallas_call | solution.py:64
  522.6 54.7 %shard_map.183 = (f32[8,8,384]{2,1,0:T(8,128)S(1)}, f32[32,8,512]{2,1,0:T(8,128)S(1)}) custom-call(f32[32,8,384]{2,1,0:T(8,128)S(1)} %bitcast.101, bf16[2048,384]{1,0:T(8,128)(2,1)S(1)} %copy-done.6), custom_call_target="tpu_custom_call" | custom-call | bytes 72000000 | tf_op jit(solution)/shard_map/pallas_call | solution.py:416
  577.6 4.8 scatter_custom_fusion
  588.0 59.0 %reduce-scatter.7.cloned.1.call-done.refs_0_ = bf16[512,1024]{1,0:T(8,128)(2,1)} async-done(((bf16[2048,1024]{1,0:T(8,128)(2,1)}), bf16[512,1024]{1,0:T(8,128)(2,1)}) %reduce-scatter.7.cloned.1.call-update) | async-done | bytes 1048592 | tf_op jit(solution)/shard_map/reduce_scatter | solution.py:507
  649.4 25.6 %shard_map.184 = (bf16[64,8192]{1,0:T(8,128)(2,1)S(1)}, bf16[64,8192]{1,0:T(8,128)(2,1)S(1)}) custom-call(bf16[512,1024]{1,0:T(8,128)(2,1)S(1)} %copy-done.11, bf16[512,1024]{1,0:T(8,128)(2,1)S(1)} %copy-done.10), custom_call_target="tpu_custom_call" | custom-call | bytes 125829120 | tf_op jit(solution)/shard_map/pallas_call | solution.py:64
  676.5 36.0 %reduce-scatter.5.cloned.1.call-done.refs_0_ = bf16[512,768]{1,0:T(8,128)(2,1)} async-done(((bf16[2048,768]{1,0:T(8,128)(2,1)}), bf16[512,768]{1,0:T(8,128)(2,1)}) %reduce-scatter.5.cloned.1.call-update) | async-done | bytes 786448 | tf_op jit(solution)/shard_map/reduce_scatter | solution.py:507
  713.6 12.8 %shard_map.185 = bf16[64,6144]{1,0:T(8,128)(2,1)S(1)} custom-call(bf16[512,768]{1,0:T(8,128)(2,1)S(1)} %copy-done.13), custom_call_target="tpu_custom_call" | custom-call | bytes 47185920 | tf_op jit(solution)/shard_map/pallas_call | solution.py:64
  (211 shorter events, 62.3 us)
Async XLA Ops:
  7.2 130.1 %all-gather.5.cloned.1.call-start = ((), (), s32[]{:S(2)}) async-start(), calls=%async_computation.4 | async-start | bytes 3932160 | tf_op jit(solution)/shard_map/all_gather | solution.py:503
  22.9 130.8 %all-gather.7.cloned.1.call-start = ((), (), s32[]{:S(2)}) async-start(), calls=%async_computation.5 | async-start | bytes 1310720 | tf_op jit(solution)/shard_map/all_gather | solution.py:503
  23.0 39.9 %collective-permute-start.1 = (bf16[64,2048]{1,0:T(8,128)(2,1)S(1)}, bf16[64,2048]{1,0:T(8,128)(2,1)S(1)}, u32[]{:S(2)}, u32[]{:S(2)}) collective-permute-start(bf16[64,2048]{1,0:T(8,128)(2,1)S(1)} %copy-done.55), channel_id=1, source_target_pairs={{0,0},{1,8},{2,16},{3,24},{4,1},{5,9},{6,17},{7,25},{8,2},{9,10},{... | collective-permute-start | bytes 786440 | tf_op jit(solution)/shard_map/ppermute | solution.py:621
  27.5 36.1 %copy-start.27 = (bf16[24,2048]{1,0:T(8,128)(2,1)}, bf16[24,2048]{1,0:T(8,128)(2,1)S(1)}, u32[]{:S(2)}) copy-start(bf16[24,2048]{1,0:T(8,128)(2,1)S(1)} %gather_fusion) | copy-start | bytes 294916
  27.6 36.1 %copy-start.20 = (bf16[1,192,2048]{2,1,0:T(8,128)(2,1)S(1)}, bf16[1,192,2048]{2,1,0:T(8,128)(2,1)}, u32[]{:S(2)}) copy-start(bf16[1,192,2048]{2,1,0:T(8,128)(2,1)} %param.11) | copy-start | bytes 2359300
  28.0 36.7 %copy-start.23 = (bf16[1,192,2048]{2,1,0:T(8,128)(2,1)S(1)}, bf16[1,192,2048]{2,1,0:T(8,128)(2,1)}, u32[]{:S(2)}) copy-start(bf16[1,192,2048]{2,1,0:T(8,128)(2,1)} %param.21) | copy-start | bytes 2359300
  28.2 35.8 %copy-start.46 = (s32[1,192]{1,0:T(1,128)}, s32[1,192]{1,0:T(1,128)S(1)}, u32[]{:S(2)}) copy-start(s32[1,192]{1,0:T(1,128)S(1)} %slice.159) | copy-start | bytes 2308
  63.6 160.7 %all-gather.9.cloned.1.call-start = ((), (), s32[]{:S(2)}) async-start(), calls=%async_computation.6 | async-start | bytes 5242880 | tf_op jit(solution)/shard_map/all_gather | solution.py:503
  63.9 38.5 %copy-start.42 = (f32[192]{0:T(256)}, f32[192]{0:T(256)S(1)}, u32[]{:S(2)}) copy-start(f32[192]{0:T(256)S(1)} %fusion.27) | copy-start | bytes 2308
  64.6 37.9 %copy-start.30 = (f32[1,1,2048]{2,1,0:T(1,128)}, f32[1,1,2048]{2,1,0:T(1,128)S(1)}, u32[]{:S(2)}) copy-start(f32[1,1,2048]{2,1,0:T(1,128)S(1)} %get-tuple-element.76) | copy-start | bytes 24580
  64.6 37.9 %copy-start.32 = (f32[1,1,2048]{2,1,0:T(1,128)}, f32[1,1,2048]{2,1,0:T(1,128)S(1)}, u32[]{:S(2)}) copy-start(f32[1,1,2048]{2,1,0:T(1,128)S(1)} %get-tuple-element.77) | copy-start | bytes 24580
  64.6 37.9 %copy-start.34 = (f32[1,1,2048]{2,1,0:T(1,128)}, f32[1,1,2048]{2,1,0:T(1,128)S(1)}, u32[]{:S(2)}) copy-start(f32[1,1,2048]{2,1,0:T(1,128)S(1)} %get-tuple-element.78) | copy-start | bytes 24580
  64.6 37.9 %copy-start.36 = (f32[1,1,2048]{2,1,0:T(1,128)}, f32[1,1,2048]{2,1,0:T(1,128)S(1)}, u32[]{:S(2)}) copy-start(f32[1,1,2048]{2,1,0:T(1,128)S(1)} %get-tuple-element.64) | copy-start | bytes 24580
  64.7 37.9 %copy-start.38 = (f32[1,1,2048]{2,1,0:T(1,128)}, f32[1,1,2048]{2,1,0:T(1,128)S(1)}, u32[]{:S(2)}) copy-start(f32[1,1,2048]{2,1,0:T(1,128)S(1)} %get-tuple-element.71) | copy-start | bytes 24580
  64.7 37.9 %copy-start.40 = (f32[1,1,2048]{2,1,0:T(1,128)}, f32[1,1,2048]{2,1,0:T(1,128)S(1)}, u32[]{:S(2)}) copy-start(f32[1,1,2048]{2,1,0:T(1,128)S(1)} %get-tuple-element.72) | copy-start | bytes 24580
  65.8 39.4 %copy-start.8 = (bf16[64,8192]{1,0:T(8,128)(2,1)S(1)}, bf16[64,8192]{1,0:T(8,128)(2,1)}, u32[]{:S(2)}) copy-start(bf16[64,8192]{1,0:T(8,128)(2,1)} %refs_0_.1) | copy-start | bytes 3145732
  65.8 39.4 %copy-start.9 = (bf16[64,8192]{1,0:T(8,128)(2,1)S(1)}, bf16[64,8192]{1,0:T(8,128)(2,1)}, u32[]{:S(2)}) copy-start(bf16[64,8192]{1,0:T(8,128)(2,1)} %refs_1_.1) | copy-start | bytes 3145732
  131.0 168.1 %all-gather.11.cloned.1.call-start = ((), (), s32[]{:S(2)}) async-start(), calls=%async_computation.7 | async-start | bytes 5242880 | tf_op jit(solution)/shard_map/all_gather | solution.py:503
  131.0 3.7 collective-permute-start
  132.9 449.5 %reduce-scatter.11.cloned.1.call-start = ((), (), s32[]{:S(2)}) async-start(), calls=%async_computation.11 | async-start | bytes 1310720 | tf_op jit(solution)/shard_map/reduce_scatter | solution.py:507
  336.1 31.8 %copy-start.18 = (f32[192,2048]{1,0:T(8,128)S(1)}, f32[192,2048]{1,0:T(8,128)}, u32[]{:S(2)}) copy-start(f32[192,2048]{1,0:T(8,128)} %copy-done.17) | copy-start | bytes 4718596
  371.3 32.9 %copy-start.26 = (bf16[256,2048]{1,0:T(8,128)(2,1)S(1)}, bf16[256,2048]{1,0:T(8,128)(2,1)}, u32[]{:S(2)}) copy-start(bf16[256,2048]{1,0:T(8,128)(2,1)} %all-gather.7.cloned.1.call-done) | copy-start | bytes 3145732
  432.2 155.9 %reduce-scatter.9.cloned.1.call-start = ((), (), s32[]{:S(2)}) async-start(), calls=%async_computation.10 | async-start | bytes 5242880 | tf_op jit(solution)/shard_map/reduce_scatter | solution.py:507
  432.7 214.3 %reduce-scatter.7.cloned.1.call-start = ((), (), s32[]{:S(2)}) async-start(), calls=%async_computation.9 | async-start | bytes 5242880 | tf_op jit(solution)/shard_map/reduce_scatter | solution.py:507
  433.5 279.0 %reduce-scatter.5.cloned.1.call-start = ((), (), s32[]{:S(2)}) async-start(), calls=%async_computation.8 | async-start | bytes 3932160 | tf_op jit(solution)/shard_map/reduce_scatter | solution.py:507
  442.1 31.4 %copy-start.54 = (bf16[2048,1024]{1,0:T(8,128)(2,1)S(1)}, bf16[2048,1024]{1,0:T(8,128)(2,1)}, u32[]{:S(2)}) copy-start(bf16[2048,1024]{1,0:T(8,128)(2,1)} %all-gather.11.cloned.1.call-done) | copy-start | bytes 12582916
  442.1 31.4 %copy-start.57 = (bf16[1536,1024]{1,0:T(8,128)(2,1)S(1)}, bf16[1536,1024]{1,0:T(8,128)(2,1)}, u32[]{:S(2)}) copy-start(bf16[1536,1024]{1,0:T(8,128)(2,1)} %copy-done.56) | copy-start | bytes 9437188
  480.7 31.0 %copy-start.21 = (bf16[1,192,2048]{2,1,0:T(8,128)(2,1)S(1)}, bf16[1,192,2048]{2,1,0:T(8,128)(2,1)}, u32[]{:S(2)}) copy-start(bf16[1,192,2048]{2,1,0:T(8,128)(2,1)} %param.11) | copy-start | bytes 2359300
  480.7 31.0 %copy-start.31 = (f32[1,1,2048]{2,1,0:T(1,128)S(1)}, f32[1,1,2048]{2,1,0:T(1,128)}, u32[]{:S(2)}) copy-start(f32[1,1,2048]{2,1,0:T(1,128)} %copy-done.30) | copy-start | bytes 24580
  480.7 31.0 %copy-start.33 = (f32[1,1,2048]{2,1,0:T(1,128)S(1)}, f32[1,1,2048]{2,1,0:T(1,128)}, u32[]{:S(2)}) copy-start(f32[1,1,2048]{2,1,0:T(1,128)} %copy-done.32) | copy-start | bytes 24580
  480.7 31.0 %copy-start.35 = (f32[1,1,2048]{2,1,0:T(1,128)S(1)}, f32[1,1,2048]{2,1,0:T(1,128)}, u32[]{:S(2)}) copy-start(f32[1,1,2048]{2,1,0:T(1,128)} %copy-done.34) | copy-start | bytes 24580
  582.4 4.8 collective-permute-start.2
  (40 other events, 209.0 us)
Sparse Core Ops, SparseCore 0:
  23.1 77.4 all-gather.4
  102.7 27.1 all-gather.6
  131.5 86.8 all-gather.8
  219.7 79.2 all-gather.10
  432.3 25.1 reduce-scatter.10
  459.7 81.7 reduce-scatter.8
  543.8 103.1 reduce-scatter.6
  649.4 63.0 reduce-scatter.4

commit v3 on v2

--- a/solution.py
+++ b/solution.py
@@ -76,159 +76,203 @@
     )(*ins)
 
 
-def gather_kernel(x, o, xv, lsem, ssem, rsem):
-    rows = x.shape[0]
-    half = rows // 2
-    top, bot = pl.ds(0, half), pl.ds(half, half)
-    load = pltpu.make_async_copy(x, xv, lsem.at[0])
+class Gather:
+    shapes = staticmethod(lambda dma: [dma((1,)), dma((13,)), dma((13,))])
+
+    def __init__(self, xv, o, sems):
+        self.xv, self.o = xv, o
+        self.lsem, self.ssem, self.rsem = sems
+        self.rows = xv.shape[0]
+        self.all = []
+
+    def block(self, k, part=None):
+        half = self.rows // 2
+        first = k * self.rows + (half if part == 1 else 0)
+        return self.o.at[pl.ds(first, self.rows if part is None else half)]
+
+    def mine(self, part):
+        half = self.rows // 2
+        return self.xv.at[pl.ds(part * half, half)]
+
+    def go(self, src, dst, k):
+        i = len(self.all)
+        self.all.append(send(src, dst, self.ssem.at[i], self.rsem.at[i], k))
+        return self.all[-1]
+
+    def begin(self):
+        self.x_bot = self.go(self.mine(1), self.block(2, 1), 2)
+        self.y_top = self.go(self.mine(0), self.block(4, 0), 4)
+        self.x_top = self.go(self.mine(0), self.block(2, 0), 2)
+        self.y_bot = self.go(self.mine(1), self.block(4, 1), 4)
+        self.sib = self.go(self.xv, self.block(1), 1)
+        self.own = pltpu.make_async_copy(self.xv, self.block(0), self.lsem.at[0])
+        self.own.start()
+
+    def relay(self):
+        self.x_bot.wait_recv()
+        self.dy = self.go(self.block(2, 1), self.block(6, 1), 4)
+        self.late = [self.go(self.block(2, 1), self.block(3, 1), 1)]
+        self.y_top.wait_recv()
+        self.dx = self.go(self.block(4, 0), self.block(6, 0), 2)
+        self.late.append(self.go(self.block(4, 0), self.block(5, 0), 1))
+
+    def finish(self):
+        self.x_top.wait_recv()
+        self.late.append(self.go(self.block(2, 0), self.block(3, 0), 1))
+        self.y_bot.wait_recv()
+        self.late.append(self.go(self.block(4, 1), self.block(5, 1), 1))
+        self.dx.wait_recv()
+        self.late.append(self.go(self.block(6, 0), self.block(7, 0), 1))
+        self.dy.wait_recv()
+        self.late.append(self.go(self.block(6, 1), self.block(7, 1), 1))
+        for copy in [self.sib] + self.late:
+            copy.wait_recv()
+        for copy in self.all:
+            copy.wait_send()
+        self.own.wait()
+
+
+def gather_kernel(x, o, xv, load_sem, *sems):
+    load = pltpu.make_async_copy(x, xv, load_sem)
     load.start()
     greet((1, 2, 4))
     load.wait()
-    go = lambda i, src, dst, k: send(src, dst, ssem.at[i], rsem.at[i], k)
-    x_bot = go(0, xv.at[bot], o.at[2, bot], 2)
-    y_top = go(1, xv.at[top], o.at[4, top], 4)
-    x_top = go(2, xv.at[top], o.at[2, top], 2)
-    y_bot = go(3, xv.at[bot], o.at[4, bot], 4)
-    sib = go(4, xv, o.at[1], 1)
-    own = pltpu.make_async_copy(xv, o.at[0], lsem.at[1])
-    own.start()
-    x_bot.wait_recv()
-    dy = go(5, o.at[2, bot], o.at[6, bot], 4)
-    c0 = go(6, o.at[2, bot], o.at[3, bot], 1)
-    y_top.wait_recv()
-    dx = go(7, o.at[4, top], o.at[6, top], 2)
-    c1 = go(8, o.at[4, top], o.at[5, top], 1)
-    x_top.wait_recv()
-    c2 = go(9, o.at[2, top], o.at[3, top], 1)
-    y_bot.wait_recv()
-    c3 = go(10, o.at[4, bot], o.at[5, bot], 1)
-    dx.wait_recv()
-    c4 = go(11, o.at[6, top], o.at[7, top], 1)
-    dy.wait_recv()
-    c5 = go(12, o.at[6, bot], o.at[7, bot], 1)
-    for copy in (sib, c0, c1, c2, c3, c4, c5):
-        copy.wait_recv()
-    for copy in (x_bot, y_top, x_top, y_bot, sib, dy, c0, dx, c1, c2, c3, c4, c5):
-        copy.wait_send()
-    own.wait()
+    gather = Gather(xv, o, sems)
+    gather.begin()
+    gather.relay()
+    gather.finish()
 
 
 def plane_gather(x, ident):
-    out = jax.ShapeDtypeStruct((PLANE,) + x.shape, x.dtype)
+    out = jax.ShapeDtypeStruct((PLANE * x.shape[0],) + x.shape[1:], x.dtype)
     dma = pltpu.SemaphoreType.DMA
-    scratch = [pltpu.VMEM(x.shape, x.dtype), dma((2,)), dma((13,)), dma((13,))]
+    scratch = [pltpu.VMEM(x.shape, x.dtype), dma] + Gather.shapes(dma)
     return call(gather_kernel, (x,), out, scratch, ident, 8, 30)
 
 
-def rows_loop(rows, body):
-    step = 16
-
+def rows_loop(rows, body, step=16):
     def one(i, carry):
-        body(pl.ds(pl.multiple_of(i * step, step), step))
+        body(pl.multiple_of(i * step, step), step)
         return carry
 
     lax.fori_loop(0, rows // step, one, 0)
 
 
-def scatter_kernel(p, o, pv, rc, q6, q2, q4, d6, rx, ry, ov, lsem, ssem, rsem):
-    rows = o.shape[0]
-    half = rows // 2
-    top, bot = pl.ds(0, half), pl.ds(half, half)
+class Scatter:
+    @staticmethod
+    def shapes(rows, width, dma):
+        whole = pltpu.VMEM((4, rows, width), BF)
+        pair = pltpu.VMEM((2, rows // 2, width), BF)
+        return [whole, whole] + [pair] * 6 + [dma((4,)), dma((11,)), dma((11,))]
+
+    def __init__(self, p, ov, scratch):
+        self.p, self.ov = p, ov
+        self.pv, self.rc, self.q6, self.q2, self.q4, self.d6, self.rx, self.ry = scratch[:8]
+        self.lsem, self.ssem, self.rsem = scratch[8:]
+        self.rows = ov.shape[0]
+        self.half = self.rows // 2
+
+    def block(self, k, first=0, count=None):
+        return self.p.at[pl.ds(k * self.rows + first, count or self.rows)]
+
+    def go(self, i, src, dst, k):
+        return send(src, dst, self.ssem.at[i], self.rsem.at[i], k)
+
+    def begin(self):
+        half = self.half
+        top, bot = pl.ds(0, half), pl.ds(half, half)
+        self.c7t = self.go(0, self.block(7, 0, half), self.rc.at[3, top], 1)
+        self.c7b = self.go(1, self.block(7, half, half), self.rc.at[3, bot], 1)
+        self.c3 = self.go(2, self.block(3), self.rc.at[1], 1)
+        self.c5 = self.go(3, self.block(5), self.rc.at[2], 1)
+        self.c1 = self.go(4, self.block(1), self.rc.at[0], 1)
+
+    def load(self):
+        self.loads = [
+            pltpu.make_async_copy(self.block(2 * i), self.pv.at[i], self.lsem.at[i])
+            for i in range(4)
+        ]
+        for i in (3, 1, 2, 0):
+            self.loads[i].start()
+
+    def add(self, dst, i, start, more=None):
+        def body(r, n):
+            s = pl.ds(pl.multiple_of(start + r, 16), n)
+            total = self.pv[i, s, :].astype(F32) + self.rc[i, s, :].astype(F32)
+            if more is not None:
+                total = total + more[pl.ds(r, n), :].astype(F32)
+            dst[pl.ds(r, n), :] = total.astype(BF)
+
+        rows_loop(self.half, body)
+
+    def middle(self):
+        half = self.half
+        self.loads[3].wait()
+        self.c7t.wait_recv()
+        self.add(self.q6.at[0], 3, 0)
+        self.s6t = self.go(5, self.q6.at[0], self.d6.at[0], 2)
+        self.c7b.wait_recv()
+        self.add(self.q6.at[1], 3, half)
+        self.s6b = self.go(6, self.q6.at[1], self.d6.at[1], 4)
+        self.loads[1].wait()
+        self.c3.wait_recv()
+        self.add(self.q2.at[0], 1, 0)
+        self.s2t = self.go(7, self.q2.at[0], self.rx.at[0], 2)
+        self.loads[2].wait()
+        self.c5.wait_recv()
+        self.add(self.q4.at[1], 2, half)
+        self.s4b = self.go(8, self.q4.at[1], self.ry.at[1], 4)
+
+    def relay(self):
+        self.s6t.wait_recv()
+        self.add(self.q4.at[0], 2, 0, self.d6.at[0])
+        self.s4t = self.go(9, self.q4.at[0], self.ry.at[0], 4)
+        self.s6b.wait_recv()
+        self.add(self.q2.at[1], 1, self.half, self.d6.at[1])
+        self.s2b = self.go(10, self.q2.at[1], self.rx.at[1], 2)
+
+    def total(self, n):
+        def body(r, count):
+            s = pl.ds(pl.multiple_of(n * self.half + r, 16), count)
+            r = pl.ds(r, count)
+            total = self.pv[0, s, :].astype(F32) + self.rc[0, s, :].astype(F32)
+            total = total + self.rx[n, r, :].astype(F32) + self.ry[n, r, :].astype(F32)
+            self.ov[s, :] = total
+
+        rows_loop(self.half, body)
+
+    def finish(self):
+        self.loads[0].wait()
+        self.c1.wait_recv()
+        self.s2t.wait_recv()
+        self.s4t.wait_recv()
+        self.total(0)
+        self.s2b.wait_recv()
+        self.s4b.wait_recv()
+        self.total(1)
+        for copy in (self.c7t, self.c7b, self.c3, self.c5, self.c1, self.s6t, self.s6b):
+            copy.wait_send()
+        for copy in (self.s2t, self.s4b, self.s4t, self.s2b):
+            copy.wait_send()
+
+
+def scatter_kernel(p, o, ov, osem, *scratch):
     greet((1, 2, 4))
-    go = lambda i, src, dst, k: send(src, dst, ssem.at[i], rsem.at[i], k)
-    load = [pltpu.make_async_copy(p.at[2 * i], pv.at[i], lsem.at[i]) for i in range(4)]
-    c7t = go(0, p.at[7, top], rc.at[3, top], 1)
-    load[3].start()
-    c7b = go(1, p.at[7, bot], rc.at[3, bot], 1)
-    load[1].start()
-    c3 = go(2, p.at[3], rc.at[1], 1)
-    load[2].start()
-    c5 = go(3, p.at[5], rc.at[2], 1)
-    load[0].start()
-    c1 = go(4, p.at[1], rc.at[0], 1)
-
-    def add2(dst, i, start):
-        def body(r):
-            s = pl.ds(pl.multiple_of(start + r.start, 16), r.size)
-            dst[r, :] = (pv[i, s, :].astype(F32) + rc[i, s, :].astype(F32)).astype(BF)
-
-        rows_loop(half, body)
-
-    def add3(dst, i, start, more):
-        def body(r):
-            s = pl.ds(pl.multiple_of(start + r.start, 16), r.size)
-            total = pv[i, s, :].astype(F32) + rc[i, s, :].astype(F32) + more[r, :].astype(F32)
-            dst[r, :] = total.astype(BF)
-
-        rows_loop(half, body)
-
-    load[3].wait()
-    c7t.wait_recv()
-    add2(q6.at[0], 3, 0)
-    s6t = go(5, q6.at[0], d6.at[0], 2)
-    c7b.wait_recv()
-    add2(q6.at[1], 3, half)
-    s6b = go(6, q6.at[1], d6.at[1], 4)
-    load[1].wait()
-    c3.wait_recv()
-    add2(q2.at[0], 1, 0)
-    s2t = go(7, q2.at[0], rx.at[0], 2)
-    load[2].wait()
-    c5.wait_recv()
-    add2(q4.at[1], 2, half)
-    s4b = go(8, q4.at[1], ry.at[1], 4)
-    s6t.wait_recv()
-    add3(q4.at[0], 2, 0, d6.at[0])
-    s4t = go(9, q4.at[0], ry.at[0], 4)
-    s6b.wait_recv()
-    add3(q2.at[1], 1, half, d6.at[1])
-    s2b = go(10, q2.at[1], rx.at[1], 2)
-    load[0].wait()
-    c1.wait_recv()
-    s2t.wait_recv()
-    s4t.wait_recv()
-
-    def finish(n, start):
-        def body(r):
-            s = pl.ds(pl.multiple_of(start + r.start, 16), r.size)
-            total = pv[0, s, :].astype(F32) + rc[0, s, :].astype(F32)
-            ov[s, :] = total + rx[n, r, :].astype(F32) + ry[n, r, :].astype(F32)
-
-        rows_loop(half, body)
-
-    finish(0, 0)
-    out0 = pltpu.make_async_copy(ov.at[top], o.at[top], lsem.at[4])
-    out0.start()
-    s2b.wait_recv()
-    s4b.wait_recv()
-    finish(1, half)
-    out1 = pltpu.make_async_copy(ov.at[bot], o.at[bot], lsem.at[5])
-    out1.start()
-    for copy in (c7t, c7b, c3, c5, c1, s6t, s6b, s2t, s4b, s4t, s2b):
-        copy.wait_send()
-    out0.wait()
-    out1.wait()
+    scatter = Scatter(p, ov, scratch)
+    scatter.begin()
+    scatter.load()
+    scatter.middle()
+    scatter.relay()
+    scatter.finish()
+    out = pltpu.make_async_copy(ov, o, osem)
+    out.start()
+    out.wait()
 
 
 def plane_scatter(p, ident):
-    _, rows, width = p.shape
-    half = rows // 2
+    rows, width = p.shape[0] // PLANE, p.shape[1]
     dma = pltpu.SemaphoreType.DMA
-    pair = pltpu.VMEM((2, half, width), BF)
-    scratch = [
-        pltpu.VMEM((4, rows, width), BF),
-        pltpu.VMEM((4, rows, width), BF),
-        pair,
-        pair,
-        pair,
-        pair,
-        pair,
-        pair,
-        pltpu.VMEM((rows, width), F32),
-        dma((6,)),
-        dma((11,)),
-        dma((11,)),
-    ]
+    scratch = [pltpu.VMEM((rows, width), F32), dma] + Scatter.shapes(rows, width, dma)
     out = jax.ShapeDtypeStruct((rows, width), F32)
     return call(scatter_kernel, (p,), out, scratch, ident, 24, 31)
 
@@ -481,30 +525,371 @@
     )
 
 
-def swap(x, k):
-    devices = PLANE * lax.axis_size("z")
-    return lax.ppermute(x, ALL, [(i, i ^ k) for i in range(devices)])
-
-
-def quiet_gather(x):
-    even = jnp.stack([x] + [swap(x, k) for k in (2, 4, 6)])
-    return jnp.stack([even, swap(even, 1)], axis=1).reshape((PLANE,) + x.shape)
-
-
-def quiet_scatter(p):
-    pairs = p.reshape((4, 2) + p.shape[1:])
-    here, there = pairs[:, 0], pairs[:, 1]
-    q = (here.astype(F32) + swap(there, 1).astype(F32)).astype(BF)
-    x, y, xy = swap(q[1], 2), swap(q[2], 4), swap(q[3], 6)
-    return q[0].astype(F32) + x.astype(F32) + y.astype(F32) + xy.astype(F32)
-
-
 def z_gather(x):
     return lax.all_gather(x, "z", axis=0, tiled=True)
 
 
 def z_scatter(g):
     return lax.psum_scatter(g, "z", scatter_dimension=0, tiled=True)
+
+
+def z_peer(m):
+    z = lax.axis_index("z")
+    if m == 1:
+        z = z + 1 - 2 * lax.rem(z, 2)
+    elif m == 2:
+        z = lax.rem(z + 2, 4)
+    else:
+        z = 3 - z
+    return z
+
+
+def greet_more():
+    barrier = pltpu.get_barrier_semaphore()
+    ids = [peer(k) for k in range(1, PLANE)] + [{"z": z_peer(m)} for m in (1, 2, 3)]
+    for where in ids:
+        pl.semaphore_signal(
+            barrier, inc=1, device_id=where, device_id_type=pl.DeviceIdType.MESH
+        )
+    pl.semaphore_wait(barrier, len(ids))
+
+
+class PlaneSum:
+    @staticmethod
+    def shapes(m, c, dma):
+        return [pltpu.VMEM((m, c), BF), dma((4,)), dma((4,))]
+
+    def __init__(self, g, landing, scratch, temps):
+        self.g, self.landing, self.temps = g, landing, temps
+        self.q, self.ssem, self.rsem = scratch
+        self.m, self.c = g.shape[1:]
+        z = lax.axis_index("z")
+        self.inner = (z == 1) | (z == 2)
+        self.outer = (z == 0) | (z == 3)
+
+    def copy(self, src, slot, m):
+        return pltpu.make_async_remote_copy(
+            src_ref=src,
+            dst_ref=self.landing.at[slot],
+            send_sem=self.ssem.at[slot],
+            recv_sem=self.rsem.at[slot],
+            device_id={"z": z_peer(m)},
+            device_id_type=pl.DeviceIdType.MESH,
+        )
+
+    def begin(self):
+        far = self.g.at[z_peer(3)]
+        pl.when(self.outer)(lambda: self.copy(far, 2, 1).start())
+        pl.when(self.inner)(lambda: self.copy(far, 3, 3).start())
+
+    def temp(self, i):
+        return self.temps.at[i, pl.ds(0, self.m), pl.ds(0, self.c)]
+
+    def load(self, src, i):
+        copy = pltpu.make_async_copy(src, self.temp(i), self.tsem.at[i])
+        copy.start()
+        return copy
+
+    def hop(self, tsem):
+        self.tsem = tsem
+        across = self.g.at[z_peer(2)]
+
+        @pl.when(self.outer)
+        def _():
+            self.copy(across, 1, 2).start()
+
+        @pl.when(self.inner)
+        def _():
+            first = self.load(across, 0)
+            self.copy(across, 2, 1).wait_recv()
+            second = self.load(self.landing.at[2], 1)
+            first.wait()
+            second.wait()
+
+            def body(r, n):
+                r = (pl.ds(r, n), pl.ds(0, self.c))
+                total = self.temps[(0,) + r].astype(F32) + self.temps[(1,) + r].astype(F32)
+                self.q[r] = total.astype(BF)
+
+            rows_loop(self.m, body)
+            self.copy(self.q, 1, 2).start()
+
+        self.near = self.copy(self.g.at[z_peer(1)], 0, 1)
+        self.near.start()
+
+    def finish(self, tsem):
+        self.tsem = tsem
+        loads = [self.load(self.g.at[lax.axis_index("z")], 0)]
+        self.near.wait_recv()
+        loads.append(self.load(self.landing.at[0], 1))
+        far = self.copy(self.q, 1, 2)
+        far.wait_recv()
+        loads.append(self.load(self.landing.at[1], 2))
+        pl.when(self.inner)(lambda: self.copy(self.g.at[0], 3, 3).wait_recv())
+        pl.when(self.inner)(lambda: self.load(self.landing.at[3], 3).wait())
+        for copy in loads:
+            copy.wait()
+        far.wait_send()
+        self.near.wait_send()
+        pl.when(self.outer)(lambda: self.copy(self.g.at[0], 2, 1).wait_send())
+        pl.when(self.inner)(lambda: self.copy(self.g.at[0], 3, 3).wait_send())
+
+        def three(r, n):
+            r = (pl.ds(r, n), pl.ds(0, self.c))
+            total = self.temps[(0,) + r].astype(F32) + self.temps[(1,) + r].astype(F32)
+            return r, total + self.temps[(2,) + r].astype(F32)
+
+        def outer(r, n):
+            r, total = three(r, n)
+            self.q[r] = total.astype(BF)
+
+        def inner(r, n):
+            r, total = three(r, n)
+            self.q[r] = (total + self.temps[(3,) + r].astype(F32)).astype(BF)
+
+        pl.when(self.outer)(lambda: rows_loop(self.m, outer))
+        pl.when(self.inner)(lambda: rows_loop(self.m, inner))
+
+
+def deal(src, out, blocks, ssem, rsem):
+    rows = out.shape[0]
+    mine = place(0)
+    copies = []
+    for n, (_, base, width, col) in enumerate(cut([out.shape[1]], blocks)):
+        cols = pl.ds(pl.multiple_of(base + mine * width, 128), width)
+        for k in (6, 7, 2, 3, 4, 5, 1, 0):
+            there = pl.ds(pl.multiple_of(place(k) * rows, 16), rows)
+            piece = src.at[there, pl.ds(col, width)]
+            if k:
+                copies.append(send(piece, out.at[:, cols], ssem.at[n, k], rsem.at[n, k], k))
+            else:
+                copies.append(pltpu.make_async_copy(piece, out.at[:, cols], ssem.at[n, 0]))
+                copies[-1].start()
+    return copies
+
+
+def pipe(body, steps, ins, outs):
+    spec = lambda a: pl.BlockSpec(a[1], a[2])
+    pltpu.emit_pipeline(
+        body, grid=(steps,), in_specs=[spec(a) for a in ins], out_specs=[spec(a) for a in outs]
+    )(*[a[0] for a in ins], *[a[0] for a in outs])
+
+
+def whole(a):
+    return (a, a.shape, lambda i: (0,) * len(a.shape))
+
+
+def some_rows(a, n, pick=lambda i: i):
+    return (a, (n, a.shape[1]), lambda i: (pick(i), 0))
+
+
+def grads_mm(a, b, g):
+    m = g.shape[1]
+
+    def body(a, b, g):
+        g[0] = over_rows(a[...], b[...]).astype(BF)
+
+    pipe(
+        body,
+        g.shape[0],
+        [(a, (a.shape[0], m), lambda i: (0, i)), whole(b)],
+        [(g, (1,) + g.shape[1:], lambda i: (i, 0, 0))],
+    )
+
+
+def rows_mm(a, b, o, n, steps, pick=lambda i: i, transposed=False):
+    def body(a, b, o):
+        o[...] = (times_t if transposed else dot)(a[...], b[...]).astype(BF)
+
+    pipe(body, steps, [some_rows(a, n, pick), whole(b)], [some_rows(o, n, pick)])
+
+
+def back_kernel(factor, nz, *refs):
+    ins, refs = refs[:16], refs[16:]
+    (dy, hid, slope, second, first, mixed, qkv, bias, up, down, outw, qkvw) = ins[:12]
+    (x_mid, scale2, gate1, grad_in) = ins[12:]
+    (e2, e1, y, c_down, c_up, c_qkv, c_out), refs = refs[:7], refs[7:]
+    (du, part, part_y, dat, dmix, dqkv, g_down, g_up, g_qkv, g_out), refs = refs[:10], refs[10:]
+    lands, refs = refs[:4], refs[4:]
+    (xv, temps, temps_out, tsem), refs = refs[:4], refs[4:]
+    sc_a, sc_b, refs = refs[:11], refs[11:22], refs[22:]
+    ga, refs = refs[:3], refs[3:]
+    zs, refs = [refs[3 * i : 3 * i + 3] for i in range(4)], refs[12:]
+    deal_sems = refs
+    rows, width = e2.shape
+    tokens = dy.shape[0]
+    group = bias.shape[1]
+    planes = nz == 4
+    sums = [
+        PlaneSum(g, land, z, t)
+        for g, land, z, t in zip(
+            (g_down, g_up, g_qkv, g_out), lands, zs, (temps, temps, temps, temps_out)
+        )
+    ]
+    s_down, s_up, s_qkv, s_out = sums if planes else [None] * 4
+    begin = lambda s: s and s.begin()
+    hop = lambda s: s and s.hop(tsem)
+    odd, even = (lambda i: 2 * i + 1), (lambda i: 2 * i)
+
+    if planes:
+        greet_more()
+    else:
+        greet(range(1, PLANE))
+    grads_mm(dy, hid, g_down)
+    begin(s_down)
+
+    def du_body(a, b, s, o):
+        o[...] = (dot(a[...], b[...]) * s[...]).astype(BF)
+
+    n = math.gcd(tokens, 256)
+    pipe(
+        du_body,
+        tokens // n,
+        [some_rows(dy, n), whole(down), some_rows(slope, n)],
+        [some_rows(du, n)],
+    )
+    grads_mm(second, du, g_up)
+    rows_mm(du, up, part, rows, 4, odd, True)
+    ra = Scatter(part, e2, sc_a)
+    ra.begin()
+    rows_mm(du, up, part, rows, 4, even, True)
+    hop(s_down)
+    begin(s_up)
+    ra.load()
+    ra.middle()
+    ra.relay()
+    ra.finish()
+
+    def norm_back(r, n):
+        r = pl.ds(r, n)
+        x = x_mid[r, :]
+        inv = lax.rsqrt(jnp.mean(x * x, axis=-1, keepdims=True) + EPS)
+        normed = x * inv
+        d_normed = e2[r, :] * (1.0 + scale2[r, :])
+        slant = jnp.mean(d_normed * normed, axis=-1, keepdims=True)
+        d_mid = grad_in[r, :].astype(F32) + inv * (d_normed - normed * slant)
+        xv[r, :] = (gate1[r, :] * d_mid).astype(BF)
+
+    rows_loop(rows, norm_back)
+    gather = Gather(xv, dat, ga)
+    gather.begin()
+    rows_mm(hid, down, part_y, rows, 8, transposed=True)
+    gather.relay()
+    hop(s_up)
+    gather.finish()
+    ry = Scatter(part_y, y, sc_b)
+    ry.begin()
+    ry.load()
+    rows_mm(dat, outw, dmix, 2 * rows, 4, transposed=True)
+    ry.middle()
+
+    def attend_body(qkv, bias, d_o, out):
+        attend_back_kernel(factor, qkv, bias, d_o, out)
+
+    pipe(
+        attend_body,
+        2,
+        [
+            some_rows(qkv, group),
+            (bias, (1, group, group), lambda i: (i, 0, 0)),
+            some_rows(dmix, group),
+        ],
+        [some_rows(dqkv, group)],
+    )
+    ry.relay()
+    grads_mm(first, dqkv, g_qkv)
+    begin(s_qkv)
+
+    def out_body(a, b, g):
+        g[...] = over_rows(a[...], b[...]).astype(BF).reshape(g.shape)
+
+    step = math.gcd(width, 512)
+    pipe(
+        out_body,
+        width // step,
+        [whole(mixed), (dat, (tokens, step), lambda i: (0, i))],
+        [(g_out, g_out.shape[:2] + (step,), lambda i: (0, 0, i))],
+    )
+    begin(s_out)
+    ry.finish()
+    rows_mm(dqkv, qkvw, part, rows, 4, odd, True)
+    rb = Scatter(part, e1, sc_a)
+    rb.begin()
+    rows_mm(dqkv, qkvw, part, rows, 4, even, True)
+    rb.load()
+    rb.middle()
+    hop(s_qkv)
+    hop(s_out)
+    rb.relay()
+    rb.finish()
+    if planes:
+        dealt = []
+        for s, out, blocks, sems in (
+            (s_down, c_down, 1, deal_sems[:2]),
+            (s_up, c_up, 1, deal_sems[2:4]),
+            (s_qkv, c_qkv, 3, deal_sems[4:6]),
+        ):
+            s.finish(tsem)
+            dealt += deal(s.q, out, blocks, *sems)
+        s_out.finish(tsem)
+        last = pltpu.make_async_copy(s_out.q, c_out, tsem.at[0])
+        last.start()
+        for copy in dealt + [last]:
+            copy.wait()
+
+
+def backward(ins, factor, nz, ident):
+    dy, hid, slope, second, first, mixed, qkv, bias, up, down, outw, qkvw = ins[:12]
+    rows, width = ins[12].shape
+    tokens, wide = hid.shape
+    part = qkvw.shape[1]
+    heads = outw.shape[0]
+    m = width // nz
+    struct = jax.ShapeDtypeStruct
+    own = struct((rows, width), F32)
+    grads = [(nz, m, wide), (nz, m, wide), (nz, m, part), (nz, heads // nz, width)]
+    lands = [(4,) + g[1:] for g in grads]
+    shares = m // PLANE
+    outs = [own] * 3 + [
+        struct((shares, wide * PLANE), BF),
+        struct((shares, wide * PLANE), BF),
+        struct((shares, part * PLANE), BF),
+        struct((heads // nz, width), BF),
+        struct((tokens, wide), BF),
+        struct((tokens, width), BF),
+        struct((tokens, width), BF),
+        struct((tokens, width), BF),
+        struct((tokens, heads), BF),
+        struct((tokens, part), BF),
+    ]
+    outs += [struct(g, BF) for g in grads + lands]
+    dma = pltpu.SemaphoreType.DMA
+    scratch = [
+        pltpu.VMEM((rows, width), BF),
+        pltpu.VMEM((4, m, max(wide, part)), BF),
+        pltpu.VMEM((4,) + grads[3][1:], BF),
+        dma((4,)),
+    ]
+    scratch += Scatter.shapes(rows, width, dma) * 2 + Gather.shapes(dma)
+    for g in grads:
+        scratch += PlaneSum.shapes(g[1], g[2], dma)
+    for blocks in (1, 1, 3):
+        scratch += [dma((blocks, PLANE))] * 2
+    vmem = pl.BlockSpec(memory_space=pltpu.VMEM)
+    anywhere = pl.BlockSpec(memory_space=pl.ANY)
+    return pl.pallas_call(
+        functools.partial(back_kernel, factor, nz),
+        out_shape=outs,
+        in_specs=[anywhere] * 12 + [vmem] * 4,
+        out_specs=[vmem] * 3 + [anywhere] * (len(outs) - 3),
+        scratch_shapes=scratch,
+        compiler_params=pltpu.CompilerParams(
+            collective_id=ident, has_side_effects=True, vmem_limit_bytes=62 * MIB
+        ),
+        cost_estimate=pl.CostEstimate(
+            flops=0, bytes_accessed=int(220 * 3.6e6), transcendentals=0
+        ),
+    )(*ins)
 
 
 def norm_mod(value, shift, scale):
@@ -655,7 +1040,7 @@
     shift1, scale1, gate1, shift2, scale2, gate2 = (pick(i) for i in range(6))
     first_f, first_back = jax.vjp(norm_mod, x_in, shift1, scale1)
     d_branch_own = (gate2 * grad_in).astype(BF)
-    first = plane_gather(after(first_f.astype(BF), qkv_part), 2).reshape(2 * group, width)
+    first = plane_gather(after(first_f.astype(BF), qkv_part), 2)
     up_part, down_part = spread([after(up_weight, first), down_weight], 3)
     outp_w, up_w, down_w = z_gather(outp), z_gather(up_part), z_gather(down_part)
 
@@ -665,53 +1050,33 @@
     mixed = per_group(
         functools.partial(attend_kernel, factor), [qkv], bias, own_cols, group, 5 * cost
     )
-    part = dot(mixed, outp_w).astype(BF).reshape(PLANE, rows, width)
+    part = dot(mixed, outp_w).astype(BF)
     attn = plane_scatter(part, 6)
     x_mid = x_in + gate1 * attn
     second_f, second_back = jax.vjp(norm_mod, x_mid, shift2, scale2)
-    second = plane_gather(second_f.astype(BF), 7).reshape(2 * group, width)
+    second = plane_gather(second_f.astype(BF), 7)
     hidden_pre = dot(second, up_w)
     hidden_f, gelu_back = jax.vjp(jax.nn.gelu, hidden_pre)
     hidden = hidden_f.astype(BF)
 
-    d_branch = plane_gather(after(d_branch_own, hidden), 5).reshape(2 * group, width)
-    d_down = over_rows(d_branch, hidden).astype(BF)
-    d_down, d_branch = lax.optimization_barrier((d_down, d_branch))
-    d_down = z_scatter(d_down)
-    d_pre = gelu_back(dot(d_branch, down_w))[0].astype(BF)
-    d_up = over_rows(second, d_pre).astype(BF)
-    d_up, d_pre = lax.optimization_barrier((d_up, d_pre))
-    d_up = z_scatter(d_up)
-    part = times_t(d_pre, up_w).astype(BF).reshape(PLANE, rows, width)
-    d_second = plane_scatter(part, 9)
+    slope = gelu_back(jnp.ones_like(hidden_pre))[0]
+    d_branch = plane_gather(after(d_branch_own, hidden), 5)
+    ins = [d_branch, hidden, slope, second, first, mixed, qkv, bias, up_w, down_w, outp_w, qkv_w]
+    ins += [x_mid, scale2, gate1, cotangent[0]]
+    outs = backward(ins, factor, nz, 9)
+    d_second, d_first, branch, d_down, d_up, d_qkv_w, d_outp = outs[:7]
+    if nz != 4:
+        flat = lambda g: z_scatter(g.reshape((-1,) + g.shape[2:]))
+        d_down, d_up, d_qkv_w, d_outp = (flat(g) for g in outs[13:17])
+        d_down, d_up = collect([d_down, d_up], 12)
+        (d_qkv_w,) = collect([d_qkv_w], 13, blocks=3)
+    block_out = (x_mid + gate2 * branch).astype(BF)
+    d_gate2 = grad_in * branch
     d_mid_norm, d_shift2, d_scale2 = second_back(d_second)
     d_mid = grad_in + d_mid_norm
-    d_attn = (gate1 * d_mid).astype(BF)
     d_gate1 = d_mid * attn
-    d_attn_all = plane_gather(d_attn, 10).reshape(2 * group, width)
-    d_mixed = times_t(d_attn_all, outp_w).astype(BF)
-    d_qkv = per_group(
-        functools.partial(attend_back_kernel, factor),
-        [qkv, d_mixed],
-        bias,
-        3 * own_cols,
-        group,
-        10 * cost,
-    )
-    d_qkv_w = over_rows(first, d_qkv).astype(BF)
-    d_qkv_w, d_qkv, d_attn_all = lax.optimization_barrier((d_qkv_w, d_qkv, d_attn_all))
-    d_qkv_w = z_scatter(d_qkv_w)
-    d_outp = over_rows(mixed, d_attn_all).astype(BF)
-    d_outp, d_qkv = lax.optimization_barrier((d_outp, d_qkv))
-    d_outp = z_scatter(d_outp)
-    part = times_t(d_qkv, qkv_w).astype(BF).reshape(PLANE, rows, width)
-    d_first = plane_scatter(part, 11)
     d_in_norm, d_shift1, d_scale1 = first_back(d_first)
     grad_tokens = d_mid + d_in_norm
-    part = times_t(after(hidden, d_first), down_w).astype(BF).reshape(PLANE, rows, width)
-    branch = plane_scatter(part, 8)
-    block_out = (x_mid + gate2 * branch).astype(BF)
-    d_gate2 = grad_in * branch
 
     tok_grads = jnp.concatenate([d_shift1, d_scale1, d_gate1, d_shift2, d_scale2, d_gate2], axis=1)
     picker = (seg_own[:, None] == jnp.arange(8, dtype=jnp.int32)[None, :]).astype(F32)
@@ -726,9 +1091,6 @@
     cond_grads = cond_grads.transpose(0, 2, 1, 3).reshape(2 * nz * images, width)
     grad_table = jax.ops.segment_sum(cond_grads, levels, num_segments=noise_table.shape[0])
 
-    d_down = after(d_down, sent)
-    d_up, d_down = collect([d_up, d_down], 12)
-    (d_qkv_w,) = collect([after(d_qkv_w, d_up)], 13, blocks=3)
     d_outp = lax.ppermute(d_outp, ALL, [(b, a) for a, b in move])
     return (
         block_out[None],

time: 741 us -> 643 us (0.87)
  waiting for transfers between devices: 118 us -> 25.9 us
  Pallas kernels: 440 us -> 511 us
  matrix products: 105 us -> 34.9 us
  local copies, waits for them, and re-layouts: 30.8 us -> 20.1 us
    pallas_call x0 -> x1, Pallas kernels: none -> 250 us  [backward(): pl.pallas_call(functools.partial(back_kernel, factor, nz), out_shape=outs...]
    pallas_call x12 -> x6, Pallas kernels: 332 us -> 169 us  [call(): pl.pallas_call(kernel, out_shape=outs, in_specs=[pl.BlockSpec(memory_spac...]
    reduce_scatter x4 -> x0, waiting for transfers between devices: 94.9 us -> none  [z_scatter(): return lax.psum_scatter(g, 'z', scatter_dimension=0, tiled=True)]
    dot_general x8 -> x0, matrix products: 59.1 us -> none  [the longest x4 32.5 us: over_rows(): lax.dot_general(left, right, (((0,), (0,)), ((), ())), preferred_element_...]
    pallas_call x2 -> x1, Pallas kernels: 18.9 us -> 6.77 us  [per_group(): pl.pallas_call(kernel, grid=(bias.shape[0],), out_shape=jax.ShapeDtypeStr...]
    dot_general x5 -> x4, matrix products: 39.5 us -> 28.5 us  [dot(): return jnp.dot(a, b, preferred_element_type=F32)]
    unnamed x125 -> x60, local copies, waits for them, and re-layouts: 26.3 us -> 15.5 us
  transfers between devices with their start and end apart: 11 -> 7, of which waited for: 4 -> 2; matrix products, arithmetic and copies ran while one was open for 11% -> 10% of each run, Pallas kernels for 46% -> 39%
where the time goes in v3:
time: 643 us; the launch traced here: 634 us
  Pallas kernels  511 us (79%)
  matrix products  34.9 us (5%)
  waiting for transfers between devices  25.9 us (4%)
  other arithmetic  23.3 us (4%)
  local copies, waits for them, and re-layouts  20.1 us (3%)
  between operations  14.5 us (2%)
    pallas_call x1, Pallas kernels, backward(): pl.pallas_call(functools.partial(back_kernel, factor, nz), out_shape=outs...  250 us
    pallas_call x6, Pallas kernels, call(): pl.pallas_call(kernel, out_shape=outs, in_specs=[pl.BlockSpec(memory_spac...  169 us
    pallas_call x2, Pallas kernels, small_call(): pl.pallas_call(kernel, out_shape=outs, in_specs=[vmem] * len(ins), out_sp...  85.2 us
    dot_general x4, matrix products, dot(): return jnp.dot(a, b, preferred_element_type=F32)  28.5 us
    all_gather x4, waiting for transfers between devices, z_gather(): return lax.all_gather(x, 'z', axis=0, tiled=True)  24.3 us
    unnamed x60, local copies, waits for them, and re-layouts  15.5 us
  transfers between devices with their start and end apart: 7, of which 2 were waited for; matrix products, arithmetic and copies ran while one was open for 10% of the time, Pallas kernels for 39%

profile of v3, /device:TPU:0, one launch (start us, length us, event | category | flops | bytes accessed | tf_op | source)
XLA Modules:
  0.0 634.4 jit_solution(14717697478583751577)
XLA Ops:
  8.5 14.4 %shard_map.171 = bf16[512,768]{1,0:T(8,128)(2,1)} custom-call(bf16[64,6144]{1,0:T(8,128)(2,1)S(1)} %copy-done.10), custom_call_target="tpu_custom_call" | custom-call | bytes 47185920 | tf_op jit(solution)/shard_map/pallas_call | solution.py:64
  24.1 3.4 gather_fusion
  28.0 34.7 %shard_map.170 = f32[32,8,384]{2,1,0:T(8,128)S(1)} custom-call(f32[32,8,384]{2,1,0:T(8,128)S(1)} %pad.4.x), custom_call_target="tpu_custom_call" | custom-call | bytes 28800000 | tf_op jit(solution)/shard_map/pallas_call | solution.py:460
  64.2 1.7 fusion.11.x
  65.9 36.6 %shard_map.172.refs_4_ = bf16[1536,2048]{1,0:T(8,128)(2,1)S(1)} custom-call(bf16[192,2048]{1,0:T(8,128)(2,1)S(1)} %fusion.11.x), custom_call_target="tpu_custom_call" | custom-call | bytes 108000000 | tf_op jit(solution)/shard_map/pallas_call | solution.py:64
  102.5 2.7 copy-done
  105.2 25.7 %shard_map.176 = (bf16[512,1024]{1,0:T(8,128)(2,1)}, bf16[512,1024]{1,0:T(8,128)(2,1)}) custom-call(bf16[64,8192]{1,0:T(8,128)(2,1)S(1)} %copy-done.8, bf16[64,8192]{1,0:T(8,128)(2,1)S(1)} %copy-done.9), custom_call_target="tpu_custom_call" | custom-call | bytes 125829120 | tf_op jit(solution)/shard_map/pallas_call | solution.py:64
  131.2 1.9 collective-permute-start
  133.4 1.5 collective-permute-done
  136.5 8.9 %convolution_convert_fusion.1.qkv.refs_6_ = bf16[1536,768]{1,0:T(8,128)(2,1)S(1)} fusion(bf16[1536,2048]{1,0:T(8,128)(2,1)} %copy-done, bf16[2048,768]{1,0:T(8,128)(2,1)} %all-gather.5.cloned.1.call-done.refs_11_), kind=kOutput, calls=%fused_computation.15 | convolution fusion | flops 4833017856 | bytes 11796480 | tf_op jit(solution)/shard_map/dot_general | solution.py:901
  145.4 6.8 %shard_map.173.refs_5_ = bf16[1536,256]{1,0:T(8,128)(2,1)S(1)} custom-call(bf16[1536,768]{1,0:T(8,128)(2,1)S(1)} %convolution_convert_fusion.1.qkv.refs_6_, bf16[2,768,768]{2,1,0:T(8,128)(2,1)S(1)} %select_convert_fusion.bias.refs_7_), custom_call_target="tpu_custom_call" | custom-call | flops 6039797760 | tf_op jit(solution)/shard_map/pallas_call | solution.py:955
  152.2 1.6 copy-done.7
  154.7 3.0 convolution_convert_fusion.p
  157.7 31.4 %shard_map.174 = f32[192,2048]{1,0:T(8,128)S(1)} custom-call(bf16[1536,2048]{1,0:T(8,128)(2,1)S(1)} %convolution_convert_fusion.p), custom_call_target="tpu_custom_call" | custom-call | bytes 111600000 | tf_op jit(solution)/shard_map/pallas_call | solution.py:64
  189.1 1.6 multiply_reduce_fusion.1
  190.8 1.9 select_select_fusion
  192.7 30.0 %shard_map.175.refs_3_ = bf16[1536,2048]{1,0:T(8,128)(2,1)S(1)} custom-call(bf16[192,2048]{1,0:T(8,128)(2,1)S(1)} %get-tuple-element.70.x), custom_call_target="tpu_custom_call" | custom-call | bytes 108000000 | tf_op jit(solution)/shard_map/pallas_call | solution.py:64
  222.7 2.6 copy-done.1
  225.3 16.3 %fusion.5 = (f32[1536,1024]{1,0:T(8,128)}, bf16[1536,1024]{1,0:T(8,128)(2,1)}) fusion(bf16[1536,2048]{1,0:T(8,128)(2,1)} %copy-done.1, bf16[2048,1024]{1,0:T(8,128)(2,1)} %all-gather.9.cloned.1.call-done.refs_8_), kind=kOutput, calls=%fused_computation.10 | convolution fusion | flops 6472335360 | bytes 19922944 | tf_op jit(solution)/shard_map/dot_general | solution.py:901
  241.6 30.5 %shard_map.177.refs_0_ = bf16[1536,2048]{1,0:T(8,128)(2,1)S(1)} custom-call(bf16[192,2048]{1,0:T(8,128)(2,1)S(1)} %get-tuple-element.29.x), custom_call_target="tpu_custom_call" | custom-call | bytes 108000000 | tf_op jit(solution)/shard_map/pallas_call | solution.py:64
  272.1 2.6 copy-done.2
  274.8 24.3 %all-gather.11.cloned.1.call-done.refs_9_ = bf16[2048,1024]{1,0:T(8,128)(2,1)} async-done(((bf16[512,1024]{1,0:T(8,128)(2,1)}), bf16[2048,1024]{1,0:T(8,128)(2,1)}) %all-gather.11.cloned.1.call-update) | async-done | bytes 4194320 | tf_op jit(solution)/shard_map/all_gather | solution.py:529
  299.1 250.3 %shard_map.178 = (f32[192,2048]{1,0:T(8,128)}, f32[192,2048]{1,0:T(8,128)}, f32[192,2048]{1,0:T(8,128)}, bf16[64,8192]{1,0:T(8,128)(2,1)}, bf16[64,8192]{1,0:T(8...) custom-call(bf16[1536,2048]{1,0:T(8,128)(2,1)} %copy-done.2, ...), custom_call_target="tpu_custom_call" | custom-call | bytes 792000000 | tf_op jit(solution)/shard_map/pallas_call | solution.py:880
  549.4 1.9 collective-permute-start.2
  551.3 2.4 convert_element_type.60
  553.7 1.5 convert_element_type.62
  559.4 2.3 multiply_reduce_fusion
  561.7 2.7 multiply_dynamic-update-slice_fusion.1
  565.1 3.2 fusion.21
  568.3 50.5 %shard_map.179 = (f32[8,8,384]{2,1,0:T(8,128)S(1)}, f32[32,8,512]{2,1,0:T(8,128)S(1)}) custom-call(f32[32,8,384]{2,1,0:T(8,128)S(1)} %bitcast.63, bf16[2048,384]{1,0:T(8,128)(2,1)S(1)} %copy-done.5), custom_call_target="tpu_custom_call" | custom-call | bytes 72000000 | tf_op jit(solution)/shard_map/pallas_call | solution.py:460
  619.0 4.7 scatter_custom_fusion
  623.7 3.2 fusion.23
  (115 shorter events, 13.1 us)
Async XLA Ops:
  7.2 20.4 %copy-start.4 = (bf16[2048,384]{1,0:T(8,128)(2,1)S(1)}, bf16[2048,384]{1,0:T(8,128)(2,1)}, u32[]{:S(2)}) copy-start(bf16[2048,384]{1,0:T(8,128)(2,1)} %w.1) | copy-start | bytes 4718596
  7.2 129.3 %all-gather.5.cloned.1.call-start = ((), (), s32[]{:S(2)}) async-start(), calls=%async_computation | async-start | bytes 3932160 | tf_op jit(solution)/shard_map/all_gather | solution.py:529
  8.5 14.5 %copy-start.27 = (bf16[64,2048]{1,0:T(8,128)(2,1)S(1)}, bf16[64,2048]{1,0:T(8,128)(2,1)}, u32[]{:S(2)}) copy-start(bf16[64,2048]{1,0:T(8,128)(2,1)} %param.15) | copy-start | bytes 786436
  8.5 15.2 %copy-start.26 = (s32[8,3]{0,1:T(4,128)S(1)}, s32[8,3]{0,1:T(4,128)}, u32[]{:S(2)}) copy-start(s32[8,3]{0,1:T(4,128)} %param.20) | copy-start | bytes 292
  8.5 15.5 %copy-start.24 = (s32[1,768]{1,0:T(1,128)S(1)}, s32[1,768]{1,0:T(1,128)}, u32[]{:S(2)}) copy-start(s32[1,768]{1,0:T(1,128)} %param.19) | copy-start | bytes 9220
  8.5 15.5 %copy-start.25 = (s32[1,768]{1,0:T(1,128)S(1)}, s32[1,768]{1,0:T(1,128)}, u32[]{:S(2)}) copy-start(s32[1,768]{1,0:T(1,128)} %param.18) | copy-start | bytes 9220
  22.9 130.9 %all-gather.7.cloned.1.call-start = ((), (), s32[]{:S(2)}) async-start(), calls=%async_computation.1 | async-start | bytes 1310720 | tf_op jit(solution)/shard_map/all_gather | solution.py:529
  23.0 39.8 %collective-permute-start.1 = (bf16[64,2048]{1,0:T(8,128)(2,1)S(1)}, bf16[64,2048]{1,0:T(8,128)(2,1)S(1)}, u32[]{:S(2)}, u32[]{:S(2)}) collective-permute-start(bf16[64,2048]{1,0:T(8,128)(2,1)S(1)} %copy-done.27), channel_id=1, source_target_pairs={{0,0},{1,8},{2,16},{3,24},{4,1},{5,9},{6,17},{7,25},{8,2},{9,10},{... | collective-permute-start | bytes 786440 | tf_op jit(solution)/shard_map/ppermute | solution.py:1006
  27.9 35.9 %copy-start.14 = (bf16[1,192,2048]{2,1,0:T(8,128)(2,1)S(1)}, bf16[1,192,2048]{2,1,0:T(8,128)(2,1)}, u32[]{:S(2)}) copy-start(bf16[1,192,2048]{2,1,0:T(8,128)(2,1)} %param.11) | copy-start | bytes 2359300
  63.6 161.8 %all-gather.9.cloned.1.call-start = ((), (), s32[]{:S(2)}) async-start(), calls=%async_computation.2 | async-start | bytes 5242880 | tf_op jit(solution)/shard_map/all_gather | solution.py:529
  65.9 39.4 %copy-start.8 = (bf16[64,8192]{1,0:T(8,128)(2,1)S(1)}, bf16[64,8192]{1,0:T(8,128)(2,1)}, u32[]{:S(2)}) copy-start(bf16[64,8192]{1,0:T(8,128)(2,1)} %refs_0_.1) | copy-start | bytes 3145732
  65.9 39.3 %copy-start.9 = (bf16[64,8192]{1,0:T(8,128)(2,1)S(1)}, bf16[64,8192]{1,0:T(8,128)(2,1)}, u32[]{:S(2)}) copy-start(bf16[64,8192]{1,0:T(8,128)(2,1)} %refs_1_.1) | copy-start | bytes 3145732
  102.5 2.7 copy-start
  131.0 168.1 %all-gather.11.cloned.1.call-start = ((), (), s32[]{:S(2)}) async-start(), calls=%async_computation.3 | async-start | bytes 5242880 | tf_op jit(solution)/shard_map/all_gather | solution.py:529
  131.2 3.7 collective-permute-start
  136.5 8.9 %copy-start.3 = (bf16[2,768,768]{2,1,0:T(8,128)(2,1)}, bf16[2,768,768]{2,1,0:T(8,128)(2,1)S(1)}, u32[]{:S(2)}) copy-start(bf16[2,768,768]{2,1,0:T(8,128)(2,1)S(1)} %select_convert_fusion.bias.refs_7_) | copy-start | bytes 7077892
  152.2 1.6 copy-start.7
  157.7 31.4 %copy-start.15 = (bf16[1,192,2048]{2,1,0:T(8,128)(2,1)S(1)}, bf16[1,192,2048]{2,1,0:T(8,128)(2,1)}, u32[]{:S(2)}) copy-start(bf16[1,192,2048]{2,1,0:T(8,128)(2,1)} %param.11) | copy-start | bytes 2359300
  189.1 1.6 copy-start.18
  190.7 1.9 copy-start.11
  222.7 2.7 copy-start.1
  272.1 2.7 copy-start.2
  549.4 4.3 copy-start.22
  549.4 77.5 %collective-permute-start.2 = (bf16[64,2048]{1,0:T(8,128)(2,1)}, bf16[64,2048]{1,0:T(8,128)(2,1)S(1)}, u32[]{:S(2)}, u32[]{:S(2)}) collective-permute-start(bf16[64,2048]{1,0:T(8,128)(2,1)} %get-tuple-element.37), channel_id=1, source_target_pairs={{0,0},{8,1},{16,2},{24,3},{1,4},{9,5},{17,6},{25,7},{2,8},{10,9},{... | collective-permute-start | bytes 786440 | tf_op jit(solution)/shard_map/ppermute | solution.py:1094
  553.6 1.6 copy-start.21
  553.6 3.9 copy-start.20
  555.3 2.2 copy-start.17
  555.3 2.5 copy-start.16
  557.4 1.5 copy-start.12
  557.4 1.9 copy-start.13
  559.4 2.3 copy-start.19
  565.1 3.3 copy-start.5
  (3 other events, 2.8 us)
Sparse Core Ops, SparseCore 0:
  23.1 77.4 all-gather.4
  102.7 27.1 all-gather.6
  131.5 86.8 all-gather.8
  219.7 79.2 all-gather.10

commit v4 on v3

--- a/solution.py
+++ b/solution.py
@@ -544,14 +544,103 @@
     return z
 
 
-def greet_more():
+def inner_plane():
+    z = lax.axis_index("z")
+    return (z == 1) | (z == 2)
+
+
+def outer_plane():
+    z = lax.axis_index("z")
+    return (z == 0) | (z == 3)
+
+
+def remote(src, dst, ssem, rsem, where):
+    return pltpu.make_async_remote_copy(
+        src_ref=src,
+        dst_ref=dst,
+        send_sem=ssem,
+        recv_sem=rsem,
+        device_id=where,
+        device_id_type=pl.DeviceIdType.MESH,
+    )
+
+
+class OutRows:
+    def __init__(self):
+        z, j = lax.axis_index("z"), place(0)
+        me = z * PLANE + j
+        self.slot = lax.rem(me, 4)
+        self.user = self.flat(self.slot * PLANE + lax.div(me, 4))
+        self.owner = self.flat(4 * j + z)
+        self.away, self.home = me != 4 * j + z, me == 4 * j + z
+
+    @staticmethod
+    def flat(d):
+        return flat_id(d)
+
+
+def greet_more(outs):
     barrier = pltpu.get_barrier_semaphore()
-    ids = [peer(k) for k in range(1, PLANE)] + [{"z": z_peer(m)} for m in (1, 2, 3)]
-    for where in ids:
+
+    def signal(where):
         pl.semaphore_signal(
             barrier, inc=1, device_id=where, device_id_type=pl.DeviceIdType.MESH
         )
-    pl.semaphore_wait(barrier, len(ids))
+
+    ids = [peer(k) for k in range(1, PLANE)] + [{"z": z_peer(m)} for m in (1, 2, 3)]
+    for where in ids:
+        signal(where)
+
+    @pl.when(outs.away)
+    def _():
+        signal(outs.user)
+        signal(outs.owner)
+        pl.semaphore_wait(barrier, len(ids) + 2)
+
+    pl.when(outs.home)(lambda: pl.semaphore_wait(barrier, len(ids)))
+
+
+class PlaneCopy:
+    shapes = staticmethod(lambda dma: [dma((4,)), dma((4,))])
+
+    def __init__(self, full, sems):
+        self.full = full
+        self.m = full.shape[0] // 4
+        self.ssem, self.rsem = sems
+
+    def copy(self, slot, t, m):
+        block = self.full.at[pl.ds(pl.multiple_of(t * self.m, self.m), self.m)]
+        return remote(block, block, self.ssem.at[slot], self.rsem.at[slot], {"z": z_peer(m)})
+
+    def begin(self):
+        z = lax.axis_index("z")
+        self.copy(1, z, 2).start()
+        self.copy(0, z, 1).start()
+        pl.when(inner_plane())(lambda: self.copy(2, z, 3).start())
+
+    def relay(self):
+        @pl.when(inner_plane())
+        def _():
+            self.copy(1, z_peer(2), 2).wait_recv()
+            self.copy(3, z_peer(2), 1).start()
+
+    def finish(self):
+        z = lax.axis_index("z")
+        self.copy(0, z_peer(1), 1).wait_recv()
+
+        @pl.when(inner_plane())
+        def _():
+            self.copy(2, z_peer(3), 3).wait_recv()
+            self.copy(2, z, 3).wait_send()
+            self.copy(3, z_peer(2), 1).wait_send()
+
+        @pl.when(outer_plane())
+        def _():
+            self.copy(1, z_peer(2), 2).wait_recv()
+            self.copy(3, z_peer(3), 1).wait_recv()
+
+        self.copy(0, z, 1).wait_send()
+        self.copy(1, z, 2).wait_send()
 
 
 class PlaneSum:
@@ -563,9 +652,7 @@
         self.g, self.landing, self.temps = g, landing, temps
         self.q, self.ssem, self.rsem = scratch
         self.m, self.c = g.shape[1:]
-        z = lax.axis_index("z")
-        self.inner = (z == 1) | (z == 2)
-        self.outer = (z == 0) | (z == 3)
+        self.inner, self.outer = inner_plane(), outer_plane()
 
     def copy(self, src, slot, m):
         return pltpu.make_async_remote_copy(
@@ -704,192 +791,517 @@
     pipe(body, steps, [some_rows(a, n, pick), whole(b)], [some_rows(o, n, pick)])
 
 
-def back_kernel(factor, nz, *refs):
-    ins, refs = refs[:16], refs[16:]
-    (dy, hid, slope, second, first, mixed, qkv, bias, up, down, outw, qkvw) = ins[:12]
-    (x_mid, scale2, gate1, grad_in) = ins[12:]
-    (e2, e1, y, c_down, c_up, c_qkv, c_out), refs = refs[:7], refs[7:]
-    (du, part, part_y, dat, dmix, dqkv, g_down, g_up, g_qkv, g_out), refs = refs[:10], refs[10:]
-    lands, refs = refs[:4], refs[4:]
-    (xv, temps, temps_out, tsem), refs = refs[:4], refs[4:]
-    sc_a, sc_b, refs = refs[:11], refs[11:22], refs[22:]
-    ga, refs = refs[:3], refs[3:]
-    zs, refs = [refs[3 * i : 3 * i + 3] for i in range(4)], refs[12:]
-    deal_sems = refs
-    rows, width = e2.shape
+class Share:
+    @staticmethod
+    def shapes(w, blocks, dma):
+        return [pltpu.VMEM(w, BF), dma, dma((blocks, PLANE)), dma((blocks, PLANE))]
+
+    def __init__(self, w, full, blocks, scratch):
+        self.w, self.full, self.blocks = w, full, blocks
+        self.held, self.lsem, self.ssem, self.rsem = scratch
+        self.load = pltpu.make_async_copy(w, self.held, self.lsem)
+        self.load.start()
+
+    def begin(self):
+        self.load.wait()
+        rows = self.w.shape[0]
+        first = lax.axis_index("z") * (PLANE * rows) + place(0) * rows
+        here = pl.ds(pl.multiple_of(first, rows), rows)
+        self.copies = []
+        for n, (_, base, width, col) in enumerate(cut([self.w.shape[1]], self.blocks)):
+            dst = self.full.at[here, pl.ds(col, width)]
+            for k in (6, 7, 2, 3, 4, 5, 1, 0):
+                cols = pl.ds(pl.multiple_of(base + place(k) * width, 128), width)
+                src = self.held.at[:, cols]
+                if k:
+                    copy = send(src, dst, self.ssem.at[n, k], self.rsem.at[n, k], k)
+                else:
+                    copy = pltpu.make_async_copy(src, dst, self.ssem.at[n, 0])
+                    copy.start()
+                self.copies.append(copy)
+
+    def finish(self):
+        for copy in self.copies:
+            copy.wait()
+
+
+IMAGES = 3
+
+
+def whole_kernel(factor, names, *refs):
+    v = dict(zip(names, refs))
+    get = lambda *keys: [v[key] for key in keys]
+    group_of = lambda prefix: [v[key] for key in names if key.startswith(prefix + ".")]
+    cols, tok, cot, pick, mods = get("cols", "tok", "cot", "pick", "mods")
+    first, second, dy, dat = get("first", "second", "dy", "dat")
+    qkv, mixed, hid, slope = get("qkv", "mixed", "hid", "slope")
+    du, part, part_y, dmix, dqkv = get("du", "part", "part_y", "dmix", "dqkv")
+    xh, xv, xg, va, vb, vd = get("xh", "xv", "xg", "va", "vb", "vd")
+    block_out, grad_tokens = get("block_out", "grad_tokens")
+    acc, img, temps, temps_out, tsem = get("acc", "img", "temps", "temps_out", "tsem")
+    rows, width = tok.shape
     tokens = dy.shape[0]
-    group = bias.shape[1]
-    planes = nz == 4
+    group = 4 * rows
+    z, y, mine = lax.axis_index("z"), lax.axis_index("y"), place(0)
+    odd, even = (lambda i: 2 * i + 1), (lambda i: 2 * i)
+    outs = OutRows()
+
+    qkv_in = Share(v["qkv_w"], v["full_qkv"], 3, group_of("in_qkv"))
+    up_in = Share(v["up_w"], v["full_up"], 1, group_of("in_up"))
+    down_in = Share(v["down_w"], v["full_down"], 1, group_of("in_down"))
+    held, lsem, osems, rsems = group_of("in_out")
+    out_load = pltpu.make_async_copy(v["out_w"], held, lsem)
+    out_load.start()
+    out_block = v["out_w"].shape[0]
+    full_out = v["full_out"]
+    out_at = lambda i: full_out.at[pl.ds(pl.multiple_of(i * out_block, out_block), out_block)]
+    out_in = remote(held, out_at(outs.slot), osems.at[0], rsems.at[0], outs.user)
+    out_local = pltpu.make_async_copy(held, out_at(z), osems.at[0])
+    greet_more(outs)
+
+    ma, mb = get("ma", "mb")
+    sa, ra, sb, rb = group_of("mod_in")
+    sent = []
+    for m in (1, 2, 3):
+        src = cols.at[pl.ds(2 * z_peer(m), 2)]
+        sent.append(remote(src, ma.at[z], sa.at[m], ra.at[m], {"z": z_peer(m)}))
+        sent[-1].start()
+    qkv_in.begin()
+    out_load.wait()
+    pl.when(outs.away)(lambda: out_in.start())
+    pl.when(outs.home)(lambda: out_local.start())
+    ma[z] = cols[pl.ds(2 * z, 2)]
+    for copy in sent:
+        copy.wait()
+    sent = []
+    for k in range(1, PLANE):
+        src = ma.at[:, peer(k)["y"]]
+        sent.append(send(src, mb.at[mine], sb.at[k], rb.at[k], k))
+    mb[mine] = ma[:, y]
+    for copy in sent:
+        copy.wait()
+    each = cols.shape[2]
+    for d in range(4 * PLANE):
+        mods[:, d * each : (d + 1) * each] = mb[d % PLANE, d // PLANE]
+
+    qkv_in.finish()
+    z_qkv = PlaneCopy(v["full_qkv"], group_of("z_qkv"))
+    z_qkv.begin()
+
+    def picker(r):
+        hot = pick[r, 0:128]
+        ones = [hot[:, i : i + 1].astype(F32) for i in range(IMAGES)]
+
+        def mod(which):
+            at = slice(which * width, (which + 1) * width)
+            return sum(ones[i] * mods[i : i + 1, at] for i in range(IMAGES))
+
+        return ones, mod
+
+    def normed_of(x):
+        inv = lax.rsqrt(jnp.mean(x * x, axis=-1, keepdims=True) + EPS)
+        return inv, x * inv
+
+    def norm_grad(inv, normed, d_normed):
+        slant = jnp.mean(d_normed * normed, axis=-1, keepdims=True)
+        return inv * (d_normed - normed * slant)
+
+    def make_first(r, n):
+        r = pl.ds(r, n)
+        _, mod = picker(r)
+        _, normed = normed_of(tok[r, :].astype(F32))
+        xh[r, 0:width] = (normed * (1.0 + mod(1)) + mod(0)).astype(BF)
+        xh[r, width:] = pick[r, :]
+        xg[r, :] = (mod(5) * cot[r, :].astype(F32)).astype(BF)
+
+    rows_loop(rows, make_first)
+    to_first = Gather(xh, first, group_of("ga"))
+    to_first.begin()
+    up_in.begin()
+    pl.when(outs.away)(lambda: out_in.wait())
+    pl.when(outs.home)(lambda: out_local.wait())
+    z_out = PlaneCopy(full_out, group_of("z_out"))
+    z_out.begin()
+    to_first.relay()
+    to_first.finish()
+    down_in.begin()
+    up_in.finish()
+    z_qkv.relay()
+    z_out.relay()
+    z_up = PlaneCopy(v["full_up"], group_of("z_up"))
+    z_up.begin()
+    z_qkv.finish()
+
+    n = math.gcd(tokens, 256)
+
+    def mm_body(a, b, o):
+        o[...] = dot(a[...], b[...]).astype(BF)
+
+    pipe(mm_body, tokens // n, [some_rows(first.at[:, 0:width], n), whole(v["full_qkv"])], [some_rows(qkv, n)])
+    masks = [
+        some_rows(first.at[:, width : width + 128], group),
+        some_rows(first.at[:, width + 128 : width + 256], group),
+    ]
+    pipe(
+        functools.partial(attend_kernel, factor),
+        2,
+        [some_rows(qkv, group)] + masks,
+        [some_rows(mixed, group)],
+    )
+    down_in.finish()
+    z_out.finish()
+    rows_mm(mixed, full_out, part, rows, 4, odd)
+    r_attn = Scatter(part, va, group_of("sc_a") + group_of("sems_1"))
+    r_attn.begin()
+    rows_mm(mixed, full_out, part, rows, 4, even)
+    r_attn.load()
+    r_attn.middle()
+    z_down = PlaneCopy(v["full_down"], group_of("z_down"))
+    z_down.begin()
+    r_attn.relay()
+    r_attn.finish()
+
+    def make_second(r, n):
+        r = pl.ds(r, n)
+        _, mod = picker(r)
+        x = tok[r, :].astype(F32) + mod(2) * va[r, :]
+        vd[r, :] = x
+        xv[r, :] = (normed_of(x)[1] * (1.0 + mod(4)) + mod(3)).astype(BF)
+
+    rows_loop(rows, make_second)
+    z_up.relay()
+    to_second = Gather(xv, second, group_of("gb"))
+    to_second.begin()
+    to_second.relay()
+    to_second.finish()
+    to_dy = Gather(xg, dy, group_of("gc"))
+    to_dy.begin()
+    z_up.finish()
+
+    def up_body(a, b, h, s):
+        u = dot(a[...], b[...])
+        c = math.sqrt(2.0 / math.pi)
+        t = jnp.tanh(c * (u + 0.044715 * (u * u * u)))
+        h[...] = (0.5 * u * (1.0 + t)).astype(BF)
+        inside = c * (1.0 + (3 * 0.044715) * (u * u))
+        s[...] = 0.5 * (1.0 + t) + 0.5 * u * (1.0 - t * t) * inside
+
+    pipe(
+        up_body,
+        tokens // n,
+        [some_rows(second, n), whole(v["full_up"])],
+        [some_rows(hid, n), some_rows(slope, n)],
+    )
+    to_dy.relay()
+    to_dy.finish()
+    z_down.relay()
     sums = [
-        PlaneSum(g, land, z, t)
-        for g, land, z, t in zip(
-            (g_down, g_up, g_qkv, g_out), lands, zs, (temps, temps, temps, temps_out)
-        )
+        PlaneSum(v["g_" + key], v["land_" + key], group_of("s_" + key), t)
+        for key, t in (("down", temps), ("up", temps), ("qkv", temps), ("out", temps_out))
     ]
-    s_down, s_up, s_qkv, s_out = sums if planes else [None] * 4
-    begin = lambda s: s and s.begin()
-    hop = lambda s: s and s.hop(tsem)
-    odd, even = (lambda i: 2 * i + 1), (lambda i: 2 * i)
-
-    if planes:
-        greet_more()
-    else:
-        greet(range(1, PLANE))
-    grads_mm(dy, hid, g_down)
-    begin(s_down)
+    s_down, s_up, s_qkv, s_out = sums
+    grads_mm(dy, hid, v["g_down"])
+    s_down.begin()
+    z_down.finish()
 
     def du_body(a, b, s, o):
         o[...] = (dot(a[...], b[...]) * s[...]).astype(BF)
 
-    n = math.gcd(tokens, 256)
     pipe(
         du_body,
         tokens // n,
-        [some_rows(dy, n), whole(down), some_rows(slope, n)],
+        [some_rows(dy, n), whole(v["full_down"]), some_rows(slope, n)],
         [some_rows(du, n)],
     )
-    grads_mm(second, du, g_up)
-    rows_mm(du, up, part, rows, 4, odd, True)
-    ra = Scatter(part, e2, sc_a)
-    ra.begin()
-    rows_mm(du, up, part, rows, 4, even, True)
-    hop(s_down)
-    begin(s_up)
-    ra.load()
-    ra.middle()
-    ra.relay()
-    ra.finish()
+    rows_mm(du, v["full_up"], part, rows, 4, odd, True)
+    r_e2 = Scatter(part, vb, group_of("sc_a") + group_of("sems_2"))
+    r_e2.begin()
+    rows_mm(du, v["full_up"], part, rows, 4, even, True)
+    s_down.hop(tsem)
+    r_e2.load()
+    r_e2.middle()
+    grads_mm(second, du, v["g_up"])
+    s_up.begin()
+    r_e2.relay()
+    r_e2.finish()
+
+    def clear():
+        acc[...] = jnp.zeros_like(acc)
+
+    def tally(ones, which, value):
+        for i in range(IMAGES):
+            acc[which, i] += ones[i] * value
+
+    def flush(blocks):
+        for q, which in enumerate(blocks):
+            for i in range(IMAGES):
+                at = slice(which * width, (which + 1) * width)
+                img[i : i + 1, at] = jnp.sum(acc[q, i], axis=0, keepdims=True)
+
+    clear()
 
     def norm_back(r, n):
         r = pl.ds(r, n)
-        x = x_mid[r, :]
-        inv = lax.rsqrt(jnp.mean(x * x, axis=-1, keepdims=True) + EPS)
-        normed = x * inv
-        d_normed = e2[r, :] * (1.0 + scale2[r, :])
-        slant = jnp.mean(d_normed * normed, axis=-1, keepdims=True)
-        d_mid = grad_in[r, :].astype(F32) + inv * (d_normed - normed * slant)
-        xv[r, :] = (gate1[r, :] * d_mid).astype(BF)
+        ones, mod = picker(r)
+        inv, normed = normed_of(vd[r, :])
+        e = vb[r, :]
+        d_mid = cot[r, :].astype(F32) + norm_grad(inv, normed, e * (1.0 + mod(4)))
+        grad_tokens[r, :] = d_mid
+        xv[r, :] = (mod(2) * d_mid).astype(BF)
+        tally(ones, 0, e)
+        tally(ones, 1, e * normed)
+        tally(ones, 2, d_mid * va[r, :])
 
     rows_loop(rows, norm_back)
-    gather = Gather(xv, dat, ga)
-    gather.begin()
-    rows_mm(hid, down, part_y, rows, 8, transposed=True)
-    gather.relay()
-    hop(s_up)
-    gather.finish()
-    ry = Scatter(part_y, y, sc_b)
-    ry.begin()
-    ry.load()
-    rows_mm(dat, outw, dmix, 2 * rows, 4, transposed=True)
-    ry.middle()
-
-    def attend_body(qkv, bias, d_o, out):
-        attend_back_kernel(factor, qkv, bias, d_o, out)
-
+    to_dat = Gather(xv, dat, group_of("gd"))
+    to_dat.begin()
+    flush((3, 4, 2))
+    rows_mm(hid, v["full_down"], part_y, rows, 8, transposed=True)
+    to_dat.relay()
+    s_up.hop(tsem)
+    to_dat.finish()
+    r_y = Scatter(part_y, va, group_of("sc_b") + group_of("sems_3"))
+    r_y.begin()
+    r_y.load()
+    rows_mm(dat, full_out, dmix, 2 * rows, 4, transposed=True)
+    r_y.middle()
     pipe(
-        attend_body,
+        functools.partial(attend_back_kernel, factor),
         2,
-        [
-            some_rows(qkv, group),
-            (bias, (1, group, group), lambda i: (i, 0, 0)),
-            some_rows(dmix, group),
-        ],
+        [some_rows(qkv, group)] + masks + [some_rows(dmix, group)],
         [some_rows(dqkv, group)],
     )
-    ry.relay()
-    grads_mm(first, dqkv, g_qkv)
-    begin(s_qkv)
+    r_y.relay()
+    grads_mm(first.at[:, 0:width], dqkv, v["g_qkv"])
+    s_qkv.begin()
 
     def out_body(a, b, g):
         g[...] = over_rows(a[...], b[...]).astype(BF).reshape(g.shape)
 
     step = math.gcd(width, 512)
+    g_out = v["g_out"]
     pipe(
         out_body,
         width // step,
         [whole(mixed), (dat, (tokens, step), lambda i: (0, i))],
         [(g_out, g_out.shape[:2] + (step,), lambda i: (0, 0, i))],
     )
-    begin(s_out)
-    ry.finish()
-    rows_mm(dqkv, qkvw, part, rows, 4, odd, True)
-    rb = Scatter(part, e1, sc_a)
-    rb.begin()
-    rows_mm(dqkv, qkvw, part, rows, 4, even, True)
-    rb.load()
-    rb.middle()
-    hop(s_qkv)
-    hop(s_out)
-    rb.relay()
-    rb.finish()
-    if planes:
-        dealt = []
-        for s, out, blocks, sems in (
-            (s_down, c_down, 1, deal_sems[:2]),
-            (s_up, c_up, 1, deal_sems[2:4]),
-            (s_qkv, c_qkv, 3, deal_sems[4:6]),
-        ):
-            s.finish(tsem)
-            dealt += deal(s.q, out, blocks, *sems)
-        s_out.finish(tsem)
-        last = pltpu.make_async_copy(s_out.q, c_out, tsem.at[0])
-        last.start()
-        for copy in dealt + [last]:
-            copy.wait()
-
-
-def backward(ins, factor, nz, ident):
-    dy, hid, slope, second, first, mixed, qkv, bias, up, down, outw, qkvw = ins[:12]
-    rows, width = ins[12].shape
-    tokens, wide = hid.shape
-    part = qkvw.shape[1]
-    heads = outw.shape[0]
-    m = width // nz
-    struct = jax.ShapeDtypeStruct
-    own = struct((rows, width), F32)
-    grads = [(nz, m, wide), (nz, m, wide), (nz, m, part), (nz, heads // nz, width)]
-    lands = [(4,) + g[1:] for g in grads]
-    shares = m // PLANE
-    outs = [own] * 3 + [
-        struct((shares, wide * PLANE), BF),
-        struct((shares, wide * PLANE), BF),
-        struct((shares, part * PLANE), BF),
-        struct((heads // nz, width), BF),
-        struct((tokens, wide), BF),
-        struct((tokens, width), BF),
-        struct((tokens, width), BF),
-        struct((tokens, width), BF),
-        struct((tokens, heads), BF),
-        struct((tokens, part), BF),
+    s_out.begin()
+    r_y.finish()
+    rows_mm(dqkv, v["full_qkv"], part, rows, 4, odd, True)
+    r_e1 = Scatter(part, vb, group_of("sc_a") + group_of("sems_4"))
+    r_e1.begin()
+    rows_mm(dqkv, v["full_qkv"], part, rows, 4, even, True)
+    r_e1.load()
+    r_e1.middle()
+    s_qkv.hop(tsem)
+    s_out.hop(tsem)
+    r_e1.relay()
+    r_e1.finish()
+    clear()
+
+    def last_norm(r, n):
+        r = pl.ds(r, n)
+        ones, mod = picker(r)
+        inv, normed = normed_of(tok[r, :].astype(F32))
+        e, out = vb[r, :], va[r, :]
+        grad_tokens[r, :] += norm_grad(inv, normed, e * (1.0 + mod(1)))
+        block_out[r, :] = (vd[r, :] + mod(5) * out).astype(BF)
+        tally(ones, 0, e)
+        tally(ones, 1, e * normed)
+        tally(ones, 2, cot[r, :].astype(F32) * out)
+
+    rows_loop(rows, last_norm)
+    flush((0, 1, 5))
+
+    pa, ga, gs, gb, pc, pd, pe, ts = get("pa", "ga_", "gs", "gb_", "pc", "pd", "pe", "ts")
+    w, t_all, dm = get("mod_w", "t_all", "dm")
+    sems = group_of("mod_out")
+    load_w = pltpu.make_async_copy(v["mod_w_in"], w, sems[10].at[0])
+    load_w.start()
+    for d in range(4 * PLANE):
+        pa[d % PLANE, d // PLANE] = img[:, d * each : (d + 1) * each]
+    plane_sent = lambda src, dst, s, r: [
+        send(src(k), dst, s.at[k], r.at[k], k) for k in range(1, PLANE)
     ]
-    outs += [struct(g, BF) for g in grads + lands]
-    dma = pltpu.SemaphoreType.DMA
-    scratch = [
-        pltpu.VMEM((rows, width), BF),
-        pltpu.VMEM((4, m, max(wide, part)), BF),
-        pltpu.VMEM((4,) + grads[3][1:], BF),
-        dma((4,)),
-    ]
-    scratch += Scatter.shapes(rows, width, dma) * 2 + Gather.shapes(dma)
-    for g in grads:
-        scratch += PlaneSum.shapes(g[1], g[2], dma)
-    for blocks in (1, 1, 3):
-        scratch += [dma((blocks, PLANE))] * 2
+    sent = plane_sent(lambda k: pa.at[place(k)], ga.at[mine], sems[0], sems[1])
+    ga[mine] = pa[mine]
+    dealt = []
+    deal_sems = group_of("deal")
+
+    def settle(s, out, blocks, sems):
+        s.finish(tsem)
+        dealt.extend(deal(s.q, out, blocks, *sems))
+
+    settle(s_down, v["c_down"], 1, deal_sems[:2])
+    for copy in sent:
+        copy.wait()
+    for g in range(2):
+        gs[:, g] = ga[4 * g] + ga[4 * g + 1] + ga[4 * g + 2] + ga[4 * g + 3]
+    sent = []
+    for m in (1, 2, 3):
+        copy = remote(
+            gs.at[z_peer(m)], gb.at[z], sems[2].at[m], sems[3].at[m], {"z": z_peer(m)}
+        )
+        copy.start()
+        sent.append(copy)
+    gb[z] = gs[z]
+    settle(s_up, v["c_up"], 1, deal_sems[2:4])
+    s_out.finish(tsem)
+    back = remote(s_out.q, v["c_out"], tsem.at[4], tsem.at[5], outs.owner)
+    back_local = pltpu.make_async_copy(s_out.q, v["c_out"], tsem.at[4])
+    pl.when(outs.away)(lambda: back.start())
+    pl.when(outs.home)(lambda: back_local.start())
+    for copy in sent:
+        copy.wait()
+    load_w.wait()
+    for t in range(4):
+        for g in range(2):
+            dm[2 * t + g] = gb[t, g]
+    own = dm[...].reshape(8 * 8, each)
+    high = own.astype(BF)
+    low = (own - high.astype(F32)).astype(BF)
+    slice_of = width // PLANE
+    for k in range(PLANE):
+        piece = w[k * slice_of : (k + 1) * slice_of, :]
+        pc[k] = times_t(high, piece) + times_t(low, piece)
+    sent = plane_sent(lambda k: pc.at[place(k)], pd.at[mine], sems[4], sems[5])
+    pd[mine] = pc[mine]
+    settle(s_qkv, v["c_qkv"], 3, deal_sems[4:6])
+    for copy in sent:
+        copy.wait()
+    total = pd[0]
+    for k in range(1, PLANE):
+        total = total + pd[k]
+    pe[z] = total
+    sent = []
+    for m in (1, 2, 3):
+        copy = remote(pe.at[z], pe.at[z], sems[6].at[m], sems[7].at[m], {"z": z_peer(m)})
+        copy.start()
+        sent.append(copy)
+    for copy in sent:
+        copy.wait()
+    ts[...] = pe[0] + pe[1] + pe[2] + pe[3]
+    sent = plane_sent(lambda k: ts, t_all.at[mine], sems[8], sems[9])
+    t_all[mine] = ts[...]
+    for copy in sent:
+        copy.wait()
+    for copy in dealt:
+        copy.wait()
+    pl.when(outs.away)(lambda: back.wait())
+    pl.when(outs.home)(lambda: back_local.wait())
+
+
+def whole_block(cols, tok, cot, pick, mod_w, qkv_w, out_w, up_w, down_w, factor, ident):
+    rows, width = tok.shape
+    nz, tokens = 4, PLANE * rows
+    share = qkv_w.shape[0]
+    m = share * PLANE
+    wide, part, heads = up_w.shape[1] // PLANE, qkv_w.shape[1] // PLANE, nz * out_w.shape[0]
+    each = cols.shape[2]
+    struct, vm, dma = jax.ShapeDtypeStruct, pltpu.VMEM, pltpu.SemaphoreType.DMA
     vmem = pl.BlockSpec(memory_space=pltpu.VMEM)
     anywhere = pl.BlockSpec(memory_space=pl.ANY)
-    return pl.pallas_call(
-        functools.partial(back_kernel, factor, nz),
-        out_shape=outs,
-        in_specs=[anywhere] * 12 + [vmem] * 4,
-        out_specs=[vmem] * 3 + [anywhere] * (len(outs) - 3),
-        scratch_shapes=scratch,
+    ins = dict(cols=cols, tok=tok, cot=cot, pick=pick)
+    far_ins = dict(mod_w_in=mod_w, qkv_w=qkv_w, out_w=out_w, up_w=up_w, down_w=down_w)
+    near = dict(
+        block_out=struct((rows, width), BF),
+        grad_tokens=struct((rows, width), F32),
+        dm=struct(cols.shape, F32),
+        t_all=struct((PLANE, 64, width // PLANE), F32),
+    )
+    far = dict(
+        c_down=struct((share, wide * PLANE), BF),
+        c_up=struct((share, wide * PLANE), BF),
+        c_qkv=struct((share, part * PLANE), BF),
+        c_out=struct((heads // nz, width), BF),
+        full_qkv=struct((nz * m, part), BF),
+        full_out=struct((heads, width), BF),
+        full_up=struct((nz * m, wide), BF),
+        full_down=struct((nz * m, wide), BF),
+        first=struct((tokens, width + 256), BF),
+        second=struct((tokens, width), BF),
+        dy=struct((tokens, width), BF),
+        dat=struct((tokens, width), BF),
+        qkv=struct((tokens, part), BF),
+        mixed=struct((tokens, heads), BF),
+        hid=struct((tokens, wide), BF),
+        slope=struct((tokens, wide), F32),
+        du=struct((tokens, wide), BF),
+        part=struct((tokens, width), BF),
+        part_y=struct((tokens, width), BF),
+        dmix=struct((tokens, heads), BF),
+        dqkv=struct((tokens, part), BF),
+    )
+    shapes = dict(
+        down=(nz, m, wide), up=(nz, m, wide), qkv=(nz, m, part), out=(nz, heads // nz, width)
+    )
+    for key, shape in shapes.items():
+        far["g_" + key] = struct(shape, BF)
+        far["land_" + key] = struct(shape, BF)
+    own = vm((rows, width), F32)
+    scratch = dict(
+        mods=vm((8, 6 * width), F32),
+        img=vm((8, 6 * width), F32),
+        ma=vm((nz, 2, 8, each), F32),
+        mb=vm((PLANE, nz, 8, each), F32),
+        xh=vm((rows, width + 256), BF),
+        xv=vm((rows, width), BF),
+        xg=vm((rows, width), BF),
+        va=own,
+        vb=own,
+        vd=own,
+        acc=vm((3, IMAGES, 16, width), F32),
+        temps=vm((4, m, max(wide, part)), BF),
+        temps_out=vm((4,) + shapes["out"][1:], BF),
+        tsem=dma((6,)),
+        mod_w=vm(mod_w.shape, BF),
+        pa=vm((PLANE, nz, 8, each), F32),
+        ga_=vm((PLANE, nz, 8, each), F32),
+        gs=vm((nz, 2, 8, each), F32),
+        gb_=vm((nz, 2, 8, each), F32),
+        pc=vm((PLANE, 64, width // PLANE), F32),
+        pd=vm((PLANE, 64, width // PLANE), F32),
+        pe=vm((nz, 64, width // PLANE), F32),
+        ts=vm((64, width // PLANE), F32),
+    )
+
+    def add(prefix, items):
+        for i, item in enumerate(items):
+            scratch[prefix + "." + str(i)] = item
+
+    add("in_qkv", Share.shapes(qkv_w.shape, 3, dma))
+    add("in_up", Share.shapes(up_w.shape, 1, dma))
+    add("in_down", Share.shapes(down_w.shape, 1, dma))
+    add("in_out", [vm(out_w.shape, BF), dma, dma((1,)), dma((1,))])
+    add("mod_in", [dma((4,)), dma((4,)), dma((PLANE,)), dma((PLANE,))])
+    add("mod_out", [dma((PLANE,))] * 10 + [dma((1,))])
+    for key in ("ga", "gb", "gc", "gd"):
+        add(key, Gather.shapes(dma))
+    sc = Scatter.shapes(rows, width, dma)
+    add("sc_a", sc[:8])
+    add("sc_b", sc[:8])
+    for i in range(1, 5):
+        add("sems_" + str(i), sc[8:])
+    for key, shape in shapes.items():
+        add("z_" + key, PlaneCopy.shapes(dma))
+        add("s_" + key, PlaneSum.shapes(shape[1], shape[2], dma))
+    add("deal", [dma((b, PLANE)) for b in (1, 1, 1, 1, 3, 3)])
+    names = list(ins) + list(far_ins) + list(near) + list(far) + list(scratch)
+    outs = pl.pallas_call(
+        functools.partial(whole_kernel, factor, names),
+        out_shape=list(near.values()) + list(far.values()),
+        in_specs=[vmem] * len(ins) + [anywhere] * len(far_ins),
+        out_specs=[vmem] * len(near) + [anywhere] * len(far),
+        scratch_shapes=list(scratch.values()),
         compiler_params=pltpu.CompilerParams(
             collective_id=ident, has_side_effects=True, vmem_limit_bytes=62 * MIB
         ),
         cost_estimate=pl.CostEstimate(
-            flops=0, bytes_accessed=int(220 * 3.6e6), transcendentals=0
+            flops=0, bytes_accessed=int(450 * 3.6e6), transcendentals=0
         ),
-    )(*ins)
+    )(*ins.values(), *far_ins.values())
+    return dict(zip(list(near) + list(far), outs))
 
 
 def norm_mod(value, shift, scale):
@@ -909,8 +1321,14 @@
     return lax.dot_general(left, right, (((1,), (1,)), ((), ())), preferred_element_type=F32)
 
 
-def softmax_rows(q, k, bias, factor):
-    scores = times_t(q, k) * factor + bias.astype(F32)
+def allowed_pairs(seg, key, r):
+    same = times_t(seg[r, :], key[...]) > 0.5
+    rows = lax.broadcasted_iota(jnp.int32, same.shape, 0) + r.start
+    return same | (rows == lax.broadcasted_iota(jnp.int32, same.shape, 1))
+
+
+def softmax_rows(q, k, allowed, factor):
+    scores = jnp.where(allowed, times_t(q, k) * factor, NEG)
     expo = jnp.exp(scores - jnp.max(scores, axis=-1, keepdims=True))
     return expo / jnp.sum(expo, axis=-1, keepdims=True)
 
@@ -920,17 +1338,18 @@
     return [slice(i, i + step) for i in range(0, count, step)]
 
 
-def attend_kernel(factor, qkv, bias, o):
+def attend_kernel(factor, qkv, seg, key, o):
     n = o.shape[1]
-    for c in range(0, n, HEAD_DIM):
-        k = qkv[:, n + c : n + c + HEAD_DIM]
-        v = qkv[:, 2 * n + c : 2 * n + c + HEAD_DIM]
-        for r in row_blocks(o.shape[0]):
-            prob = softmax_rows(qkv[r, c : c + HEAD_DIM], k, bias[0, r, :], factor)
+    for r in row_blocks(o.shape[0]):
+        allowed = allowed_pairs(seg, key, r)
+        for c in range(0, n, HEAD_DIM):
+            k = qkv[:, n + c : n + c + HEAD_DIM]
+            v = qkv[:, 2 * n + c : 2 * n + c + HEAD_DIM]
+            prob = softmax_rows(qkv[r, c : c + HEAD_DIM], k, allowed, factor)
             o[r, c : c + HEAD_DIM] = dot(prob.astype(BF), v).astype(BF)
 
 
-def attend_back_kernel(factor, qkv, bias, d_o, d_qkv):
+def attend_back_kernel(factor, qkv, seg, key, d_o, d_qkv):
     n = d_o.shape[1]
     for c in range(0, n, HEAD_DIM):
         k = qkv[:, n + c : n + c + HEAD_DIM]
@@ -939,7 +1358,7 @@
         for r in row_blocks(d_o.shape[0]):
             q = qkv[r, c : c + HEAD_DIM]
             out = d_o[r, c : c + HEAD_DIM]
-            prob = softmax_rows(q, k, bias[0, r, :], factor)
+            prob = softmax_rows(q, k, allowed_pairs(seg, key, r), factor)
             d_prob = times_t(out, v)
             delta = jnp.sum(prob * d_prob, axis=-1, keepdims=True)
             d_scores = (prob * (d_prob - delta)).astype(BF)
@@ -950,18 +1369,20 @@
         d_qkv[:, 2 * n + c : 2 * n + c + HEAD_DIM] = dv.astype(BF)
 
 
-def per_group(kernel, ins, bias, columns, group, flops):
+def per_group(kernel, qkv, first, d_o, columns, group, flops):
+    last = first.shape[1] // 128
     block = lambda c: pl.BlockSpec((group, c), lambda i: (i, 0))
+    mask = lambda c: pl.BlockSpec((group, 128), lambda i: (i, c))
     return pl.pallas_call(
         kernel,
-        grid=(bias.shape[0],),
-        out_shape=jax.ShapeDtypeStruct((bias.shape[0] * group, columns), BF),
-        in_specs=[block(ins[0].shape[1]), pl.BlockSpec((1, group, group), lambda i: (i, 0, 0))]
-        + [block(a.shape[1]) for a in ins[1:]],
+        grid=(qkv.shape[0] // group,),
+        out_shape=jax.ShapeDtypeStruct((qkv.shape[0], columns), BF),
+        in_specs=[block(qkv.shape[1]), mask(last - 2), mask(last - 1)]
+        + [block(a.shape[1]) for a in d_o],
         out_specs=block(columns),
         compiler_params=pltpu.CompilerParams(vmem_limit_bytes=48 * MIB),
         cost_estimate=pl.CostEstimate(flops=flops, bytes_accessed=0, transcendentals=0),
-    )(ins[0], bias, *ins[1:])
+    )(qkv, first, first, *d_o)
 
 
 def after(value, *others):
@@ -984,114 +1405,28 @@
     rows, width = tokens.shape[1:]
     images = noise_level.shape[1]
     nz = lax.axis_size("z")
-    blks = lax.axis_size("blk")
-    z, y, blk = (lax.axis_index(a) for a in ALL)
-    devices = nz * PLANE
-    group = rows * blks
-    local = HEADS // PLANE
+    blk = lax.axis_index("blk")
+    groups = 2 * nz
     factor = 1.0 / math.sqrt(HEAD_DIM)
-
     levels = noise_level.reshape(-1)
     cond = jnp.take(noise_table, levels, axis=0)
-    cols = dot(cond, mod_weight).reshape(2 * nz, 1, images, -1)
-    sent = jnp.broadcast_to(cols, (2 * nz, blks) + cols.shape[2:])
-    sent = jnp.pad(sent.reshape((devices,) + cols.shape[2:]), ((0, 0), (0, 8 - images), (0, 0)))
-
-    mods = exchange(sent, 14)[:, :images]
-
-    (qkv_part,) = spread([after(qkv_weight, mods)], 1, blocks=3)
-    mods = mods.transpose(1, 0, 2).reshape(images, 6, width)
-    qkv_w = z_gather(qkv_part)
-    move = [(nz * k + i, i * PLANE + k) for k in range(PLANE) for i in range(nz)]
-    outp = lax.ppermute(after(out_weight, qkv_part), ALL, move)
-
-    both = jnp.concatenate([segment, key_valid], axis=0)
-    other = lax.ppermute(both, "y", [(0, 1), (1, 0)])
-    order = lambda a: jnp.stack(
-        [
-            lax.dynamic_index_in_dim(
-                a.reshape(2, blks, rows),
-                (lax.div(blk, 2) ^ (k >> 1)) * 2 + (lax.rem(blk, 2) ^ (k & 1)),
-                1,
-                keepdims=False,
-            )
-            for k in range(blks)
-        ],
-        axis=1,
-    ).reshape(2, group)
-    both, other = order(both), order(other)
-    seg = jnp.stack([both[0], other[0]])
-    valid = jnp.stack([both[1], other[1]])
-    seg_own = seg[0, :rows]
-    eye = jnp.arange(group)[:, None] == jnp.arange(group)[None, :]
-    allowed = (seg[:, :, None] == seg[:, None, :]) & ((valid[:, None, :] == 1) | eye[None])
-    bias = jnp.where(allowed, 0.0, NEG).astype(BF)
-
-    def pick(which):
-        m = mods[:, which]
-        s = seg_own[:, None]
-        out = m[images - 1][None]
-        for i in range(images - 2, -1, -1):
-            out = jnp.where(s == i, m[i][None], out)
-        return out
-
-    x_in = tokens[0].astype(F32)
-    grad_in = cotangent[0].astype(F32)
-    shift1, scale1, gate1, shift2, scale2, gate2 = (pick(i) for i in range(6))
-    first_f, first_back = jax.vjp(norm_mod, x_in, shift1, scale1)
-    d_branch_own = (gate2 * grad_in).astype(BF)
-    first = plane_gather(after(first_f.astype(BF), qkv_part), 2)
-    up_part, down_part = spread([after(up_weight, first), down_weight], 3)
-    outp_w, up_w, down_w = z_gather(outp), z_gather(up_part), z_gather(down_part)
-
-    qkv = dot(first, qkv_w).astype(BF)
-    own_cols = local * HEAD_DIM
-    cost = 4 * 2 * group * group * own_cols
-    mixed = per_group(
-        functools.partial(attend_kernel, factor), [qkv], bias, own_cols, group, 5 * cost
-    )
-    part = dot(mixed, outp_w).astype(BF)
-    attn = plane_scatter(part, 6)
-    x_mid = x_in + gate1 * attn
-    second_f, second_back = jax.vjp(norm_mod, x_mid, shift2, scale2)
-    second = plane_gather(second_f.astype(BF), 7)
-    hidden_pre = dot(second, up_w)
-    hidden_f, gelu_back = jax.vjp(jax.nn.gelu, hidden_pre)
-    hidden = hidden_f.astype(BF)
-
-    slope = gelu_back(jnp.ones_like(hidden_pre))[0]
-    d_branch = plane_gather(after(d_branch_own, hidden), 5)
-    ins = [d_branch, hidden, slope, second, first, mixed, qkv, bias, up_w, down_w, outp_w, qkv_w]
-    ins += [x_mid, scale2, gate1, cotangent[0]]
-    outs = backward(ins, factor, nz, 9)
-    d_second, d_first, branch, d_down, d_up, d_qkv_w, d_outp = outs[:7]
-    if nz != 4:
-        flat = lambda g: z_scatter(g.reshape((-1,) + g.shape[2:]))
-        d_down, d_up, d_qkv_w, d_outp = (flat(g) for g in outs[13:17])
-        d_down, d_up = collect([d_down, d_up], 12)
-        (d_qkv_w,) = collect([d_qkv_w], 13, blocks=3)
-    block_out = (x_mid + gate2 * branch).astype(BF)
-    d_gate2 = grad_in * branch
-    d_mid_norm, d_shift2, d_scale2 = second_back(d_second)
-    d_mid = grad_in + d_mid_norm
-    d_gate1 = d_mid * attn
-    d_in_norm, d_shift1, d_scale1 = first_back(d_first)
-    grad_tokens = d_mid + d_in_norm
-
-    tok_grads = jnp.concatenate([d_shift1, d_scale1, d_gate1, d_shift2, d_scale2, d_gate2], axis=1)
-    picker = (seg_own[:, None] == jnp.arange(8, dtype=jnp.int32)[None, :]).astype(F32)
-    image_grads = lax.dot_general(picker, tok_grads, (((0,), (0,)), ((), ())), precision=HIGH)
-    sent = image_grads.reshape(8, devices, -1).transpose(1, 0, 2)
-    mod_grads, cond_grads = mods_back(sent, mod_weight, 15)
-    mod_grads = mod_grads[:, :images].reshape(2 * nz * images, -1)
+    cols = dot(cond, mod_weight).reshape(groups, images, -1)
+    cols = jnp.pad(cols, ((0, 0), (0, 8 - images), (0, 0)))
+
+    own = lambda a: lax.dynamic_slice_in_dim(a[0], blk * rows, rows, 0)[:, None]
+    lane = jnp.arange(256, dtype=jnp.int32)[None, :]
+    hot = (own(segment) == lane % 128) & ((lane < 128) | (own(key_valid) == 1))
+    pick = hot.astype(BF)
+
+    args = (tokens[0], cotangent[0], pick, mod_weight)
+    weights = (qkv_weight, out_weight, up_weight, down_weight)
+    run = on_four_planes if nz == 4 else on_any_planes
+    out = run(cols, *args, *weights, factor, images)
+    block_out, grad_tokens, mod_grads, cond_grads, d_qkv_w, d_outp, d_up, d_down = out
     grad_mod = lax.dot_general(
         cond.astype(F32), mod_grads, (((0,), (0,)), ((), ())), precision=HIGH
     )
-    cond_grads = cond_grads.reshape(2 * nz, 4, 8, width // 4)[:, :, :images]
-    cond_grads = cond_grads.transpose(0, 2, 1, 3).reshape(2 * nz * images, width)
     grad_table = jax.ops.segment_sum(cond_grads, levels, num_segments=noise_table.shape[0])
-
-    d_outp = lax.ppermute(d_outp, ALL, [(b, a) for a, b in move])
     return (
         block_out[None],
         grad_tokens[None],
@@ -1102,6 +1437,125 @@
         d_up.astype(F32),
         d_down.astype(F32),
     )
+
+
+def on_four_planes(
+    cols, tok, cot, pick, mod_weight, qkv_weight, out_weight, up_weight, down_weight, factor, images
+):
+    out = whole_block(
+        cols,
+        tok,
+        cot,
+        pick,
+        mod_weight,
+        qkv_weight,
+        out_weight,
+        up_weight,
+        down_weight,
+        factor,
+        1,
+    )
+    count, width = cols.shape[0] * images, tok.shape[1]
+    mod_grads = out["dm"][:, :images].reshape(count, -1)
+    cond_grads = out["t_all"].reshape(PLANE, -1, 8, width // PLANE)[:, :, :images]
+    cond_grads = cond_grads.transpose(1, 2, 0, 3).reshape(count, width)
+    return (
+        out["block_out"],
+        out["grad_tokens"],
+        mod_grads,
+        cond_grads,
+        out["c_qkv"],
+        out["c_out"],
+        out["c_up"],
+        out["c_down"],
+    )
+
+
+def on_any_planes(
+    cols, tok, cot, pick, mod_weight, qkv_weight, out_weight, up_weight, down_weight, factor, images
+):
+    rows, width = tok.shape
+    nz, blks = lax.axis_size("z"), lax.axis_size("blk")
+    devices = nz * PLANE
+    group = rows * blks
+    own_cols = HEADS // PLANE * HEAD_DIM
+    sent = jnp.broadcast_to(cols[:, None], (2 * nz, blks) + cols.shape[1:])
+    mods = exchange(sent.reshape((devices,) + cols.shape[1:]), 14)[:, :images]
+    mods = mods.transpose(1, 0, 2).reshape(images, 6, width)
+
+    (qkv_part,) = spread([after(qkv_weight, mods)], 1, blocks=3)
+    qkv_w = z_gather(qkv_part)
+    move = [(nz * k + i, i * PLANE + k) for k in range(PLANE) for i in range(nz)]
+    outp = lax.ppermute(after(out_weight, qkv_part), ALL, move)
+
+    picker = pick[:, :images].astype(F32)
+    shift1, scale1, gate1, shift2, scale2, gate2 = (
+        jnp.dot(picker, mods[:, i], precision=HIGH) for i in range(6)
+    )
+    x_in, grad_in = tok.astype(F32), cot.astype(F32)
+    first_f, first_back = jax.vjp(norm_mod, x_in, shift1, scale1)
+    first = jnp.concatenate([first_f.astype(BF), pick], axis=1)
+    first_all = plane_gather(after(first, qkv_part), 2)
+    first = first_all[:, :width]
+    up_part, down_part = spread([after(up_weight, first), down_weight], 3)
+    outp_w, up_w, down_w = z_gather(outp), z_gather(up_part), z_gather(down_part)
+
+    qkv = dot(first, qkv_w).astype(BF)
+    cost = 4 * 2 * group * group * own_cols
+    mixed = per_group(
+        functools.partial(attend_kernel, factor), qkv, first_all, [], own_cols, group, 5 * cost
+    )
+    attn = plane_scatter(dot(mixed, outp_w).astype(BF), 6)
+    x_mid = x_in + gate1 * attn
+    second_f, second_back = jax.vjp(norm_mod, x_mid, shift2, scale2)
+    second = plane_gather(second_f.astype(BF), 7)
+    hidden_f, gelu_back = jax.vjp(jax.nn.gelu, dot(second, up_w))
+    hidden = hidden_f.astype(BF)
+
+    d_branch = plane_gather(after((gate2 * grad_in).astype(BF), hidden), 5)
+    d_down = z_scatter(over_rows(d_branch, hidden).astype(BF))
+    d_pre = gelu_back(dot(d_branch, down_w))[0].astype(BF)
+    d_up = z_scatter(over_rows(second, d_pre).astype(BF))
+    d_second = plane_scatter(times_t(d_pre, up_w).astype(BF), 9)
+    d_mid_norm, d_shift2, d_scale2 = second_back(d_second)
+    d_mid = grad_in + d_mid_norm
+    d_gate1 = d_mid * attn
+    d_attn = plane_gather((gate1 * d_mid).astype(BF), 10)
+    d_mixed = times_t(d_attn, outp_w).astype(BF)
+    d_qkv = per_group(
+        functools.partial(attend_back_kernel, factor),
+        qkv,
+        first_all,
+        [d_mixed],
+        3 * own_cols,
+        group,
+        10 * cost,
+    )
+    d_qkv_w = z_scatter(over_rows(first, d_qkv).astype(BF))
+    d_outp = z_scatter(over_rows(mixed, d_attn).astype(BF))
+    d_first = plane_scatter(times_t(d_qkv, qkv_w).astype(BF), 11)
+    d_in_norm, d_shift1, d_scale1 = first_back(d_first)
+    part = times_t(after(hidden, d_first), down_w).astype(BF)
+    branch = plane_scatter(part, 8)
+    block_out = (x_mid + gate2 * branch).astype(BF)
+    d_gate2 = grad_in * branch
+
+    tok_grads = jnp.concatenate([d_shift1, d_scale1, d_gate1, d_shift2, d_scale2, d_gate2], axis=1)
+    image_grads = lax.dot_general(
+        pick[:, :8].astype(F32), tok_grads, (((0,), (0,)), ((), ())), precision=HIGH
+    )
+    sent = image_grads.reshape(8, devices, -1).transpose(1, 0, 2)
+    mod_grads, cond_grads = mods_back(sent, mod_weight, 15)
+    count = 2 * nz * images
+    mod_grads = mod_grads[:, :images].reshape(count, -1)
+    cond_grads = cond_grads.reshape(2 * nz, 4, 8, width // 4)[:, :, :images]
+    cond_grads = cond_grads.transpose(0, 2, 1, 3).reshape(count, width)
+
+    d_up, d_down = collect([after(d_up, sent), d_down], 12)
+    (d_qkv_w,) = collect([after(d_qkv_w, d_up)], 13, blocks=3)
+    d_outp = lax.ppermute(d_outp, ALL, [(b, a) for a, b in move])
+    grads = (d_qkv_w, d_outp, d_up, d_down)
+    return (block_out, d_mid + d_in_norm, mod_grads, cond_grads) + grads
 
 
 def solution(mesh):

time: 643 us -> 570 us (0.89)
  matrix products: 34.9 us -> 4.94 us
  Pallas kernels: 511 us -> 539 us
  waiting for transfers between devices: 25.9 us -> 0 us
  between operations: 14.5 us -> 0.74 us
  local copies, waits for them, and re-layouts: 20.1 us -> 9.46 us
  other arithmetic: 23.3 us -> 13.3 us
    pallas_call x10 -> x1, Pallas kernels: 511 us -> 539 us  [whole_block(): pl.pallas_call(functools.partial(whole_kernel, factor, names), out_shape=...]
    dot_general x4 -> x1, matrix products: 28.5 us -> 1.77 us  [dot(): return jnp.dot(a, b, preferred_element_type=F32)]
    all_gather x4 -> x0, waiting for transfers between devices: 24.3 us -> none  [z_gather(): return lax.all_gather(x, 'z', axis=0, tiled=True)]
    unnamed x60 -> x16, local copies, waits for them, and re-layouts: 15.5 us -> 2.88 us
  transfers between devices with their start and end apart: 7 -> 0, of which waited for: 2 -> 0; matrix products, arithmetic and copies ran while one was open for 10% -> 0% of each run, Pallas kernels for 39% -> 0%
where the time goes in v4:
time: 570 us; the launch traced here: 567 us
  Pallas kernels  539 us (95%)
  other arithmetic  13.3 us (2%)
  local copies, waits for them, and re-layouts  9.46 us (2%)
    pallas_call x1, Pallas kernels, whole_block(): pl.pallas_call(functools.partial(whole_kernel, factor, names), out_shape=...  539 us

profile of v4, /device:TPU:0, one launch (start us, length us, event | category | flops | bytes accessed | tf_op | source)
XLA Modules:
  0.0 567.3 jit_solution(11481113971434104665)
XLA Ops:
  0.6 0.0 copy-start
  0.7 0.8 compare_reduce_fusion
  1.4 0.0 copy-done
  1.4 0.1 constant_dynamic-slice_fusion
  1.5 0.8 copy.22
  2.3 0.1 reshape.101
  2.4 0.1 reshape.102
  2.5 3.4 gather_fusion
  5.9 1.8 fusion.3
  7.7 0.7 pad.4.refs_0_
  8.3 0.8 and_convert_fusion.refs_3_
  9.1 538.8 %shard_map.170 = (bf16[192,2048]{1,0:T(8,128)(2,1)}, f32[192,2048]{1,0:T(8,128)}, f32[8,8,384]{2,1,0:T(8,128)}, f32[8,64,256]{2,1,0:T(8,128)}, bf16[64,8192]{1,0...) custom-call(f32[8,8,384]{2,1,0:T(8,128)} %pad.4.refs_0_, ...), custom_call_target="tpu_custom_call" | custom-call | bytes 1620000000 | tf_op jit(solution)/shard_map/pallas_call | solution.py:1291
  547.9 0.0 copy-start.4
  547.9 0.0 copy-start.3
  548.0 1.0 slice.7
  549.0 1.1 slice_bitcast_fusion
  550.1 0.1 copy.24
  550.2 0.1 copy.25
  550.3 1.8 convert_element_type.20
  552.1 2.4 convert_element_type.19
  554.5 0.0 copy-done.4
  554.5 1.5 convert_element_type.21
  555.9 0.0 copy-done.3
  555.9 1.5 convert_element_type.22
  557.4 3.2 fusion.2
  560.6 0.0 copy-start.5
  560.6 4.7 scatter_custom_fusion
  565.2 0.0 copy-done.5
  565.2 0.9 copy.28
  566.1 0.0 copy-done.2
  566.1 1.1 copy.29
  567.3 0.0 copy-done.1
  (9 shorter events, 0.1 us)
Async XLA Ops:
  0.6 0.8 copy-start
  547.9 6.5 %copy-start.4 = (bf16[64,8192]{1,0:T(8,128)(2,1)S(1)}, bf16[64,8192]{1,0:T(8,128)(2,1)}, u32[]{:S(2)}) copy-start(bf16[64,8192]{1,0:T(8,128)(2,1)} %get-tuple-element.22) | copy-start | bytes 3145732
  547.9 8.0 %copy-start.3 = (bf16[64,8192]{1,0:T(8,128)(2,1)S(1)}, bf16[64,8192]{1,0:T(8,128)(2,1)}, u32[]{:S(2)}) copy-start(bf16[64,8192]{1,0:T(8,128)(2,1)} %get-tuple-element.23) | copy-start | bytes 3145732
  560.6 4.7 copy-start.5
  560.6 5.6 copy-start.2
  560.6 6.7 %copy-start.1 = (s32[1,768]{1,0:T(1,128)S(1)}, s32[1,768]{1,0:T(1,128)}, u32[]{:S(2)}) copy-start(s32[1,768]{1,0:T(1,128)} %param.18) | copy-start | bytes 9220

commit v5 on v4

--- a/solution.py
+++ b/solution.py
@@ -616,13 +616,13 @@
         z = lax.axis_index("z")
         self.copy(1, z, 2).start()
         self.copy(0, z, 1).start()
-        pl.when(inner_plane())(lambda: self.copy(2, z, 3).start())
 
     def relay(self):
         @pl.when(inner_plane())
         def _():
             self.copy(1, z_peer(2), 2).wait_recv()
             self.copy(3, z_peer(2), 1).start()
+            self.copy(2, lax.axis_index("z"), 3).start()
 
     def finish(self):
         z = lax.axis_index("z")
@@ -664,10 +664,15 @@
             device_id_type=pl.DeviceIdType.MESH,
         )
 
+    def begin_far(self):
+        pl.when(self.outer)(lambda: self.copy(self.g.at[z_peer(3)], 2, 1).start())
+
+    def begin_swap(self):
+        pl.when(self.inner)(lambda: self.copy(self.g.at[z_peer(3)], 3, 3).start())
+
     def begin(self):
-        far = self.g.at[z_peer(3)]
-        pl.when(self.outer)(lambda: self.copy(far, 2, 1).start())
-        pl.when(self.inner)(lambda: self.copy(far, 3, 3).start())
+        self.begin_far()
+        self.begin_swap()
 
     def temp(self, i):
         return self.temps.at[i, pl.ds(0, self.m), pl.ds(0, self.c)]
@@ -838,7 +843,7 @@
     du, part, part_y, dmix, dqkv = get("du", "part", "part_y", "dmix", "dqkv")
     xh, xv, xg, va, vb, vd = get("xh", "xv", "xg", "va", "vb", "vd")
     block_out, grad_tokens = get("block_out", "grad_tokens")
-    acc, img, temps, temps_out, tsem = get("acc", "img", "temps", "temps_out", "tsem")
+    img, temps, temps_out, tsem = get("img", "temps", "temps_out", "tsem")
     rows, width = tok.shape
     tokens = dy.shape[0]
     group = 4 * rows
@@ -866,10 +871,10 @@
         src = cols.at[pl.ds(2 * z_peer(m), 2)]
         sent.append(remote(src, ma.at[z], sa.at[m], ra.at[m], {"z": z_peer(m)}))
         sent[-1].start()
-    qkv_in.begin()
     out_load.wait()
     pl.when(outs.away)(lambda: out_in.start())
     pl.when(outs.home)(lambda: out_local.start())
+    qkv_in.begin()
     ma[z] = cols[pl.ds(2 * z, 2)]
     for copy in sent:
         copy.wait()
@@ -877,6 +882,13 @@
     for k in range(1, PLANE):
         src = ma.at[:, peer(k)["y"]]
         sent.append(send(src, mb.at[mine], sb.at[k], rb.at[k], k))
+    pl.when(outs.away)(lambda: out_in.wait())
+    pl.when(outs.home)(lambda: out_local.wait())
+    z_out = PlaneCopy(full_out, group_of("z_out"))
+    z_out.begin()
+    qkv_in.finish()
+    z_qkv = PlaneCopy(v["full_qkv"], group_of("z_qkv"))
+    z_qkv.begin()
     mb[mine] = ma[:, y]
     for copy in sent:
         copy.wait()
@@ -884,10 +896,6 @@
     for d in range(4 * PLANE):
         mods[:, d * each : (d + 1) * each] = mb[d % PLANE, d // PLANE]
 
-    qkv_in.finish()
-    z_qkv = PlaneCopy(v["full_qkv"], group_of("z_qkv"))
-    z_qkv.begin()
-
     def picker(r):
         hot = pick[r, 0:128]
         ones = [hot[:, i : i + 1].astype(F32) for i in range(IMAGES)]
@@ -896,7 +904,7 @@
             at = slice(which * width, (which + 1) * width)
             return sum(ones[i] * mods[i : i + 1, at] for i in range(IMAGES))
 
-        return ones, mod
+        return mod
 
     def normed_of(x):
         inv = lax.rsqrt(jnp.mean(x * x, axis=-1, keepdims=True) + EPS)
@@ -908,7 +916,7 @@
 
     def make_first(r, n):
         r = pl.ds(r, n)
-        _, mod = picker(r)
+        mod = picker(r)
         _, normed = normed_of(tok[r, :].astype(F32))
         xh[r, 0:width] = (normed * (1.0 + mod(1)) + mod(0)).astype(BF)
         xh[r, width:] = pick[r, :]
@@ -918,19 +926,15 @@
     to_first = Gather(xh, first, group_of("ga"))
     to_first.begin()
     up_in.begin()
-    pl.when(outs.away)(lambda: out_in.wait())
-    pl.when(outs.home)(lambda: out_local.wait())
-    z_out = PlaneCopy(full_out, group_of("z_out"))
-    z_out.begin()
+    z_out.relay()
     to_first.relay()
+    z_qkv.relay()
     to_first.finish()
     down_in.begin()
     up_in.finish()
-    z_qkv.relay()
-    z_out.relay()
+    z_qkv.finish()
     z_up = PlaneCopy(v["full_up"], group_of("z_up"))
     z_up.begin()
-    z_qkv.finish()
 
     n = math.gcd(tokens, 256)
 
@@ -956,20 +960,20 @@
     rows_mm(mixed, full_out, part, rows, 4, even)
     r_attn.load()
     r_attn.middle()
+    r_attn.relay()
+    z_up.relay()
     z_down = PlaneCopy(v["full_down"], group_of("z_down"))
     z_down.begin()
-    r_attn.relay()
     r_attn.finish()
 
     def make_second(r, n):
         r = pl.ds(r, n)
-        _, mod = picker(r)
+        mod = picker(r)
         x = tok[r, :].astype(F32) + mod(2) * va[r, :]
         vd[r, :] = x
         xv[r, :] = (normed_of(x)[1] * (1.0 + mod(4)) + mod(3)).astype(BF)
 
     rows_loop(rows, make_second)
-    z_up.relay()
     to_second = Gather(xv, second, group_of("gb"))
     to_second.begin()
     to_second.relay()
@@ -993,16 +997,18 @@
         [some_rows(hid, n), some_rows(slope, n)],
     )
     to_dy.relay()
+    z_down.relay()
     to_dy.finish()
-    z_down.relay()
     sums = [
         PlaneSum(v["g_" + key], v["land_" + key], group_of("s_" + key), t)
         for key, t in (("down", temps), ("up", temps), ("qkv", temps), ("out", temps_out))
     ]
     s_down, s_up, s_qkv, s_out = sums
     grads_mm(dy, hid, v["g_down"])
-    s_down.begin()
+    s_down.begin_far()
     z_down.finish()
+    s_down.begin_swap()
+    s_down.hop(tsem)
 
     def du_body(a, b, s, o):
         o[...] = (dot(a[...], b[...]) * s[...]).astype(BF)
@@ -1017,7 +1023,6 @@
     r_e2 = Scatter(part, vb, group_of("sc_a") + group_of("sems_2"))
     r_e2.begin()
     rows_mm(du, v["full_up"], part, rows, 4, even, True)
-    s_down.hop(tsem)
     r_e2.load()
     r_e2.middle()
     grads_mm(second, du, v["g_up"])
@@ -1025,34 +1030,35 @@
     r_e2.relay()
     r_e2.finish()
 
-    def clear():
-        acc[...] = jnp.zeros_like(acc)
-
-    def tally(ones, which, value):
-        for i in range(IMAGES):
-            acc[which, i] += ones[i] * value
+    pv = v["sc_b.0"]
+    parts = [(pv.at[0], pv.at[1]), (pv.at[2], pv.at[3]), (xg, xh.at[:, 0:width])]
+
+    def tally(which, r, value):
+        high = value.astype(BF)
+        parts[which][0][r, :] = high
+        parts[which][1][r, :] = (value - high.astype(F32)).astype(BF)
 
     def flush(blocks):
-        for q, which in enumerate(blocks):
-            for i in range(IMAGES):
-                at = slice(which * width, (which + 1) * width)
-                img[i : i + 1, at] = jnp.sum(acc[q, i], axis=0, keepdims=True)
-
-    clear()
+        hot = pick[:, 0:128]
+        for (high, low), which in zip(parts, blocks):
+            total = over_rows(hot, high[...]) + over_rows(hot, low[...])
+            img[:, which * width : (which + 1) * width] = total[0:8]
 
     def norm_back(r, n):
         r = pl.ds(r, n)
-        ones, mod = picker(r)
+        mod = picker(r)
         inv, normed = normed_of(vd[r, :])
         e = vb[r, :]
         d_mid = cot[r, :].astype(F32) + norm_grad(inv, normed, e * (1.0 + mod(4)))
         grad_tokens[r, :] = d_mid
         xv[r, :] = (mod(2) * d_mid).astype(BF)
-        tally(ones, 0, e)
-        tally(ones, 1, e * normed)
-        tally(ones, 2, d_mid * va[r, :])
+        tally(0, r, e)
+        tally(1, r, e * normed)
+        tally(2, r, d_mid * va[r, :])
 
     rows_loop(rows, norm_back)
+    load_w = pltpu.make_async_copy(v["mod_w_in"], v["mod_w"], group_of("mod_out")[10].at[0])
+    load_w.start()
     to_dat = Gather(xv, dat, group_of("gd"))
     to_dat.begin()
     flush((3, 4, 2))
@@ -1074,19 +1080,13 @@
     r_y.relay()
     grads_mm(first.at[:, 0:width], dqkv, v["g_qkv"])
     s_qkv.begin()
-
-    def out_body(a, b, g):
-        g[...] = over_rows(a[...], b[...]).astype(BF).reshape(g.shape)
-
-    step = math.gcd(width, 512)
-    g_out = v["g_out"]
-    pipe(
-        out_body,
-        width // step,
-        [whole(mixed), (dat, (tokens, step), lambda i: (0, i))],
-        [(g_out, g_out.shape[:2] + (step,), lambda i: (0, 0, i))],
-    )
-    s_out.begin()
+    dealt = []
+    deal_sems = group_of("deal")
+
+    def settle(s, out, blocks, sems):
+        s.finish(tsem)
+        dealt.extend(deal(s.q, out, blocks, *sems))
+
     r_y.finish()
     rows_mm(dqkv, v["full_qkv"], part, rows, 4, odd, True)
     r_e1 = Scatter(part, vb, group_of("sc_a") + group_of("sems_4"))
@@ -1095,21 +1095,33 @@
     r_e1.load()
     r_e1.middle()
     s_qkv.hop(tsem)
+
+    def out_body(a, b, g):
+        g[...] = over_rows(a[...], b[...]).astype(BF).reshape(g.shape)
+
+    step = math.gcd(width, 512)
+    g_out = v["g_out"]
+    pipe(
+        out_body,
+        width // step,
+        [whole(mixed), (dat, (tokens, step), lambda i: (0, i))],
+        [(g_out, g_out.shape[:2] + (step,), lambda i: (0, 0, i))],
+    )
+    s_out.begin()
+    r_e1.relay()
     s_out.hop(tsem)
-    r_e1.relay()
     r_e1.finish()
-    clear()
 
     def last_norm(r, n):
         r = pl.ds(r, n)
-        ones, mod = picker(r)
+        mod = picker(r)
         inv, normed = normed_of(tok[r, :].astype(F32))
         e, out = vb[r, :], va[r, :]
         grad_tokens[r, :] += norm_grad(inv, normed, e * (1.0 + mod(1)))
         block_out[r, :] = (vd[r, :] + mod(5) * out).astype(BF)
-        tally(ones, 0, e)
-        tally(ones, 1, e * normed)
-        tally(ones, 2, cot[r, :].astype(F32) * out)
+        tally(0, r, e)
+        tally(1, r, e * normed)
+        tally(2, r, cot[r, :].astype(F32) * out)
 
     rows_loop(rows, last_norm)
     flush((0, 1, 5))
@@ -1117,27 +1129,22 @@
     pa, ga, gs, gb, pc, pd, pe, ts = get("pa", "ga_", "gs", "gb_", "pc", "pd", "pe", "ts")
     w, t_all, dm = get("mod_w", "t_all", "dm")
     sems = group_of("mod_out")
-    load_w = pltpu.make_async_copy(v["mod_w_in"], w, sems[10].at[0])
-    load_w.start()
     for d in range(4 * PLANE):
-        pa[d % PLANE, d // PLANE] = img[:, d * each : (d + 1) * each]
+        t = d // PLANE * IMAGES
+        pa[d % PLANE, t : t + IMAGES] = img[0:IMAGES, d * each : (d + 1) * each]
     plane_sent = lambda src, dst, s, r: [
         send(src(k), dst, s.at[k], r.at[k], k) for k in range(1, PLANE)
     ]
     sent = plane_sent(lambda k: pa.at[place(k)], ga.at[mine], sems[0], sems[1])
     ga[mine] = pa[mine]
-    dealt = []
-    deal_sems = group_of("deal")
-
-    def settle(s, out, blocks, sems):
-        s.finish(tsem)
-        dealt.extend(deal(s.q, out, blocks, *sems))
-
+    gs[...] = jnp.zeros_like(gs)
     settle(s_down, v["c_down"], 1, deal_sems[:2])
     for copy in sent:
         copy.wait()
     for g in range(2):
-        gs[:, g] = ga[4 * g] + ga[4 * g + 1] + ga[4 * g + 2] + ga[4 * g + 3]
+        total = ga[4 * g] + ga[4 * g + 1] + ga[4 * g + 2] + ga[4 * g + 3]
+        for t in range(4):
+            gs[t, g * IMAGES : (g + 1) * IMAGES] = total[t * IMAGES : (t + 1) * IMAGES]
     sent = []
     for m in (1, 2, 3):
         copy = remote(
@@ -1146,7 +1153,7 @@
         copy.start()
         sent.append(copy)
     gb[z] = gs[z]
-    settle(s_up, v["c_up"], 1, deal_sems[2:4])
+    s_up.finish(tsem)
     s_out.finish(tsem)
     back = remote(s_out.q, v["c_out"], tsem.at[4], tsem.at[5], outs.owner)
     back_local = pltpu.make_async_copy(s_out.q, v["c_out"], tsem.at[4])
@@ -1155,10 +1162,8 @@
     for copy in sent:
         copy.wait()
     load_w.wait()
-    for t in range(4):
-        for g in range(2):
-            dm[2 * t + g] = gb[t, g]
-    own = dm[...].reshape(8 * 8, each)
+    dm[...] = gb[...]
+    own = dm[...].reshape(4 * 8, each)
     high = own.astype(BF)
     low = (own - high.astype(F32)).astype(BF)
     slice_of = width // PLANE
@@ -1167,7 +1172,7 @@
         pc[k] = times_t(high, piece) + times_t(low, piece)
     sent = plane_sent(lambda k: pc.at[place(k)], pd.at[mine], sems[4], sems[5])
     pd[mine] = pc[mine]
-    settle(s_qkv, v["c_qkv"], 3, deal_sems[4:6])
+    dealt.extend(deal(s_up.q, v["c_up"], 1, *deal_sems[2:4]))
     for copy in sent:
         copy.wait()
     total = pd[0]
@@ -1179,6 +1184,7 @@
         copy = remote(pe.at[z], pe.at[z], sems[6].at[m], sems[7].at[m], {"z": z_peer(m)})
         copy.start()
         sent.append(copy)
+    settle(s_qkv, v["c_qkv"], 3, deal_sems[4:6])
     for copy in sent:
         copy.wait()
     ts[...] = pe[0] + pe[1] + pe[2] + pe[3]
@@ -1207,8 +1213,8 @@
     near = dict(
         block_out=struct((rows, width), BF),
         grad_tokens=struct((rows, width), F32),
-        dm=struct(cols.shape, F32),
-        t_all=struct((PLANE, 64, width // PLANE), F32),
+        dm=struct((nz, 8, each), F32),
+        t_all=struct((PLANE, 32, width // PLANE), F32),
     )
     far = dict(
         c_down=struct((share, wide * PLANE), BF),
@@ -1251,19 +1257,18 @@
         va=own,
         vb=own,
         vd=own,
-        acc=vm((3, IMAGES, 16, width), F32),
         temps=vm((4, m, max(wide, part)), BF),
         temps_out=vm((4,) + shapes["out"][1:], BF),
         tsem=dma((6,)),
         mod_w=vm(mod_w.shape, BF),
-        pa=vm((PLANE, nz, 8, each), F32),
-        ga_=vm((PLANE, nz, 8, each), F32),
-        gs=vm((nz, 2, 8, each), F32),
-        gb_=vm((nz, 2, 8, each), F32),
-        pc=vm((PLANE, 64, width // PLANE), F32),
-        pd=vm((PLANE, 64, width // PLANE), F32),
-        pe=vm((nz, 64, width // PLANE), F32),
-        ts=vm((64, width // PLANE), F32),
+        pa=vm((PLANE, 16, each), F32),
+        ga_=vm((PLANE, 16, each), F32),
+        gs=vm((nz, 8, each), F32),
+        gb_=vm((nz, 8, each), F32),
+        pc=vm((PLANE, 32, width // PLANE), F32),
+        pd=vm((PLANE, 32, width // PLANE), F32),
+        pe=vm((nz, 32, width // PLANE), F32),
+        ts=vm((32, width // PLANE), F32),
     )
 
     def add(prefix, items):
@@ -1456,8 +1461,8 @@
         1,
     )
     count, width = cols.shape[0] * images, tok.shape[1]
-    mod_grads = out["dm"][:, :images].reshape(count, -1)
-    cond_grads = out["t_all"].reshape(PLANE, -1, 8, width // PLANE)[:, :, :images]
+    mod_grads = out["dm"][:, : 2 * images].reshape(count, -1)
+    cond_grads = out["t_all"].reshape(PLANE, 4, 8, width // PLANE)[:, :, : 2 * images]
     cond_grads = cond_grads.transpose(1, 2, 0, 3).reshape(count, width)
     return (
         out["block_out"],

time: 570 us -> 529 us (0.928)
  Pallas kernels: 539 us -> 499 us
    pallas_call x1, Pallas kernels: 539 us -> 499 us  [whole_block(): pl.pallas_call(functools.partial(whole_kernel, factor, names), out_shape=...]
where the time goes in v5:
time: 529 us; the launch traced here: 527 us
  Pallas kernels  499 us (94%)
  other arithmetic  13.3 us (3%)
  local copies, waits for them, and re-layouts  9.23 us (2%)
    pallas_call x1, Pallas kernels, whole_block(): pl.pallas_call(functools.partial(whole_kernel, factor, names), out_shape=...  499 us

profile of v5, /device:TPU:0, one launch (start us, length us, event | category | flops | bytes accessed | tf_op | source)
XLA Modules:
  0.0 526.9 jit_solution(1283270351028229863)
XLA Ops:
  0.6 0.0 copy-start
  0.7 0.8 compare_reduce_fusion
  1.4 0.0 copy-done
  1.4 0.1 constant_dynamic-slice_fusion
  1.5 0.8 copy.22
  2.3 0.1 reshape.101
  2.4 0.1 reshape.102
  2.5 3.4 gather_fusion
  5.9 1.8 fusion.3
  7.7 0.7 pad.4.refs_0_
  8.3 0.8 and_convert_fusion.refs_3_
  9.1 498.7 %shard_map.170 = (bf16[192,2048]{1,0:T(8,128)(2,1)}, f32[192,2048]{1,0:T(8,128)}, f32[4,8,384]{2,1,0:T(8,128)}, f32[8,32,256]{2,1,0:T(8,128)}, bf16[64,8192]{1,0...) custom-call(f32[8,8,384]{2,1,0:T(8,128)} %pad.4.refs_0_, ...), custom_call_target="tpu_custom_call" | custom-call | bytes 1620000000 | tf_op jit(solution)/shard_map/pallas_call | solution.py:1296
  507.8 0.0 copy-start.4
  507.8 0.0 copy-start.3
  507.8 1.0 reshape.106
  508.7 1.0 slice_bitcast_fusion
  509.7 0.1 copy.24
  509.8 0.1 copy.25
  509.9 1.8 convert_element_type.20
  511.7 2.4 convert_element_type.19
  514.1 0.0 copy-done.4
  514.1 1.5 convert_element_type.21
  515.5 0.0 copy-done.3
  515.5 1.5 convert_element_type.22
  517.0 3.2 fusion.2
  520.2 0.0 copy-start.5
  520.2 4.7 scatter_custom_fusion
  524.9 0.0 copy-done.5
  524.9 0.9 copy.28
  525.7 0.0 copy-done.2
  525.7 1.1 copy.29
  526.9 0.0 copy-done.1
  (8 shorter events, 0.1 us)
Async XLA Ops:
  0.6 0.8 copy-start
  507.8 6.3 %copy-start.4 = (bf16[64,8192]{1,0:T(8,128)(2,1)S(1)}, bf16[64,8192]{1,0:T(8,128)(2,1)}, u32[]{:S(2)}) copy-start(bf16[64,8192]{1,0:T(8,128)(2,1)} %get-tuple-element.22) | copy-start | bytes 3145732
  507.8 7.7 %copy-start.3 = (bf16[64,8192]{1,0:T(8,128)(2,1)S(1)}, bf16[64,8192]{1,0:T(8,128)(2,1)}, u32[]{:S(2)}) copy-start(bf16[64,8192]{1,0:T(8,128)(2,1)} %get-tuple-element.23) | copy-start | bytes 3145732
  520.2 4.7 copy-start.5
  520.2 5.6 %copy-start.2 = (f32[192,2048]{1,0:T(8,128)S(1)}, f32[192,2048]{1,0:T(8,128)}, u32[]{:S(2)}) copy-start(f32[192,2048]{1,0:T(8,128)} %get-tuple-element.17) | copy-start | bytes 4718596
  520.2 6.7 %copy-start.1 = (s32[1,768]{1,0:T(1,128)S(1)}, s32[1,768]{1,0:T(1,128)}, u32[]{:S(2)}) copy-start(s32[1,768]{1,0:T(1,128)} %param.18) | copy-start | bytes 9220

commit v6 on v5

--- a/solution.py
+++ b/solution.py
@@ -1008,7 +1008,6 @@
     s_down.begin_far()
     z_down.finish()
     s_down.begin_swap()
-    s_down.hop(tsem)
 
     def du_body(a, b, s, o):
         o[...] = (dot(a[...], b[...]) * s[...]).astype(BF)
@@ -1019,6 +1018,7 @@
         [some_rows(dy, n), whole(v["full_down"]), some_rows(slope, n)],
         [some_rows(du, n)],
     )
+    s_down.hop(tsem)
     rows_mm(du, v["full_up"], part, rows, 4, odd, True)
     r_e2 = Scatter(part, vb, group_of("sc_a") + group_of("sems_2"))
     r_e2.begin()
@@ -1110,6 +1110,7 @@
     s_out.begin()
     r_e1.relay()
     s_out.hop(tsem)
+    settle(s_down, v["c_down"], 1, deal_sems[:2])
     r_e1.finish()
 
     def last_norm(r, n):
@@ -1138,7 +1139,6 @@
     sent = plane_sent(lambda k: pa.at[place(k)], ga.at[mine], sems[0], sems[1])
     ga[mine] = pa[mine]
     gs[...] = jnp.zeros_like(gs)
-    settle(s_down, v["c_down"], 1, deal_sems[:2])
     for copy in sent:
         copy.wait()
     for g in range(2):

time: 529 us -> 522 us (0.987)
  Pallas kernels: 499 us -> 491 us
    pallas_call x1, Pallas kernels: 499 us -> 491 us  [whole_block(): pl.pallas_call(functools.partial(whole_kernel, factor, names), out_shape=...]
where the time goes in v6:
time: 522 us; the launch traced here: 519 us
  Pallas kernels  491 us (94%)
  other arithmetic  13.3 us (3%)
  local copies, waits for them, and re-layouts  9.23 us (2%)
    pallas_call x1, Pallas kernels, whole_block(): pl.pallas_call(functools.partial(whole_kernel, factor, names), out_shape=...  491 us

profile of v6, /device:TPU:0, one launch (start us, length us, event | category | flops | bytes accessed | tf_op | source)
XLA Modules:
  0.0 518.8 jit_solution(78127096685874531)
XLA Ops:
  0.6 0.0 copy-start
  0.7 0.8 compare_reduce_fusion
  1.4 0.0 copy-done
  1.4 0.1 constant_dynamic-slice_fusion
  1.5 0.8 copy.22
  2.3 0.1 reshape.101
  2.4 0.1 reshape.102
  2.5 3.4 gather_fusion
  5.9 1.8 fusion.3
  7.7 0.7 pad.4.refs_0_
  8.3 0.8 and_convert_fusion.refs_3_
  9.1 490.6 %shard_map.170 = (bf16[192,2048]{1,0:T(8,128)(2,1)}, f32[192,2048]{1,0:T(8,128)}, f32[4,8,384]{2,1,0:T(8,128)}, f32[8,32,256]{2,1,0:T(8,128)}, bf16[64,8192]{1,0...) custom-call(f32[8,8,384]{2,1,0:T(8,128)} %pad.4.refs_0_, ...), custom_call_target="tpu_custom_call" | custom-call | bytes 1620000000 | tf_op jit(solution)/shard_map/pallas_call | solution.py:1296
  499.7 0.0 copy-start.4
  499.7 0.0 copy-start.3
  499.7 1.0 reshape.106
  500.7 1.0 slice_bitcast_fusion
  501.6 0.1 copy.24
  501.7 0.1 copy.25
  501.8 1.8 convert_element_type.20
  503.6 2.4 convert_element_type.19
  506.0 0.0 copy-done.4
  506.0 1.5 convert_element_type.21
  507.4 0.0 copy-done.3
  507.4 1.5 convert_element_type.22
  508.9 3.2 fusion.2
  512.1 0.0 copy-start.5
  512.1 4.7 scatter_custom_fusion
  516.8 0.0 copy-done.5
  516.8 0.9 copy.28
  517.6 0.0 copy-done.2
  517.6 1.1 copy.29
  518.8 0.0 copy-done.1
  (8 shorter events, 0.1 us)
Async XLA Ops:
  0.6 0.8 copy-start
  499.7 6.3 %copy-start.4 = (bf16[64,8192]{1,0:T(8,128)(2,1)S(1)}, bf16[64,8192]{1,0:T(8,128)(2,1)}, u32[]{:S(2)}) copy-start(bf16[64,8192]{1,0:T(8,128)(2,1)} %get-tuple-element.22) | copy-start | bytes 3145732
  499.7 7.7 %copy-start.3 = (bf16[64,8192]{1,0:T(8,128)(2,1)S(1)}, bf16[64,8192]{1,0:T(8,128)(2,1)}, u32[]{:S(2)}) copy-start(bf16[64,8192]{1,0:T(8,128)(2,1)} %get-tuple-element.23) | copy-start | bytes 3145732
  512.1 4.7 copy-start.5
  512.1 5.6 %copy-start.2 = (f32[192,2048]{1,0:T(8,128)S(1)}, f32[192,2048]{1,0:T(8,128)}, u32[]{:S(2)}) copy-start(f32[192,2048]{1,0:T(8,128)} %get-tuple-element.17) | copy-start | bytes 4718596
  512.1 6.7 %copy-start.1 = (s32[1,768]{1,0:T(1,128)S(1)}, s32[1,768]{1,0:T(1,128)}, u32[]{:S(2)}) copy-start(s32[1,768]{1,0:T(1,128)} %param.18) | copy-start | bytes 9220

commit v7 on v6

--- a/solution.py
+++ b/solution.py
@@ -1064,8 +1064,8 @@
     flush((3, 4, 2))
     rows_mm(hid, v["full_down"], part_y, rows, 8, transposed=True)
     to_dat.relay()
+    to_dat.finish()
     s_up.hop(tsem)
-    to_dat.finish()
     r_y = Scatter(part_y, va, group_of("sc_b") + group_of("sems_3"))
     r_y.begin()
     r_y.load()

time: 522 us -> 529 us (1.013)
  Pallas kernels: 491 us -> 498 us
    pallas_call x1, Pallas kernels: 491 us -> 498 us  [whole_block(): pl.pallas_call(functools.partial(whole_kernel, factor, names), out_shape=...]
where the time goes in v7:
time: 529 us; the launch traced here: 526 us
  Pallas kernels  498 us (94%)
  other arithmetic  13.3 us (3%)
  local copies, waits for them, and re-layouts  9.23 us (2%)
    pallas_call x1, Pallas kernels, whole_block(): pl.pallas_call(functools.partial(whole_kernel, factor, names), out_shape=...  498 us

profile of v7, /device:TPU:0, one launch (start us, length us, event | category | flops | bytes accessed | tf_op | source)
XLA Modules:
  0.0 526.5 jit_solution(8532189429367890230)
XLA Ops:
  0.6 0.0 copy-start
  0.7 0.8 compare_reduce_fusion
  1.4 0.0 copy-done
  1.4 0.1 constant_dynamic-slice_fusion
  1.5 0.8 copy.22
  2.3 0.1 reshape.101
  2.4 0.1 reshape.102
  2.5 3.4 gather_fusion
  5.9 1.8 fusion.3
  7.7 0.7 pad.4.refs_0_
  8.3 0.8 and_convert_fusion.refs_3_
  9.1 498.2 %shard_map.170 = (bf16[192,2048]{1,0:T(8,128)(2,1)}, f32[192,2048]{1,0:T(8,128)}, f32[4,8,384]{2,1,0:T(8,128)}, f32[8,32,256]{2,1,0:T(8,128)}, bf16[64,8192]{1,0...) custom-call(f32[8,8,384]{2,1,0:T(8,128)} %pad.4.refs_0_, ...), custom_call_target="tpu_custom_call" | custom-call | bytes 1620000000 | tf_op jit(solution)/shard_map/pallas_call | solution.py:1296
  507.4 0.0 copy-start.4
  507.4 0.0 copy-start.3
  507.4 1.0 reshape.106
  508.3 1.0 slice_bitcast_fusion
  509.3 0.1 copy.24
  509.4 0.1 copy.25
  509.5 1.8 convert_element_type.20
  511.3 2.4 convert_element_type.19
  513.7 0.0 copy-done.4
  513.7 1.5 convert_element_type.21
  515.1 0.0 copy-done.3
  515.1 1.5 convert_element_type.22
  516.6 3.2 fusion.2
  519.7 0.0 copy-start.5
  519.8 4.7 scatter_custom_fusion
  524.4 0.0 copy-done.5
  524.4 0.9 copy.28
  525.3 0.0 copy-done.2
  525.3 1.1 copy.29
  526.5 0.0 copy-done.1
  (8 shorter events, 0.1 us)
Async XLA Ops:
  0.6 0.8 copy-start
  507.4 6.3 %copy-start.4 = (bf16[64,8192]{1,0:T(8,128)(2,1)S(1)}, bf16[64,8192]{1,0:T(8,128)(2,1)}, u32[]{:S(2)}) copy-start(bf16[64,8192]{1,0:T(8,128)(2,1)} %get-tuple-element.22) | copy-start | bytes 3145732
  507.4 7.7 %copy-start.3 = (bf16[64,8192]{1,0:T(8,128)(2,1)S(1)}, bf16[64,8192]{1,0:T(8,128)(2,1)}, u32[]{:S(2)}) copy-start(bf16[64,8192]{1,0:T(8,128)(2,1)} %get-tuple-element.23) | copy-start | bytes 3145732
  519.7 4.7 copy-start.5
  519.7 5.6 %copy-start.2 = (f32[192,2048]{1,0:T(8,128)S(1)}, f32[192,2048]{1,0:T(8,128)}, u32[]{:S(2)}) copy-start(f32[192,2048]{1,0:T(8,128)} %get-tuple-element.17) | copy-start | bytes 4718596
  519.7 6.7 %copy-start.1 = (s32[1,768]{1,0:T(1,128)S(1)}, s32[1,768]{1,0:T(1,128)}, u32[]{:S(2)}) copy-start(s32[1,768]{1,0:T(1,128)} %param.18) | copy-start | bytes 9220
